TPU v7x, 128 devices: a whole 4x4x4 slice. The times are simulated.
128 devices in a mesh: dp: 8 (over z, core), ctx: 16 (over x, y).
Axes of the slice: x: 4, y: 4, z: 4, core: 2. Of those that a mesh axis runs over, the one named last changes fastest.
Arguments:
- q_load: bfloat16 [16384, 4096], P(('dp', 'ctx')), may hold values from -6.5 to 6.5, as said below
- k_load: bfloat16 [16384, 1024], P(('dp', 'ctx')), may hold values from -6.5 to 6.5, as said below
- v_load: bfloat16 [16384, 1024], P(('dp', 'ctx')), may hold values from -6 to 6
- grad_out: bfloat16 [16384, 4096], P(('dp', 'ctx')), may hold values from -6 to 6
- pack_rows: int32 [128, 128, 2], P(('dp', 'ctx')), may hold values from -1 to 127, as said below
- unpack: int32 [128, 128], P(('dp', 'ctx')), may hold values from 0 to 255, as said below
- doc_lengths: int32 [8, 16], P('dp'), may hold values from 1 to 1024, 2048 in all within a row
Outputs:
- attended: bfloat16 [16384, 4096], P(('dp', 'ctx'))
- grad_q: bfloat16 [16384, 4096], P(('dp', 'ctx'))
- grad_k: bfloat16 [16384, 1024], P(('dp', 'ctx'))
- grad_v: bfloat16 [16384, 1024], P(('dp', 'ctx'))
Inputs may be any that keep to these rules, and one draw needn't show every extreme that they name: `q_load`: custom queries: every entry lies in the stated range. `k_load`: custom keys: every entry lies in the stated range. pack_rows[s, b, j] is the row of device s's loader block sent in slot j of its message to device b, or -1 for an empty slot. Every row of a device is sent exactly once, every device receives exactly 128 rows, at most 2 rows go from one device to one device, and in every draw some pairs of devices carry exactly 2. Non-empty slots of a message come first. unpack[b, r] = s * 2 + j names a non-empty slot j of the message from device s to device b; each non-empty slot to b is named by exactly one r.
All inputs are finite; a program needn't handle non-finite values.
Results may differ from a plain program's by a relative error of at most 0.009.
The roundings to bfloat16 on the way count: a program that leaves them out, or rounds other values in their place, can miss the bound.
Values may be sent and summed in bfloat16 or wider, within the bound.
A program may use at most 128 MiB of HBM per device.

v0:
```python
import math

import jax
import jax.numpy as jnp
from jax import lax
from jax.sharding import PartitionSpec as P

H = 32
KVH = 8
DH = 128


def document_ids(positions, lengths):
    doc_ends = jnp.cumsum(lengths)
    return jnp.sum((doc_ends[None, :] <= positions[:, None]).astype(jnp.int32), axis=1)


def visible_pairs(query_pos, query_doc, key_pos, key_doc):
    return (
        (key_doc[None, :] == query_doc[:, None])
        & (key_pos[None, :] <= query_pos[:, None])
        & (key_pos[None, :] >= 0)
    )


def local_attention(queries, grad_block, key_rows, value_rows, allowed):
    row_count = queries.shape[0]
    width = key_rows.shape[0]
    replicas = H // KVH
    score_scale = 1.0 / math.sqrt(DH)
    query_groups = (
        queries.reshape(row_count, KVH, replicas, DH)
        .transpose(1, 2, 0, 3)
        .reshape(KVH, replicas * row_count, DH)
    )
    grad_groups = (
        grad_block.reshape(row_count, KVH, replicas, DH)
        .transpose(1, 2, 0, 3)
        .reshape(KVH, replicas * row_count, DH)
    )
    key_groups = key_rows.reshape(width, KVH, DH).transpose(1, 0, 2)
    value_groups = value_rows.reshape(width, KVH, DH).transpose(1, 0, 2)
    mask_rows = jnp.tile(allowed, (replicas, 1))

    def per_group(operands):
        query_head, grad_head, key_head, value_head = operands
        scores = (
            jnp.einsum("rd,kd->rk", query_head, key_head, preferred_element_type=jnp.float32)
            * score_scale
        )
        row_max = jnp.max(jnp.where(mask_rows, scores, -jnp.inf), axis=-1, keepdims=True)
        weights = jnp.where(mask_rows, jnp.exp(scores - row_max), 0.0)
        prob_full = weights / jnp.sum(weights, axis=-1, keepdims=True)
        prob_low = prob_full.astype(jnp.bfloat16)
        attended = jnp.dot(prob_low, value_head, preferred_element_type=jnp.float32).astype(
            jnp.bfloat16
        )
        dprobs = jnp.einsum("rd,kd->rk", grad_head, value_head, preferred_element_type=jnp.float32)
        row_delta = jnp.sum(
            grad_head.astype(jnp.float32) * attended.astype(jnp.float32), axis=-1, keepdims=True
        )
        dscores = (prob_full * (dprobs - row_delta) * score_scale).astype(jnp.bfloat16)
        grad_query = jnp.dot(dscores, key_head, preferred_element_type=jnp.float32).astype(
            jnp.bfloat16
        )
        grad_key = jnp.einsum("rk,rd->kd", dscores, query_head, preferred_element_type=jnp.float32)
        grad_value = jnp.einsum(
            "rk,rd->kd", prob_low, grad_head, preferred_element_type=jnp.float32
        )
        return (attended, grad_query, grad_key, grad_value)

    attended, grad_query, grad_key, grad_value = lax.map(
        per_group, (query_groups, grad_groups, key_groups, value_groups)
    )
    attended = (
        attended.reshape(KVH, replicas, row_count, DH)
        .transpose(2, 0, 1, 3)
        .reshape(row_count, H * DH)
    )
    grad_query = (
        grad_query.reshape(KVH, replicas, row_count, DH)
        .transpose(2, 0, 1, 3)
        .reshape(row_count, H * DH)
    )
    grad_key = grad_key.transpose(1, 0, 2).reshape(width, KVH * DH)
    grad_value = grad_value.transpose(1, 0, 2).reshape(width, KVH * DH)
    return (attended, grad_query, grad_key, grad_value)


def outgoing(block, clipped, occupied):
    taken = block[clipped]
    return jnp.where(occupied[..., None], taken, jnp.zeros_like(taken))


def local(q_load, k_load, v_load, grad_out, pack_rows, unpack, doc_lengths):
    row_count = q_load.shape[0]
    slot_rows = pack_rows[0]
    devices_all, capacity = slot_rows.shape
    occupied = slot_rows >= 0
    clipped = jnp.maximum(slot_rows, 0)
    ctx_size = lax.axis_size("ctx")
    sent_q = outgoing(q_load, clipped, occupied)
    sent_k = outgoing(k_load, clipped, occupied)
    sent_v = outgoing(v_load, clipped, occupied)
    arrived = (
        lax.all_to_all(sent_q, ("dp", "ctx"), split_axis=0, concat_axis=0, tiled=True),
        lax.all_to_all(sent_k, ("dp", "ctx"), split_axis=0, concat_axis=0, tiled=True),
        lax.all_to_all(sent_v, ("dp", "ctx"), split_axis=0, concat_axis=0, tiled=True),
    )
    arrival = unpack[0]
    q_bal, k_bal, v_bal = [piece.reshape(devices_all * capacity, -1)[arrival] for piece in arrived]
    ctx_index = lax.axis_index("ctx")
    lengths = doc_lengths[0]
    query_pos = ctx_index * row_count + jnp.arange(row_count, dtype=jnp.int32)
    query_doc = document_ids(query_pos, lengths)
    all_keys, all_values = (
        lax.all_gather(k_bal, "ctx", axis=0, tiled=True),
        lax.all_gather(v_bal, "ctx", axis=0, tiled=True),
    )
    key_pos = jnp.arange(ctx_size * row_count, dtype=jnp.int32)
    allowed = visible_pairs(query_pos, query_doc, key_pos, document_ids(key_pos, lengths))
    attended, grad_query, part_k, part_v = local_attention(
        q_bal, grad_out, all_keys, all_values, allowed
    )
    total_k, total_v = (
        lax.psum_scatter(
            part_k.astype(jnp.bfloat16), "ctx", scatter_dimension=0, tiled=True
        ).astype(jnp.float32),
        lax.psum_scatter(
            part_v.astype(jnp.bfloat16), "ctx", scatter_dimension=0, tiled=True
        ).astype(jnp.float32),
    )
    grad_key = total_k.astype(jnp.bfloat16)
    grad_value = total_v.astype(jnp.bfloat16)
    filled = jnp.zeros((devices_all * capacity,), jnp.bool_).at[arrival].set(True)
    source_row = (
        jnp.zeros((devices_all * capacity,), jnp.int32)
        .at[arrival]
        .set(jnp.arange(row_count, dtype=jnp.int32))
    )

    def outgoing_back(block):
        taken = block[source_row]
        return jnp.where(filled[:, None], taken, jnp.zeros_like(taken))

    back_q = outgoing_back(grad_query)
    back_k = outgoing_back(grad_key)
    back_v = outgoing_back(grad_value)
    returned = (
        lax.all_to_all(
            back_q.reshape(devices_all, capacity, -1),
            ("dp", "ctx"),
            split_axis=0,
            concat_axis=0,
            tiled=True,
        ),
        lax.all_to_all(
            back_k.reshape(devices_all, capacity, -1),
            ("dp", "ctx"),
            split_axis=0,
            concat_axis=0,
            tiled=True,
        ),
        lax.all_to_all(
            back_v.reshape(devices_all, capacity, -1),
            ("dp", "ctx"),
            split_axis=0,
            concat_axis=0,
            tiled=True,
        ),
    )
    target = jnp.where(occupied, slot_rows, row_count).reshape(-1)
    position = (
        jnp.zeros((row_count,), jnp.int32)
        .at[target]
        .set(jnp.arange(devices_all * capacity, dtype=jnp.int32), mode="drop")
    )
    grad_q, grad_k, grad_v = [
        piece.reshape(devices_all * capacity, -1)[position] for piece in returned
    ]
    return (attended, grad_q, grad_k, grad_v)


def solution(mesh):
    return jax.shard_map(
        local,
        mesh=mesh,
        in_specs=(
            P(("dp", "ctx"), None),
            P(("dp", "ctx"), None),
            P(("dp", "ctx"), None),
            P(("dp", "ctx"), None),
            P(("dp", "ctx"), None, None),
            P(("dp", "ctx"), None),
            P("dp", None),
        ),
        out_specs=(
            P(("dp", "ctx"), None),
            P(("dp", "ctx"), None),
            P(("dp", "ctx"), None),
            P(("dp", "ctx"), None),
        ),
        check_vma=False,
    )
```

profile of v0, /device:TPU:1, one launch (start us, length us, event | category | flops | bytes accessed | tf_op | source)
XLA Modules:
  0.0 534.4 jit_solution(11402107784042400225)
XLA Ops:
  8.9 2.5 gather_fusion.2
  15.0 11.5 %all-to-all-start.2 = ((bf16[128,2,1024]{2,1,0:T(2,128)(2,1)}), bf16[128,2,1024]{2,1,0:T(2,128)(2,1)S(1)}, u32[]{:S(2)}, u32[]{:S(2)}) async-start(bf16[128,2,1024]{2,1,0:T(2,128)(2,1)} %get-tuple-element.142), calls=%async_computation.2 | async-start | bytes 1048576 | tf_op jit(solution)/shard_map/all_to_all | solution.py:108
  26.6 13.3 %all-to-all-done.2 = bf16[128,2,1024]{2,1,0:T(2,128)(2,1)S(1)} async-done(((bf16[128,2,1024]{2,1,0:T(2,128)(2,1)}), bf16[128,2,1024]{2,1,0:T(2,128)(2,1)S(1)}, u32[]{:S(2)}, u32[]{:S(2)}) %all-to-all-start.2) | async-done | bytes 524320 | tf_op jit(solution)/shard_map/all_to_all | solution.py:108
  41.7 19.6 %all_to_all.30 = bf16[128,2,1024]{2,1,0:T(2,128)(2,1)S(1)} all-to-all(bf16[128,2,1024]{2,1,0:T(2,128)(2,1)S(1)} %get-tuple-element.143), channel_id=1, replica_groups=mesh['dp'=8,'ctx'=16] {'dp','ctx'}, dimensions={0} | all-to-all | bytes 1048576 | tf_op jit(solution)/shard_map/all_to_all | solution.py:107
  63.1 3.2 gather_fusion
  66.3 3.2 reshape.258
  69.5 3.2 broadcast_select_fusion.1
  72.7 6.1 %all-to-all-start = ((bf16[128,2,4096]{2,1,0:T(2,128)(2,1)}), bf16[128,2,4096]{2,1,0:T(2,128)(2,1)}, u32[]{:S(2)}, u32[]{:S(2)}) async-start(bf16[128,2,4096]{2,1,0:T(2,128)(2,1)} %broadcast_select_fusion.1), calls=%async_computation | async-start | bytes 4194304 | tf_op jit(solution)/shard_map/all_to_all | solution.py:106
  83.7 34.3 %all-to-all-done = bf16[128,2,4096]{2,1,0:T(2,128)(2,1)} async-done(((bf16[128,2,4096]{2,1,0:T(2,128)(2,1)}), bf16[128,2,4096]{2,1,0:T(2,128)(2,1)}, u32[]{:S(2)}, u32[]{:S(2)}) %all-to-all-start) | async-done | bytes 2097184 | tf_op jit(solution)/shard_map/all_to_all | solution.py:106
  118.0 2.7 reshape.239
  120.8 2.2 gather_fusion.1
  125.2 5.0 bitcast_bitcast_fusion
  130.2 36.8 %all-gather.5.cloned.1.call-done = bf16[2048,1024]{1,0:T(8,128)(2,1)} async-done(((bf16[128,1024]{1,0:T(8,128)(2,1)}), bf16[2048,1024]{1,0:T(8,128)(2,1)}) %all-gather.5.cloned.1.call-update) | async-done | bytes 4194320 | tf_op jit(solution)/shard_map/all_gather | solution.py:117
  167.0 4.9 bitcast_bitcast_fusion.1
  171.9 126.5 %while.17 = (s32[]{:T(128)}, bf16[8,512,128]{1,2,0:T(8,128)(2,1)S(1)}, bf16[8,512,128]{2,1,0:T(8,128)(2,1)}, bf16[8,2048,128]{2,1,0:T(8,128)(2,1)}, bf16[8,2048,...) while((s32[]{:T(128)}, ...), condition=%wide.region_7.8_spmd.clone, body=%wide.region_3.7_spmd.clone.sunk | while | flops 1628830208 | bytes 41832560 | solution.py:72
  182.9 2.4 fusion.73
  185.3 2.5 fusion.75
  198.7 2.4 fusion.73
  201.1 2.5 fusion.75
  214.5 2.4 fusion.73
  216.9 2.5 fusion.75
  230.2 2.4 fusion.73
  232.7 2.5 fusion.75
  246.1 2.4 fusion.73
  248.5 2.5 fusion.75
  261.9 2.4 fusion.73
  264.3 2.5 fusion.75
  277.7 2.4 fusion.73
  280.1 2.5 fusion.75
  293.5 2.4 fusion.73
  295.9 2.5 fusion.75
  298.4 5.1 copy_bitcast_fusion.1
  303.8 4.8 copy_bitcast_fusion
  314.3 2.7 gather.49
  317.0 4.9 broadcast_select_fusion
  321.9 8.0 %all-to-all-start.3 = ((bf16[128,2,4096]{2,1,0:T(2,128)(2,1)}), bf16[128,2,4096]{2,1,0:T(2,128)(2,1)S(1)}, u32[]{:S(2)}, u32[]{:S(2)}) async-start(bf16[128,2,4096]{2,1,0:T(2,128)(2,1)} %broadcast_select_fusion), calls=%async_computation.3 | async-start | bytes 4194304 | tf_op jit(solution)/shard_map/all_to_all | solution.py:150
  329.9 63.6 %reduce-scatter.3.cloned.1.call-done = bf16[128,1024]{1,0:T(8,128)(2,1)} async-done(((bf16[2048,1024]{1,0:T(8,128)(2,1)}), bf16[128,1024]{1,0:T(8,128)(2,1)}) %reduce-scatter.3.cloned.1.call-update) | async-done | bytes 262160 | tf_op jit(solution)/shard_map/reduce_scatter | solution.py:126
  393.5 2.5 gather_fusion.8
  396.3 77.7 %reduce-scatter.5.cloned.1.call-done = bf16[128,1024]{1,0:T(8,128)(2,1)} async-done(((bf16[2048,1024]{1,0:T(8,128)(2,1)}), bf16[128,1024]{1,0:T(8,128)(2,1)}) %reduce-scatter.5.cloned.1.call-update) | async-done | bytes 262160 | tf_op jit(solution)/shard_map/reduce_scatter | solution.py:129
  473.9 2.5 gather_fusion.10
  477.5 3.0 broadcast_select_fusion.2
  480.5 9.3 %all-to-all-start.5 = ((bf16[128,2,1024]{2,1,0:T(2,128)(2,1)}), bf16[128,2,1024]{2,1,0:T(2,128)(2,1)S(1)}, u32[]{:S(2)}, u32[]{:S(2)}) async-start(bf16[128,2,1024]{2,1,0:T(2,128)(2,1)} %get-tuple-element.140), calls=%async_computation.7 | async-start | bytes 1048576 | tf_op jit(solution)/shard_map/all_to_all | solution.py:164
  490.1 13.1 %all-to-all-done.5 = bf16[128,2,1024]{2,1,0:T(2,128)(2,1)S(1)} async-done(((bf16[128,2,1024]{2,1,0:T(2,128)(2,1)}), bf16[128,2,1024]{2,1,0:T(2,128)(2,1)S(1)}, u32[]{:S(2)}, u32[]{:S(2)}) %all-to-all-start.5) | async-done | bytes 524320 | tf_op jit(solution)/shard_map/all_to_all | solution.py:164
  503.2 6.0 %all-to-all-start.4 = ((bf16[128,2,1024]{2,1,0:T(2,128)(2,1)}), bf16[128,2,1024]{2,1,0:T(2,128)(2,1)}, u32[]{:S(2)}, u32[]{:S(2)}) async-start(bf16[128,2,1024]{2,1,0:T(2,128)(2,1)} %get-tuple-element.141), calls=%async_computation.5 | async-start | bytes 1048576 | tf_op jit(solution)/shard_map/all_to_all | solution.py:157
  512.1 2.2 copy.46
  514.3 2.6 reshape.251
  516.9 2.7 reshape.254
  519.7 2.2 gather_fusion.7
  (147 shorter events, 118.9 us)
Async XLA Ops:
  7.2 55.9 %copy-start = (bf16[128,4096]{1,0:T(8,128)(2,1)S(1)}, bf16[128,4096]{1,0:T(8,128)(2,1)}, u32[]{:S(2)}) copy-start(bf16[128,4096]{1,0:T(8,128)(2,1)} %param.9) | copy-start | bytes 3145732
  7.2 4.5 copy-start.2
  11.7 14.9 %copy-start.11 = (s32[1,128]{1,0:T(1,128)S(1)}, s32[1,128]{1,0:T(1,128)}, u32[]{:S(2)}) copy-start(s32[1,128]{1,0:T(1,128)} %param.14) | copy-start | bytes 1540
  15.0 24.8 %all-to-all-start.2 = ((bf16[128,2,1024]{2,1,0:T(2,128)(2,1)}), bf16[128,2,1024]{2,1,0:T(2,128)(2,1)S(1)}, u32[]{:S(2)}, u32[]{:S(2)}) async-start(bf16[128,2,1024]{2,1,0:T(2,128)(2,1)} %get-tuple-element.142), calls=%async_computation.2 | async-start | bytes 1048576 | tf_op jit(solution)/shard_map/all_to_all | solution.py:108
  26.5 98.6 %all-gather.7.cloned.1.call-start = ((), (), s32[]{:S(2)}) async-start(), calls=%async_computation.11 | async-start | bytes 4456448 | tf_op jit(solution)/shard_map/all_gather | solution.py:118
  41.7 125.3 %all-gather.5.cloned.1.call-start = ((), (), s32[]{:S(2)}) async-start(), calls=%async_computation.10 | async-start | bytes 4456448 | tf_op jit(solution)/shard_map/all_gather | solution.py:117
  69.5 9.5 %copy-start.10 = (s32[1,16]{1,0:T(1,128)S(1)}, s32[1,16]{1,0:T(1,128)}, u32[]{:S(2)}) copy-start(s32[1,16]{1,0:T(1,128)} %param.15) | copy-start | bytes 196
  69.5 9.7 %copy-start.5 = (bf16[128,4096]{1,0:T(8,128)(2,1)S(1)}, bf16[128,4096]{1,0:T(8,128)(2,1)}, u32[]{:S(2)}) copy-start(bf16[128,4096]{1,0:T(8,128)(2,1)} %param.12) | copy-start | bytes 3145732
  72.7 45.3 %all-to-all-start = ((bf16[128,2,4096]{2,1,0:T(2,128)(2,1)}), bf16[128,2,4096]{2,1,0:T(2,128)(2,1)}, u32[]{:S(2)}, u32[]{:S(2)}) async-start(bf16[128,2,4096]{2,1,0:T(2,128)(2,1)} %broadcast_select_fusion.1), calls=%async_computation | async-start | bytes 4194304 | tf_op jit(solution)/shard_map/all_to_all | solution.py:106
  78.8 314.7 %reduce-scatter.3.cloned.1.call-start = ((), (), s32[]{:S(2)}) async-start(), calls=%async_computation.8 | async-start | bytes 4456448 | tf_op jit(solution)/shard_map/reduce_scatter | solution.py:126
  130.2 41.7 %copy-start.6 = (bf16[8,512,128]{1,2,0:T(8,128)(2,1)S(1)}, bf16[8,512,128]{1,2,0:T(8,128)(2,1)}, u32[]{:S(2)}) copy-start(bf16[8,512,128]{1,2,0:T(8,128)(2,1)} %custom-call.24) | copy-start | bytes 3145732
  298.4 5.1 copy-start.7
  303.5 170.4 %reduce-scatter.5.cloned.1.call-start = ((), (), s32[]{:S(2)}) async-start(), calls=%async_computation.9 | async-start | bytes 4456448 | tf_op jit(solution)/shard_map/reduce_scatter | solution.py:129
  308.6 2.2 copy-start.8
  321.9 158.6 %all-to-all-start.3 = ((bf16[128,2,4096]{2,1,0:T(2,128)(2,1)}), bf16[128,2,4096]{2,1,0:T(2,128)(2,1)S(1)}, u32[]{:S(2)}, u32[]{:S(2)}) async-start(bf16[128,2,4096]{2,1,0:T(2,128)(2,1)} %broadcast_select_fusion), calls=%async_computation.3 | async-start | bytes 4194304 | tf_op jit(solution)/shard_map/all_to_all | solution.py:150
  396.2 93.6 %copy-start.9 = (s32[1,128,2]{1,2,0:T(2,128)S(1)}, s32[1,128,2]{1,2,0:T(2,128)}, u32[]{:S(2)}) copy-start(s32[1,128,2]{1,2,0:T(2,128)} %param.13) | copy-start | bytes 3076
  480.5 33.8 %copy-start.3 = (bf16[128,2,4096]{2,1,0:T(2,128)(2,1)}, bf16[128,2,4096]{2,1,0:T(2,128)(2,1)S(1)}, u32[]{:S(2)}) copy-start(bf16[128,2,4096]{2,1,0:T(2,128)(2,1)S(1)} %all-to-all-done.3) | copy-start | bytes 6291460
  480.5 22.7 %all-to-all-start.5 = ((bf16[128,2,1024]{2,1,0:T(2,128)(2,1)}), bf16[128,2,1024]{2,1,0:T(2,128)(2,1)S(1)}, u32[]{:S(2)}, u32[]{:S(2)}) async-start(bf16[128,2,1024]{2,1,0:T(2,128)(2,1)} %get-tuple-element.140), calls=%async_computation.7 | async-start | bytes 1048576 | tf_op jit(solution)/shard_map/all_to_all | solution.py:164
  503.2 7.5 %copy-start.4 = (bf16[128,2,1024]{2,1,0:T(2,128)(2,1)}, bf16[128,2,1024]{2,1,0:T(2,128)(2,1)S(1)}, u32[]{:S(2)}) copy-start(bf16[128,2,1024]{2,1,0:T(2,128)(2,1)S(1)} %all-to-all-done.5) | copy-start | bytes 1572868
  503.2 21.4 %all-to-all-start.4 = ((bf16[128,2,1024]{2,1,0:T(2,128)(2,1)}), bf16[128,2,1024]{2,1,0:T(2,128)(2,1)}, u32[]{:S(2)}, u32[]{:S(2)}) async-start(bf16[128,2,1024]{2,1,0:T(2,128)(2,1)} %get-tuple-element.141), calls=%async_computation.5 | async-start | bytes 1048576 | tf_op jit(solution)/shard_map/all_to_all | solution.py:157
  519.7 7.8 %copy-start.1 = (bf16[128,4096]{1,0:T(8,128)(2,1)S(1)}, bf16[128,4096]{1,0:T(8,128)(2,1)}, u32[]{:S(2)}) copy-start(bf16[128,4096]{1,0:T(8,128)(2,1)} %param.9) | copy-start | bytes 3145732
Sparse Core Ops, SparseCore 0:
  41.8 68.3 all-gather.6
  112.9 54.0 all-gather.4
  303.7 89.7 reduce-scatter.2
  397.0 76.8 reduce-scatter.4
where the time goes:
time: 544 us; the launch traced here: 534 us
  waiting for transfers between devices  239 us (44%)
  matrix products  98.9 us (18%)
  local copies, waits for them, and re-layouts  78.3 us (14%)
  other arithmetic  42.6 us (8%)
  starting transfers between devices  41.4 us (8%)
  blocking collectives  19.6 us (4%)
  between operations  14.7 us (3%)
    reduce_scatter x1, waiting for transfers between devices, local(): lax.psum_scatter(part_v.astype(jnp.bfloat16), 'ctx', scatter_dimension=0,...  77.7 us
    reduce_scatter x1, waiting for transfers between devices, local(): lax.psum_scatter(part_k.astype(jnp.bfloat16), 'ctx', scatter_dimension=0,...  63.6 us
    all_gather x1, waiting for transfers between devices, local(): lax.all_gather(k_bal, 'ctx', axis=0, tiled=True)  36.8 us
    all_to_all x1, waiting for transfers between devices, local(): lax.all_to_all(sent_q, ('dp', 'ctx'), split_axis=0, concat_axis=0, tiled=...  34.3 us
    dot_general x8, matrix products, per_group(): jnp.einsum('rk,rd->kd', prob_low, grad_head, preferred_element_type=jnp.f...  19.7 us
    all_to_all x1, blocking collectives, local(): lax.all_to_all(sent_k, ('dp', 'ctx'), split_axis=0, concat_axis=0, tiled=...  19.6 us
    dot_general x8, matrix products, per_group(): jnp.dot(dscores, key_head, preferred_element_type=jnp.float32)  19.3 us
    dot_general x8, matrix products, per_group(): jnp.einsum('rd,kd->rk', grad_head, value_head, preferred_element_type=jnp...  16.4 us
  transfers between devices with their start and end apart: 9, of which 6 were waited for; matrix products, arithmetic and copies ran while one was open for 13% of the time, Pallas kernels for 0%

commit v1 on v0

v1 whole, which is shorter than its diff:
```python
import functools
import math

import jax
import jax.numpy as jnp
from jax import lax
from jax.experimental import pallas as pl
from jax.experimental.pallas import tpu as pltpu
from jax.sharding import PartitionSpec as P

H = 32
KVH = 8
DH = 128
TOK = 128
CTX = 16
DP = 8
DEV = 128
SEQ = 2048
MOST = 1024
COLS = 512
K = 32
GROWS = 144
BQ = 128
BK = 256
WMAX = MOST // BK + 1
VMEM_LIMIT = 56 * 2**20

F32 = jnp.float32
BF16 = jnp.bfloat16
MESH = pl.DeviceIdType.MESH


def dot(a, b, ca, cb):
    return lax.dot_general(a, b, (((ca,), (cb,)), ((), ())), preferred_element_type=F32)


def iota(shape, dim):
    return lax.broadcasted_iota(jnp.int32, shape, dim)


def pack_kernel(prow, pcol, unp, q, k, v, g, send, sendg, sel, sel_s):
    @pl.when(pl.program_id(0) == 0)
    def _():
        occupied = (prow[...] >= 0).astype(BF16)
        a, b = iota((256, 256), 0), iota((256, 256), 1)
        earlier = ((a < b) & (a // 32 == b // 32)).astype(BF16)
        rank = dot(jnp.broadcast_to(occupied, (16, 256)), earlier, 1, 0)[0:1]
        slot = iota((1, 256), 1) // 32 * K + rank.astype(jnp.int32)
        slot = jnp.where(prow[...] >= 0, slot, -1)
        place = (iota((8 * K, 256), 0) == slot).astype(BF16)
        holds = (pcol[...] == iota((256, TOK), 1)).astype(BF16)
        value = dot(place, holds, 1, 0).astype(BF16)
        sel_s[...] = value
        sel[...] = value

    s = sel_s[...]
    yq = dot(s, q[...], 1, 0)
    yk = dot(s, k[...], 1, 0)
    yv = dot(s, v[...], 1, 0)
    for d in range(DP):
        rows = slice(d * K, (d + 1) * K)
        for e in range(2):
            send[d, e, :, 0:256] = yq[rows, e * 256 : (e + 1) * 256].astype(BF16)
            send[d, e, :, 256:384] = yk[rows].astype(BF16)
            send[d, e, :, 384:512] = yv[rows].astype(BF16)
    ints = jnp.broadcast_to(unp[...].astype(F32), (16, TOK)).astype(BF16)
    for e in range(2):
        sendg[e, 0:TOK, :] = g[:, e * 256 : (e + 1) * 256]
        sendg[e, TOK:GROWS, 0:TOK] = ints
        sendg[e, TOK:GROWS, TOK:256] = jnp.zeros((16, 128), BF16)


def pack(prow, pcol, unp, q, k, v, g):
    whole = lambda shape: pl.BlockSpec(shape, lambda i: (0,) * len(shape))
    return pl.pallas_call(
        pack_kernel,
        grid=(KVH,),
        in_specs=[
            whole((1, 256)),
            whole((256, 1)),
            whole((1, TOK)),
            pl.BlockSpec((TOK, 512), lambda i: (0, i)),
            pl.BlockSpec((TOK, 128), lambda i: (0, i)),
            pl.BlockSpec((TOK, 128), lambda i: (0, i)),
            pl.BlockSpec((TOK, 512), lambda i: (0, i)),
        ],
        out_specs=[
            pl.BlockSpec((DP, 2, K, COLS), lambda i: (0, i, 0, 0)),
            pl.BlockSpec((2, GROWS, 256), lambda i: (i, 0, 0)),
            whole((8 * K, TOK)),
        ],
        out_shape=[
            jax.ShapeDtypeStruct((DP, CTX, K, COLS), BF16),
            jax.ShapeDtypeStruct((CTX, GROWS, 256), BF16),
            jax.ShapeDtypeStruct((8 * K, TOK), BF16),
        ],
        scratch_shapes=[pltpu.VMEM((8 * K, TOK), BF16)],
        compiler_params=pltpu.CompilerParams(vmem_limit_bytes=VMEM_LIMIT),
        name="pack_rows_to_messages",
    )(prow, pcol, unp, q, k, v, g)


def exchange_kernel(src, srcg, dst, dstg, send_sem, recv_sem, sendg_sem, recvg_sem, own_sem, owng_sem):
    d = lax.axis_index("dp")
    c = lax.axis_index("ctx")
    me = d * CTX + c
    z, core = lax.div(d, 2), lax.rem(d, 2)
    x, y = lax.div(c, 4), lax.rem(c, 4)

    own = pltpu.make_async_copy(src.at[me], dst.at[me], own_sem)
    own.start()
    owng = pltpu.make_async_copy(srcg.at[c], dstg.at[c], owng_sem)
    owng.start()

    def one(n):
        j = lax.rem(n * 37, DEV)
        dy = lax.rem(j, 2) + 2 * lax.rem(lax.div(j, 16), 2)
        dx = lax.rem(lax.div(j, 2), 2) + 2 * lax.rem(lax.div(j, 32), 2)
        dz = lax.rem(lax.div(j, 4), 2) + 2 * lax.div(j, 64)
        dcore = lax.rem(lax.div(j, 8), 2)
        td = lax.rem(z + dz, 4) * 2 + lax.rem(core + dcore, 2)
        tc = lax.rem(x + dx, 4) * 4 + lax.rem(y + dy, 4)
        pltpu.make_async_remote_copy(
            src_ref=src.at[td * CTX + tc],
            dst_ref=dst.at[me],
            send_sem=send_sem,
            recv_sem=recv_sem,
            device_id=(td, tc),
            device_id_type=MESH,
        ).start()

    def turn(n, carry):
        tc = lax.rem(c + lax.rem(n * 5, CTX), CTX)
        pltpu.make_async_remote_copy(
            src_ref=srcg.at[tc],
            dst_ref=dstg.at[c],
            send_sem=sendg_sem,
            recv_sem=recvg_sem,
            device_id=(d, tc),
            device_id_type=MESH,
        ).start()
        for i in range(8):
            one(8 * n - 8 + i + 1)
        return carry

    lax.fori_loop(1, CTX, turn, 0)
    for n in range(121, DEV):
        one(n)
    own.wait()
    owng.wait()
    pltpu.make_async_remote_copy(
        src_ref=srcg.at[pl.ds(0, CTX - 1)],
        dst_ref=dstg.at[pl.ds(0, CTX - 1)],
        send_sem=sendg_sem,
        recv_sem=recvg_sem,
        device_id=(d, c),
        device_id_type=MESH,
    ).wait()
    pltpu.make_async_remote_copy(
        src_ref=src.at[pl.ds(0, DEV - 1)],
        dst_ref=dst.at[pl.ds(0, DEV - 1)],
        send_sem=send_sem,
        recv_sem=recv_sem,
        device_id=(d, c),
        device_id_type=MESH,
    ).wait()


def exchange(src, srcg):
    return pl.pallas_call(
        exchange_kernel,
        in_specs=[pl.BlockSpec(memory_space=pl.ANY)] * 2,
        out_specs=[pl.BlockSpec(memory_space=pl.ANY)] * 2,
        out_shape=[
            jax.ShapeDtypeStruct(src.shape, src.dtype),
            jax.ShapeDtypeStruct(srcg.shape, srcg.dtype),
        ],
        scratch_shapes=[pltpu.SemaphoreType.DMA] * 6,
        compiler_params=pltpu.CompilerParams(has_side_effects=True),
        name="exchange",
    )(src, srcg)


def attention_kernel(lengths, recv, recvg, att, back, x, xo, mid, ts, dk, dv, col):
    scale = 1.0 / math.sqrt(DH)

    def slots_of(c):
        row = recvg[c, TOK : TOK + 8, 0:TOK].astype(F32)[0:1]
        return (iota((256, TOK), 0).astype(F32) == row).astype(BF16)

    occ = jnp.zeros((256, 128), F32)
    for c in range(CTX):
        occ = occ + dot(slots_of(c), (iota((TOK, 128), 1) == c).astype(BF16), 1, 0)
    pair = (iota((256, 256), 0) // 2 == iota((256, 256), 1) // 2).astype(BF16)
    count = dot(pair, occ.astype(BF16), 1, 0)
    before = (iota((128, 128), 0) < iota((128, 128), 1)).astype(BF16)
    base = dot(count.astype(BF16), before, 1, 0)
    u = iota((256, 128), 0)
    col[...] = base + (u % 2 + (u // 2) % 8 * K).astype(F32)

    lanes = iota((16, 8 * K), 1).astype(F32)

    def sort_senders(grp, carry):
        r0 = pl.multiple_of(grp * 16, 16)
        tab = col[pl.ds(r0, 16), :]
        t = jnp.concatenate(
            [(lanes == tab[:, c : c + 1]).astype(F32) for c in range(CTX)], axis=0
        ).astype(BF16)
        ts[grp] = t
        rows = dot(t, recv[grp], 1, 0).astype(BF16)
        for c in range(CTX):
            mid[c, pl.ds(r0, 16), :] = rows[c * 16 : (c + 1) * 16]
        return carry

    lax.fori_loop(0, 16, sort_senders, 0)

    def sort_rows(c, carry):
        x[pl.ds(pl.multiple_of(c * TOK, TOK), TOK), :] = dot(slots_of(c), mid[c], 0, 0).astype(BF16)
        return carry

    lax.fori_loop(0, CTX, sort_rows, 0)

    dk[...] = jnp.zeros_like(dk)
    dv[...] = jnp.zeros_like(dv)

    def doc_start(position):
        def step(n, carry):
            start, end = carry
            return (jnp.where(end <= position, end, start), end + lengths[0, n])

        return lax.fori_loop(0, 16, step, (jnp.int32(0), jnp.int32(0)))[0]

    def starts_of(positions):
        def step(n, carry):
            start, end = carry
            return (jnp.where(end <= positions, end, start), end + lengths[0, n])

        return lax.fori_loop(0, 16, step, (jnp.zeros_like(positions), jnp.int32(0)))[0]

    def tile(i, carry):
        q0 = pl.multiple_of(i * BQ, BQ)
        lo = doc_start(q0) // BK
        width = q0 // BK - lo + 1

        def attend(w):
            k0 = pl.multiple_of(lo * BK, BK)
            span = w * BK
            keys = x[pl.ds(k0, span), 256:384]
            values = x[pl.ds(k0, span), 384:512]
            queries = jnp.concatenate([x[pl.ds(q0, BQ), 0:128], x[pl.ds(q0, BQ), 128:256]], axis=0)
            grads = jnp.concatenate([recvg[i, 0:TOK, 0:128], recvg[i, 0:TOK, 128:256]], axis=0)
            qpos = q0 + iota((BQ, 1), 0)
            qstart = starts_of(qpos)
            qpos = jnp.concatenate([qpos, qpos], axis=0)
            qstart = jnp.concatenate([qstart, qstart], axis=0)
            kpos = k0 + iota((2 * BQ, span), 1)
            s = dot(queries, keys, 1, 1) * scale
            s = jnp.where((kpos >= qstart) & (kpos <= qpos), s, -1e30)
            top = jnp.max(s, axis=1, keepdims=True)
            e = jnp.exp(s - top)
            p = e * (1.0 / jnp.sum(e, axis=1, keepdims=True))
            low = p.astype(BF16)
            out = dot(low, values, 1, 0).astype(BF16)
            att[i, :, 0:128] = out[0:BQ]
            att[i, :, 128:256] = out[BQ:]
            delta = jnp.sum(grads.astype(F32) * out.astype(F32), axis=1, keepdims=True)
            dp = dot(grads, values, 1, 1)
            ds = (p * (dp - delta) * scale).astype(BF16)
            dq = dot(ds, keys, 1, 0).astype(BF16)
            xo[pl.ds(q0, BQ), 0:128] = dq[0:BQ]
            xo[pl.ds(q0, BQ), 128:256] = dq[BQ:]
            dk[pl.ds(k0, span), :] += dot(ds, queries, 0, 0)
            dv[pl.ds(k0, span), :] += dot(low, grads, 0, 0)

        for w in range(1, WMAX + 1):
            pl.when(width == w)(functools.partial(attend, w))
        return carry

    lax.fori_loop(0, SEQ // BQ, tile, 0)
    xo[:, 256:384] = dk[...].astype(BF16)
    xo[:, 384:512] = dv[...].astype(BF16)

    def unsort_rows(c, carry):
        mid[c] = dot(
            slots_of(c), xo[pl.ds(pl.multiple_of(c * TOK, TOK), TOK), :], 1, 0
        ).astype(BF16)
        return carry

    lax.fori_loop(0, CTX, unsort_rows, 0)

    def unsort_senders(grp, carry):
        r0 = pl.multiple_of(grp * 16, 16)
        rows = jnp.concatenate([mid[c, pl.ds(r0, 16), :] for c in range(CTX)], axis=0)
        back[grp] = dot(ts[grp], rows, 0, 0).astype(BF16)
        return carry

    lax.fori_loop(0, 16, unsort_senders, 0)


def attention(lengths, recv, recvg):
    vmem = pl.BlockSpec(memory_space=pltpu.VMEM)
    return pl.pallas_call(
        attention_kernel,
        in_specs=[pl.BlockSpec(memory_space=pltpu.SMEM), vmem, vmem],
        out_specs=[vmem, vmem],
        out_shape=[
            jax.ShapeDtypeStruct((CTX, TOK, 256), BF16),
            jax.ShapeDtypeStruct((16, 8 * K, COLS), BF16),
        ],
        scratch_shapes=[
            pltpu.VMEM((SEQ, COLS), BF16),
            pltpu.VMEM((SEQ, COLS), BF16),
            pltpu.VMEM((CTX, 256, COLS), BF16),
            pltpu.VMEM((16, 256, 8 * K), BF16),
            pltpu.VMEM((SEQ, DH), F32),
            pltpu.VMEM((SEQ, DH), F32),
            pltpu.VMEM((256, 128), F32),
        ],
        compiler_params=pltpu.CompilerParams(vmem_limit_bytes=VMEM_LIMIT),
        name="attention",
    )(lengths, recv, recvg)


def unpack_kernel(sel, back, att, attended, gq, gk, gv):
    s = sel[...]
    for e in range(2):
        attended[:, e * 256 : (e + 1) * 256] = att[e]
    parts = []
    for e in range(2):
        rows = jnp.concatenate([back[d, e].astype(F32) for d in range(DP)], axis=0).astype(BF16)
        parts.append(dot(s, rows, 0, 0))
        gq[:, e * 256 : (e + 1) * 256] = parts[e][:, 0:256].astype(BF16)
    both = parts[0][:, 256:] + parts[1][:, 256:]
    gk[...] = both[:, 0:128].astype(BF16)
    gv[...] = both[:, 128:256].astype(BF16)


def unpack_rows(sel, back, att):
    return pl.pallas_call(
        unpack_kernel,
        grid=(KVH,),
        in_specs=[
            pl.BlockSpec((8 * K, TOK), lambda i: (0, 0)),
            pl.BlockSpec((DP, 2, K, COLS), lambda i: (0, i, 0, 0)),
            pl.BlockSpec((2, TOK, 256), lambda i: (i, 0, 0)),
        ],
        out_specs=[
            pl.BlockSpec((TOK, 512), lambda i: (0, i)),
            pl.BlockSpec((TOK, 512), lambda i: (0, i)),
            pl.BlockSpec((TOK, 128), lambda i: (0, i)),
            pl.BlockSpec((TOK, 128), lambda i: (0, i)),
        ],
        out_shape=[
            jax.ShapeDtypeStruct((TOK, H * DH), BF16),
            jax.ShapeDtypeStruct((TOK, H * DH), BF16),
            jax.ShapeDtypeStruct((TOK, KVH * DH), BF16),
            jax.ShapeDtypeStruct((TOK, KVH * DH), BF16),
        ],
        compiler_params=pltpu.CompilerParams(vmem_limit_bytes=VMEM_LIMIT),
        name="messages_to_rows",
    )(sel, back, att)


def local(q_load, k_load, v_load, grad_out, pack_rows, unpack, doc_lengths):
    flat = pack_rows.reshape(1, 2 * DEV)
    send, sendg, sel = pack(
        flat, flat.reshape(2 * DEV, 1), unpack, q_load, k_load, v_load, grad_out
    )
    recv, recvg = exchange(send.reshape(DEV, K, COLS), sendg)
    att, back = attention(doc_lengths, recv.reshape(16, 8 * K, COLS), recvg)
    returned, turned = exchange(back.reshape(DEV, K, COLS), att)
    return unpack_rows(sel, returned.reshape(DP, CTX, K, COLS), turned)


def solution(mesh):
    rows = P(("dp", "ctx"), None)
    return jax.shard_map(
        local,
        mesh=mesh,
        in_specs=(rows, rows, rows, rows, P(("dp", "ctx"), None, None), rows, P("dp", None)),
        out_specs=(rows, rows, rows, rows),
        check_vma=False,
    )
```

time: 544 us -> 210 us (0.39); the launches traced: 534 us -> 209 us
  waiting for transfers between devices: 239 us -> 0 us
  Pallas kernels: 0 us -> 207 us
  matrix products: 98.9 us -> 0 us
  local copies, waits for them, and re-layouts: 78.3 us -> 2.23 us
  other arithmetic: 42.6 us -> 0 us
  starting transfers between devices: 41.4 us -> 0 us
  blocking collectives: 19.6 us -> 0 us
  between operations: 14.7 us -> 0.65 us
    pallas_call x0 -> x5, Pallas kernels: none -> 207 us  [the longest x2 147 us: exchange(): pl.pallas_call(exchange_kernel, in_specs=[pl.BlockSpec(memory_space=pl.AN...]
    reduce_scatter x2 -> x0, waiting for transfers between devices: 141 us -> none  [the longest x1 77.7 us: local(): lax.psum_scatter(part_v.astype(jnp.bfloat16), 'ctx', scatter_dimension=0,...]
    dot_general x48 -> x0, matrix products: 98.9 us -> none  [the longest x8 19.7 us: per_group(): jnp.einsum('rk,rd->kd', prob_low, grad_head, preferred_element_type=jnp.f...]
    all_to_all x5 -> x0, waiting for transfers between devices: 60.7 us -> none  [the longest x1 34.3 us: local(): lax.all_to_all(sent_q, ('dp', 'ctx'), split_axis=0, concat_axis=0, tiled=...]
    all_to_all x5 -> x0, starting transfers between devices: 41 us -> none  [the longest x1 11.5 us: local(): lax.all_to_all(sent_v, ('dp', 'ctx'), split_axis=0, concat_axis=0, tiled=...]
    all_gather x2 -> x0, waiting for transfers between devices: 36.8 us -> none  [the longest x1 36.8 us: local(): lax.all_gather(k_bal, 'ctx', axis=0, tiled=True)]
    gather x18 -> x0, local copies, waits for them, and re-layouts: 31.8 us -> none  [the longest x6 10.8 us: outgoing_back(): taken = block[source_row]]
    reshape x15 -> x1, local copies, waits for them, and re-layouts: 21.8 us -> 0.7 us  [local(): flat = pack_rows.reshape(1, 2 * DEV)]
  transfers between devices with their start and end apart: 9 -> 0, of which waited for: 6 -> 0; matrix products, arithmetic and copies ran while one was open for 13% -> 0% of each run, Pallas kernels for 0% -> 0%
where the time goes in v1:
time: 210 us; the launch traced here: 209 us
  Pallas kernels  207 us (99%)
  local copies, waits for them, and re-layouts  2.23 us (1%)
    pallas_call x2, Pallas kernels, exchange(): pl.pallas_call(exchange_kernel, in_specs=[pl.BlockSpec(memory_space=pl.AN...  147 us
    pallas_call x1, Pallas kernels, attention(): pl.pallas_call(attention_kernel, in_specs=[pl.BlockSpec(memory_space=pltp...  44.2 us
    pallas_call x1, Pallas kernels, pack(): pl.pallas_call(pack_kernel, grid=(KVH,), in_specs=[whole((1, 256)), whole...  7.97 us
    pallas_call x1, Pallas kernels, unpack_rows(): pl.pallas_call(unpack_kernel, grid=(KVH,), in_specs=[pl.BlockSpec((8 * K,...  7.01 us

profile of v1, /device:TPU:1, one launch (start us, length us, event | category | flops | bytes accessed | tf_op | source)
XLA Modules:
  0.0 209.5 jit_solution(6915919368406293928)
XLA Ops:
  0.6 0.8 copy.13
  1.4 0.7 reshape.23.prow
  2.1 0.7 reshape_reshape.4.pcol
  2.9 8.0 %pack_rows_to_messages.1 = (bf16[8,16,32,512]{3,2,1,0:T(8,128)(2,1)}, bf16[16,144,256]{2,1,0:T(8,128)(2,1)}, bf16[256,128]{1,0:T(8,128)(2,1)}) custom-call(s32[1,256]{1,0:T(1,128)} %reshape.23.prow, s32[256,1]{1,0:T(8,128)} %reshape_reshape.4.pcol, s32[1,128]{1,0:T(1,128)} %unp.1, bf16[128,4096]{1,0:T(8,128)(2,1)} %q.1, bf16[128,1024]{1,0:T(8,128)(2,1)} %k.1, ...), custom_call_target="tpu_custom_call" | custom-call | tf_op jit(solution)/shard_map/pack_rows_to_messages/pallas_call | solution.py:75
  10.8 78.0 %exchange.2 = (bf16[128,32,512]{2,1,0:T(8,128)(2,1)}, bf16[16,144,256]{2,1,0:T(8,128)(2,1)}) custom-call(bf16[128,32,512]{2,1,0:T(8,128)(2,1)} %bitcast.6, bf16[16,144,256]{2,1,0:T(8,128)(2,1)} %get-tuple-element.15.srcg), custom_call_target="tpu_custom_call" | custom-call | tf_op jit(solution)/shard_map/exchange/pallas_call | solution.py:170
  88.8 44.2 %attention.1 = (bf16[16,128,256]{2,1,0:T(8,128)(2,1)}, bf16[16,256,512]{2,1,0:T(8,128)(2,1)}) custom-call(s32[1,16]{1,0:T(1,128)} %lengths.1, bf16[16,256,512]{2,1,0:T(8,128)(2,1)} %bitcast.7, bf16[16,144,256]{2,1,0:T(8,128)(2,1)} %get-tuple-element.17.recvg), custom_call_target="tpu_custom_call" | custom-call | tf_op jit(solution)/shard_map/attention/pallas_call | solution.py:302
  133.0 69.4 %exchange.3 = (bf16[128,32,512]{2,1,0:T(8,128)(2,1)}, bf16[16,128,256]{2,1,0:T(8,128)(2,1)}) custom-call(bf16[128,32,512]{2,1,0:T(8,128)(2,1)} %bitcast.4, bf16[16,128,256]{2,1,0:T(8,128)(2,1)} %get-tuple-element.19.srcg), custom_call_target="tpu_custom_call" | custom-call | tf_op jit(solution)/shard_map/exchange/pallas_call | solution.py:170
  202.4 7.0 %messages_to_rows.1 = (bf16[128,4096]{1,0:T(8,128)(2,1)}, bf16[128,4096]{1,0:T(8,128)(2,1)}, bf16[128,1024]{1,0:T(8,128)(2,1)}, bf16[128,1024]{1,0:T(8,128)(2,1)}) custom-call(bf16[256,128]{1,0:T(8,128)(2,1)} %get-tuple-element.13.sel, bf16[8,16,32,512]{3,2,1,0:T(8,128)(2,1)} %bitcast.5, bf16[16,128,256]{2,1,0:T(8,128)(2,1)} %get-tuple-element.21.att), custom_call_target="tpu_custom_call" | custom-call | tf_op jit(solution)/shard_map/messages_to_rows/pallas_call | solution.py:339

commit v2 on v1

--- a/solution.py
+++ b/solution.py
@@ -18,7 +18,8 @@
 SEQ = 2048
 MOST = 1024
 COLS = 512
-K = 32
+FULL = 32
+SHORT = 24
 GROWS = 144
 BQ = 128
 BK = 256
@@ -38,15 +39,19 @@
     return lax.broadcasted_iota(jnp.int32, shape, dim)
 
 
-def pack_kernel(prow, pcol, unp, q, k, v, g, send, sendg, sel, sel_s):
+def pack_kernel(K, prow, pcol, unp, q, k, v, g, send, sendg, sel, sel_s, over_s):
     @pl.when(pl.program_id(0) == 0)
     def _():
         occupied = (prow[...] >= 0).astype(BF16)
         a, b = iota((256, 256), 0), iota((256, 256), 1)
         earlier = ((a < b) & (a // 32 == b // 32)).astype(BF16)
         rank = dot(jnp.broadcast_to(occupied, (16, 256)), earlier, 1, 0)[0:1]
-        slot = iota((1, 256), 1) // 32 * K + rank.astype(jnp.int32)
-        slot = jnp.where(prow[...] >= 0, slot, -1)
+        rank = rank.astype(jnp.int32)
+        slot = iota((1, 256), 1) // 32 * K + rank
+        slot = jnp.where((prow[...] >= 0) & ((rank < K - 1) | (K == FULL)), slot, -1)
+        over = jnp.max(jnp.where((prow[...] >= 0) & (rank >= K - 1), 1.0, 0.0), axis=1, keepdims=True)
+        last = (iota((8 * K, TOK), 0) % K == K - 1) & (K < FULL)
+        over_s[...] = jnp.where(last, over, 0.0)
         place = (iota((8 * K, 256), 0) == slot).astype(BF16)
         holds = (pcol[...] == iota((256, TOK), 1)).astype(BF16)
         value = dot(place, holds, 1, 0).astype(BF16)
@@ -56,7 +61,7 @@
     s = sel_s[...]
     yq = dot(s, q[...], 1, 0)
     yk = dot(s, k[...], 1, 0)
-    yv = dot(s, v[...], 1, 0)
+    yv = dot(s, v[...], 1, 0) + over_s[...]
     for d in range(DP):
         rows = slice(d * K, (d + 1) * K)
         for e in range(2):
@@ -70,10 +75,10 @@
         sendg[e, TOK:GROWS, TOK:256] = jnp.zeros((16, 128), BF16)
 
 
-def pack(prow, pcol, unp, q, k, v, g):
+def pack(K, prow, pcol, unp, q, k, v, g):
     whole = lambda shape: pl.BlockSpec(shape, lambda i: (0,) * len(shape))
     return pl.pallas_call(
-        pack_kernel,
+        functools.partial(pack_kernel, K),
         grid=(KVH,),
         in_specs=[
             whole((1, 256)),
@@ -94,7 +99,7 @@
             jax.ShapeDtypeStruct((CTX, GROWS, 256), BF16),
             jax.ShapeDtypeStruct((8 * K, TOK), BF16),
         ],
-        scratch_shapes=[pltpu.VMEM((8 * K, TOK), BF16)],
+        scratch_shapes=[pltpu.VMEM((8 * K, TOK), BF16), pltpu.VMEM((8 * K, TOK), F32)],
         compiler_params=pltpu.CompilerParams(vmem_limit_bytes=VMEM_LIMIT),
         name="pack_rows_to_messages",
     )(prow, pcol, unp, q, k, v, g)
@@ -181,7 +186,7 @@
     )(src, srcg)
 
 
-def attention_kernel(lengths, recv, recvg, att, back, x, xo, mid, ts, dk, dv, col):
+def attention_kernel(K, lengths, recv, recvg, att, back, x, xo, mid, ts, dk, dv, col):
     scale = 1.0 / math.sqrt(DH)
 
     def slots_of(c):
@@ -297,10 +302,10 @@
     lax.fori_loop(0, 16, unsort_senders, 0)
 
 
-def attention(lengths, recv, recvg):
+def attention(K, lengths, recv, recvg):
     vmem = pl.BlockSpec(memory_space=pltpu.VMEM)
     return pl.pallas_call(
-        attention_kernel,
+        functools.partial(attention_kernel, K),
         in_specs=[pl.BlockSpec(memory_space=pltpu.SMEM), vmem, vmem],
         out_specs=[vmem, vmem],
         out_shape=[
@@ -335,7 +340,7 @@
     gv[...] = both[:, 128:256].astype(BF16)
 
 
-def unpack_rows(sel, back, att):
+def unpack_rows(K, sel, back, att):
     return pl.pallas_call(
         unpack_kernel,
         grid=(KVH,),
@@ -361,15 +366,30 @@
     )(sel, back, att)
 
 
-def local(q_load, k_load, v_load, grad_out, pack_rows, unpack, doc_lengths):
+def forward(K, q_load, k_load, v_load, grad_out, pack_rows, unpack):
     flat = pack_rows.reshape(1, 2 * DEV)
     send, sendg, sel = pack(
-        flat, flat.reshape(2 * DEV, 1), unpack, q_load, k_load, v_load, grad_out
+        K, flat, flat.reshape(2 * DEV, 1), unpack, q_load, k_load, v_load, grad_out
     )
     recv, recvg = exchange(send.reshape(DEV, K, COLS), sendg)
-    att, back = attention(doc_lengths, recv.reshape(16, 8 * K, COLS), recvg)
+    return sel, recv, recvg
+
+
+def finish(K, doc_lengths, sel, recv, recvg):
+    att, back = attention(K, doc_lengths, recv.reshape(16, 8 * K, COLS), recvg)
     returned, turned = exchange(back.reshape(DEV, K, COLS), att)
-    return unpack_rows(sel, returned.reshape(DP, CTX, K, COLS), turned)
+    return unpack_rows(K, sel, returned.reshape(DP, CTX, K, COLS), turned)
+
+
+def local(q_load, k_load, v_load, grad_out, pack_rows, unpack, doc_lengths):
+    operands = (q_load, k_load, v_load, grad_out, pack_rows, unpack)
+    sel, recv, recvg = forward(SHORT, *operands)
+    over = jnp.max(recv[:, SHORT - 1, COLS - 1].astype(F32)) > 0.5
+    return lax.cond(
+        over,
+        lambda: finish(FULL, doc_lengths, *forward(FULL, *operands)),
+        lambda: finish(SHORT, doc_lengths, sel, recv, recvg),
+    )
 
 
 def solution(mesh):

time: 210 us -> 188 us (0.90)
  Pallas kernels: 207 us -> 182 us
    pallas_call x2, Pallas kernels: 147 us -> 126 us  [exchange(): pl.pallas_call(exchange_kernel, in_specs=[pl.BlockSpec(memory_space=pl.AN...]
    pallas_call x2, Pallas kernels: 52.2 us -> 49 us  [the longest x1 41.2 us: attention(): pl.pallas_call(functools.partial(attention_kernel, K), in_specs=[pl.Block...]
where the time goes in v2:
time: 188 us; the launch traced here: 187 us
  Pallas kernels  182 us (97%)
  local copies, waits for them, and re-layouts  2.26 us (1%)
    pallas_call x2, Pallas kernels, exchange(): pl.pallas_call(exchange_kernel, in_specs=[pl.BlockSpec(memory_space=pl.AN...  126 us
    pallas_call x1, Pallas kernels, attention(): pl.pallas_call(functools.partial(attention_kernel, K), in_specs=[pl.Block...  41.2 us
    pallas_call x1, Pallas kernels, pack(): pl.pallas_call(functools.partial(pack_kernel, K), grid=(KVH,), in_specs=[...  7.84 us
    pallas_call x1, Pallas kernels, unpack_rows(): pl.pallas_call(unpack_kernel, grid=(KVH,), in_specs=[pl.BlockSpec((8 * K,...  6.81 us

profile of v2, /device:TPU:1, one launch (start us, length us, event | category | flops | bytes accessed | tf_op | source)
XLA Modules:
  0.0 187.4 jit_solution(5067558345434996555)
XLA Ops:
  0.6 0.8 copy.23
  1.4 0.7 reshape.41.prow
  2.1 0.7 reshape_reshape.4.pcol
  2.9 0.0 copy-start
  2.9 0.0 copy-start.1
  2.9 0.0 copy-start.2
  2.9 0.0 copy-start.4
  2.9 0.0 copy-start.5
  2.9 0.0 copy-start.6
  2.9 7.8 %pack_rows_to_messages.3 = (bf16[8,16,24,512]{3,2,1,0:T(8,128)(2,1)}, bf16[16,144,256]{2,1,0:T(8,128)(2,1)}, bf16[192,128]{1,0:T(8,128)(2,1)}) custom-call(s32[1,256]{1,0:T(1,128)} %reshape.41.prow, s32[256,1]{1,0:T(8,128)} %reshape_reshape.4.pcol, s32[1,128]{1,0:T(1,128)} %unp.1, bf16[128,4096]{1,0:T(8,128)(2,1)} %q.1, bf16[128,1024]{1,0:T(8,128)(2,1)} %k.1, ...), custom_call_target="tpu_custom_call" | custom-call | tf_op jit(solution)/shard_map/pack_rows_to_messages/pallas_call | solution.py:80
  10.7 65.9 %exchange.7 = (bf16[128,24,512]{2,1,0:T(8,128)(2,1)}, bf16[16,144,256]{2,1,0:T(8,128)(2,1)S(1)}) custom-call(bf16[128,24,512]{2,1,0:T(8,128)(2,1)} %bitcast.14, bf16[16,144,256]{2,1,0:T(8,128)(2,1)} %get-tuple-element.56.srcg), custom_call_target="tpu_custom_call" | custom-call | tf_op jit(solution)/shard_map/exchange/pallas_call | solution.py:175
  76.7 1.8 slice_reduce_fusion
  79.1 0.0 copy-done
  79.1 0.0 copy-done.1
  79.1 0.0 copy-done.2
  79.1 0.0 copy-done.4
  79.2 0.0 copy-done.5
  79.2 0.0 copy-done.6
  79.2 108.1 %conditional.1 = ((bf16[128,4096]{1,0:T(8,128)(2,1)}, bf16[128,4096]{1,0:T(8,128)(2,1)}, bf16[128,1024]{1,0:T(8,128)(2,1)}, bf16[128,1024]{1,0:T(8,128)(2,1)})) conditional(s32[]{:T(128)} %convert_element_type.4, (bf16[128,24,512]{2,1,0:T(8,128)(2,1)}, s32[1,16]{1,0:T(1,128)S(1)}, bf16[16,144,256]{2,1,0:T(8,128)(2,1)S(1)}, ...), branch_computations={%region_1.0_spmd, %region_2.0_spmd} | conditional | bytes 196644 | solution.py:388
  79.2 41.2 %attention.2 = (bf16[16,128,256]{2,1,0:T(8,128)(2,1)}, bf16[16,192,512]{2,1,0:T(8,128)(2,1)}) custom-call(s32[1,16]{1,0:T(1,128)S(1)} %get-tuple-element.23.lengths, bf16[16,192,512]{2,1,0:T(8,128)(2,1)} %bitcast.12, bf16[16,144,256]{2,1,0:T(8,128)(2,1)S(1)} %get-tuple-element.25.recvg), custom_call_target="tpu_custom_call" | custom-call | tf_op jit(solution)/shard_map/cond/branch_0_fun/attention/pallas_call | solution.py:307
  120.4 0.0 copy-start.3
  120.4 60.1 %exchange.4 = (bf16[128,24,512]{2,1,0:T(8,128)(2,1)}, bf16[16,128,256]{2,1,0:T(8,128)(2,1)}) custom-call(bf16[128,24,512]{2,1,0:T(8,128)(2,1)} %bitcast.15, bf16[16,128,256]{2,1,0:T(8,128)(2,1)} %get-tuple-element.27.srcg), custom_call_target="tpu_custom_call" | custom-call | tf_op jit(solution)/shard_map/cond/branch_0_fun/exchange/pallas_call | solution.py:175
  180.4 0.0 copy-done.3
  180.5 6.8 %messages_to_rows.2 = (bf16[128,4096]{1,0:T(8,128)(2,1)}, bf16[128,4096]{1,0:T(8,128)(2,1)}, bf16[128,1024]{1,0:T(8,128)(2,1)}, bf16[128,1024]{1,0:T(8,128)(2,1)}) custom-call(bf16[192,128]{1,0:T(8,128)(2,1)S(1)} %copy-done.3, bf16[8,16,24,512]{3,2,1,0:T(8,128)(2,1)} %bitcast.13, bf16[16,128,256]{2,1,0:T(8,128)(2,1)} %get-tuple-element.29.att), custom_call_target="tpu_custom_call" | custom-call | tf_op jit(solution)/shard_map/cond/branch_0_fun/messages_to_rows/pallas_call | solution.py:344
Async XLA Ops:
  2.9 76.3 %copy-start = (bf16[128,4096]{1,0:T(8,128)(2,1)S(1)}, bf16[128,4096]{1,0:T(8,128)(2,1)}, u32[]{:S(2)}) copy-start(bf16[128,4096]{1,0:T(8,128)(2,1)} %q.1) | copy-start | bytes 3145732
  2.9 76.3 %copy-start.1 = (bf16[128,4096]{1,0:T(8,128)(2,1)S(1)}, bf16[128,4096]{1,0:T(8,128)(2,1)}, u32[]{:S(2)}) copy-start(bf16[128,4096]{1,0:T(8,128)(2,1)} %g.1) | copy-start | bytes 3145732
  2.9 76.3 %copy-start.2 = (bf16[128,1024]{1,0:T(8,128)(2,1)S(1)}, bf16[128,1024]{1,0:T(8,128)(2,1)}, u32[]{:S(2)}) copy-start(bf16[128,1024]{1,0:T(8,128)(2,1)} %k.1) | copy-start | bytes 786436
  2.9 76.3 %copy-start.4 = (s32[1,128,2]{1,2,0:T(2,128)S(1)}, s32[1,128,2]{1,2,0:T(2,128)}, u32[]{:S(2)}) copy-start(s32[1,128,2]{1,2,0:T(2,128)} %param.13) | copy-start | bytes 3076
  2.9 76.3 %copy-start.5 = (s32[1,16]{1,0:T(1,128)S(1)}, s32[1,16]{1,0:T(1,128)}, u32[]{:S(2)}) copy-start(s32[1,16]{1,0:T(1,128)} %param.15) | copy-start | bytes 196
  2.9 76.3 %copy-start.6 = (s32[1,128]{1,0:T(1,128)S(1)}, s32[1,128]{1,0:T(1,128)}, u32[]{:S(2)}) copy-start(s32[1,128]{1,0:T(1,128)} %unp.1) | copy-start | bytes 1540
  120.4 60.1 %copy-start.3 = (bf16[192,128]{1,0:T(8,128)(2,1)S(1)}, bf16[192,128]{1,0:T(8,128)(2,1)}, u32[]{:S(2)}) copy-start(bf16[192,128]{1,0:T(8,128)(2,1)} %get-tuple-element.22.sel) | copy-start | bytes 147460 | tf_op jit(solution)/shard_map/cond

commit v3 on v2

v3 whole, which is shorter than its diff:
```python
import functools
import math

import jax
import jax.numpy as jnp
from jax import lax
from jax.experimental import pallas as pl
from jax.experimental.pallas import tpu as pltpu
from jax.sharding import PartitionSpec as P

H = 32
KVH = 8
DH = 128
TOK = 128
CTX = 16
DP = 8
DEV = 128
SEQ = 2048
MOST = 1024
COLS = 384
FULL = 32
SHORT = 24
GROWS = 144
BQ = 128
BK = 256
WMAX = MOST // BK + 1
VMEM_LIMIT = 56 * 2**20

F32 = jnp.float32
BF16 = jnp.bfloat16
MESH = pl.DeviceIdType.MESH


def dot(a, b, ca, cb):
    return lax.dot_general(a, b, (((ca,), (cb,)), ((), ())), preferred_element_type=F32)


def iota(shape, dim):
    return lax.broadcasted_iota(jnp.int32, shape, dim)


def pack_kernel(K, prow, pcol, unp, lengths, q, k, v, g, send, sendg, sel, sel_s, over_s):
    @pl.when(pl.program_id(0) == 0)
    def _():
        occupied = (prow[...] >= 0).astype(BF16)
        a, b = iota((256, 256), 0), iota((256, 256), 1)
        earlier = ((a < b) & (a // 32 == b // 32)).astype(BF16)
        rank = dot(jnp.broadcast_to(occupied, (16, 256)), earlier, 1, 0)[0:1]
        rank = rank.astype(jnp.int32)
        slot = iota((1, 256), 1) // 32 * K + rank
        slot = jnp.where((prow[...] >= 0) & ((rank < K - 1) | (K == FULL)), slot, -1)
        over = jnp.max(jnp.where((prow[...] >= 0) & (rank >= K - 1), 1.0, 0.0), axis=1, keepdims=True)
        last = (iota((8 * K, TOK), 0) % K == K - 1) & (K < FULL)
        over_s[...] = jnp.where(last, over, 0.0)
        place = (iota((8 * K, 256), 0) == slot).astype(BF16)
        holds = (pcol[...] == iota((256, TOK), 1)).astype(BF16)
        value = dot(place, holds, 1, 0).astype(BF16)
        sel_s[...] = value
        sel[...] = value

    s = sel_s[...]
    yq = dot(s, q[...], 1, 0)
    yk = dot(s, k[...], 1, 0)
    yv = dot(s, v[...], 1, 0)
    ykv = (yk + over_s[...], yv + over_s[...])
    for z in range(4):
        for core in range(2):
            for e in range(2):
                rows = slice((2 * z + e) * K, (2 * z + e + 1) * K)
                send[z, core, e, 0, :, 0:256] = yq[rows, core * 256 : (core + 1) * 256].astype(BF16)
                send[z, core, e, 0, :, 256:384] = ykv[core][rows].astype(BF16)
    r = iota((16, TOK), 0)
    spread = (iota((16, TOK), 0) == iota((16, TOK), 1)).astype(BF16)
    sizes = jnp.broadcast_to(lengths[...], (16, 16))
    high = dot((sizes // 8).astype(F32).astype(BF16), spread, 1, 0)
    low = dot((sizes % 8).astype(F32).astype(BF16), spread, 1, 0)
    ints = jnp.where(r < 8, unp[...].astype(F32), jnp.where(r < 12, high, low)).astype(BF16)
    for core in range(2):
        sendg[core, 0, 0:TOK, :] = g[:, core * 256 : (core + 1) * 256]
        sendg[core, 0, TOK:GROWS, 0:TOK] = ints
        sendg[core, 0, TOK:GROWS, TOK:256] = jnp.zeros((16, 128), BF16)


def pack(K, prow, pcol, unp, lengths, q, k, v, g):
    whole = lambda shape: pl.BlockSpec(shape, lambda i: (0,) * len(shape))
    return pl.pallas_call(
        functools.partial(pack_kernel, K),
        grid=(KVH,),
        in_specs=[
            whole((1, 256)),
            whole((256, 1)),
            whole((1, TOK)),
            whole((1, 16)),
            pl.BlockSpec((TOK, 512), lambda i: (0, i)),
            pl.BlockSpec((TOK, 128), lambda i: (0, i)),
            pl.BlockSpec((TOK, 128), lambda i: (0, i)),
            pl.BlockSpec((TOK, 512), lambda i: (0, i)),
        ],
        out_specs=[
            pl.BlockSpec((4, 2, 2, 1, K, COLS), lambda i: (0, 0, 0, i, 0, 0)),
            pl.BlockSpec((2, 1, GROWS, 256), lambda i: (0, i, 0, 0)),
            whole((8 * K, TOK)),
        ],
        out_shape=[
            jax.ShapeDtypeStruct((4, 2, 2, KVH, K, COLS), BF16),
            jax.ShapeDtypeStruct((2, KVH, GROWS, 256), BF16),
            jax.ShapeDtypeStruct((8 * K, TOK), BF16),
        ],
        scratch_shapes=[pltpu.VMEM((8 * K, TOK), BF16), pltpu.VMEM((8 * K, TOK), F32)],
        compiler_params=pltpu.CompilerParams(vmem_limit_bytes=VMEM_LIMIT),
        name="pack_rows_to_messages",
    )(prow, pcol, unp, lengths, q, k, v, g)


def remote(src, dst, send_sem, recv_sem, target):
    return pltpu.make_async_remote_copy(
        src_ref=src,
        dst_ref=dst,
        send_sem=send_sem,
        recv_sem=recv_sem,
        device_id=target,
        device_id_type=MESH,
    )


def place():
    d = lax.axis_index("dp")
    c = lax.axis_index("ctx")
    return d, c, lax.div(d, 2), lax.rem(d, 2)


def partner(n):
    d, c, z, core = place()
    x, y = lax.div(c, 4), lax.rem(c, 4)
    j = lax.rem(n * 37, DEV)
    dy = lax.rem(j, 2) + 2 * lax.rem(lax.div(j, 16), 2)
    dx = lax.rem(lax.div(j, 2), 2) + 2 * lax.rem(lax.div(j, 32), 2)
    dz = lax.rem(lax.div(j, 4), 2) + 2 * lax.div(j, 64)
    dcore = lax.rem(lax.div(j, 8), 2)
    return lax.rem(z + dz, 4) * 2 + lax.rem(core + dcore, 2), lax.rem(x + dx, 4) * 4 + lax.rem(y + dy, 4)


def to_all(src, dst, send_sem, recv_sem, beside=None):
    d, c, _, _ = place()
    me = d * CTX + c

    def one(n):
        td, tc = partner(n)
        remote(src.at[td * CTX + tc], dst.at[me], send_sem, recv_sem, (td, tc)).start()

    def some(n, carry):
        if beside is not None:
            beside(n)
        for i in range(8):
            one(8 * n - 7 + i)
        return carry

    lax.fori_loop(1, CTX, some, 0)
    for n in range(121, DEV):
        one(n)


def wait_all(src, dst, send_sem, recv_sem, count):
    d, c, _, _ = place()
    remote(src.at[pl.ds(0, count)], dst.at[pl.ds(0, count)], send_sem, recv_sem, (d, c)).wait()


def exchange_in_kernel(
    src, srcg, dst, other, dstg,
    send_sem, recv_sem, sendg_sem, recvg_sem, sendo_sem, recvo_sem, own_sem, owng_sem,
):
    d, c, z, core = place()
    me = d * CTX + c
    mine = core == lax.div(c, 8)
    first = core * 8 + lax.rem(c, 8)

    def grads(j):
        target = (2 * z + lax.div(j, 8), core * 8 + lax.rem(j, 8))
        remote(srcg.at[j], dstg.at[c], sendg_sem, recvg_sem, target).start()

    own = pltpu.make_async_copy(src.at[me], dst.at[me], own_sem)
    own.start()
    owng = pltpu.make_async_copy(srcg.at[first], dstg.at[c], owng_sem)

    @pl.when(mine)
    def _():
        owng.start()

    @pl.when(jnp.logical_not(mine))
    def _():
        grads(first)

    to_all(src, dst, send_sem, recv_sem, lambda n: grads(lax.rem(first + lax.rem(n * 5, CTX), CTX)))
    own.wait()
    wait_all(src, dst, send_sem, recv_sem, DEV - 1)
    swap = remote(dst.at[:, :, pl.ds(256, 128)], other, sendo_sem, recvo_sem, (2 * z + 1 - core, c))
    swap.start()

    @pl.when(mine)
    def _():
        owng.wait()
        wait_all(srcg, dstg, sendg_sem, recvg_sem, CTX - 1)

    @pl.when(jnp.logical_not(mine))
    def _():
        wait_all(srcg, dstg, sendg_sem, recvg_sem, CTX)

    swap.wait()


def exchange_in(src, srcg):
    anywhere = pl.BlockSpec(memory_space=pl.ANY)
    return pl.pallas_call(
        exchange_in_kernel,
        in_specs=[anywhere] * 2,
        out_specs=[anywhere] * 3,
        out_shape=[
            jax.ShapeDtypeStruct(src.shape, BF16),
            jax.ShapeDtypeStruct(src.shape[:2] + (128,), BF16),
            jax.ShapeDtypeStruct(srcg.shape, BF16),
        ],
        scratch_shapes=[pltpu.SemaphoreType.DMA] * 8,
        compiler_params=pltpu.CompilerParams(has_side_effects=True),
        name="exchange_in",
    )(src, srcg)


def exchange_out_kernel(
    src, keep, give, srcg, dst, dstkv, dstg,
    other, total,
    send_sem, recv_sem, sendk_sem, recvk_sem, sendg_sem, recvg_sem, sendo_sem, recvo_sem,
    own_sem, ownk_sem, owng_sem,
):
    d, c, z, core = place()
    me = d * CTX + c
    e = lax.div(c, 8)
    mine = core == e
    slot = core * 8 + lax.rem(c, 8)

    def grads(j):
        remote(srcg.at[j], dstg.at[slot], sendg_sem, recvg_sem, (2 * z + e, j)).start()

    swap = remote(give, other, sendo_sem, recvo_sem, (2 * z + 1 - core, c))
    swap.start()
    own = pltpu.make_async_copy(src.at[me], dst.at[me], own_sem)
    own.start()
    owng = pltpu.make_async_copy(srcg.at[c], dstg.at[slot], owng_sem)

    @pl.when(mine)
    def _():
        owng.start()

    @pl.when(jnp.logical_not(mine))
    def _():
        grads(c)

    to_all(src, dst, send_sem, recv_sem, lambda n: grads(lax.rem(c + lax.rem(n * 5, CTX), CTX)))
    swap.wait()
    total[...] = (keep[...].astype(F32) + other[...].astype(F32)).astype(BF16)
    ownk = pltpu.make_async_copy(total.at[me], dstkv.at[me], ownk_sem)
    ownk.start()
    to_all(total, dstkv, sendk_sem, recvk_sem)
    own.wait()
    ownk.wait()

    @pl.when(mine)
    def _():
        owng.wait()
        wait_all(srcg, dstg, sendg_sem, recvg_sem, CTX - 1)

    @pl.when(jnp.logical_not(mine))
    def _():
        wait_all(srcg, dstg, sendg_sem, recvg_sem, CTX)

    wait_all(src, dst, send_sem, recv_sem, DEV - 1)
    wait_all(total, dstkv, sendk_sem, recvk_sem, DEV - 1)


def exchange_out(src, keep, give, srcg):
    anywhere = pl.BlockSpec(memory_space=pl.ANY)
    return pl.pallas_call(
        exchange_out_kernel,
        in_specs=[anywhere, pl.BlockSpec(memory_space=pltpu.VMEM), anywhere, anywhere],
        out_specs=[anywhere] * 3,
        out_shape=[
            jax.ShapeDtypeStruct(src.shape, BF16),
            jax.ShapeDtypeStruct(keep.shape, BF16),
            jax.ShapeDtypeStruct(srcg.shape, BF16),
        ],
        scratch_shapes=[pltpu.VMEM(keep.shape, BF16)] * 2 + [pltpu.SemaphoreType.DMA] * 11,
        compiler_params=pltpu.CompilerParams(has_side_effects=True, vmem_limit_bytes=VMEM_LIMIT),
        name="exchange_out",
    )(src, keep, give, srcg)


def attention_kernel(
    K, recv, other, recvg, att, back, keep, give, x, xo, mid, ts, dk, dv, col, lengths
):
    scale = 1.0 / math.sqrt(DH)
    first_core = lax.rem(lax.axis_index("dp"), 2) == 0
    sizes = recvg[0, TOK:GROWS, 0:TOK].astype(F32)
    sizes = (sizes[8:9] * 8 + sizes[12:13]).astype(jnp.int32)
    for n in range(16):
        lengths[n] = jnp.sum(jnp.where(iota((1, TOK), 1) == n, sizes, 0))

    def slots_of(c):
        row = recvg[c, TOK : TOK + 8, 0:TOK].astype(F32)[0:1]
        return (iota((256, TOK), 0).astype(F32) == row).astype(BF16)

    occ = jnp.zeros((256, 128), F32)
    for c in range(CTX):
        occ = occ + dot(slots_of(c), (iota((TOK, 128), 1) == c).astype(BF16), 1, 0)
    pair = (iota((256, 256), 0) // 2 == iota((256, 256), 1) // 2).astype(BF16)
    count = dot(pair, occ.astype(BF16), 1, 0)
    before = (iota((128, 128), 0) < iota((128, 128), 1)).astype(BF16)
    base = dot(count.astype(BF16), before, 1, 0)
    u = iota((256, 128), 0)
    col[...] = base + (u % 2 + (u // 2) % 8 * K).astype(F32)

    lanes = iota((16, 8 * K), 1).astype(F32)

    def sort_senders(grp, carry):
        r0 = pl.multiple_of(grp * 16, 16)
        tab = col[pl.ds(r0, 16), :]
        t = jnp.concatenate(
            [(lanes == tab[:, c : c + 1]).astype(F32) for c in range(CTX)], axis=0
        ).astype(BF16)
        ts[grp] = t
        rows = dot(t, recv[grp], 1, 0).astype(BF16)
        rows2 = dot(t, other[grp], 1, 0).astype(BF16)
        for c in range(CTX):
            mid[c, pl.ds(r0, 16), 0:384] = rows[c * 16 : (c + 1) * 16]
            mid[c, pl.ds(r0, 16), 384:512] = rows2[c * 16 : (c + 1) * 16]
        return carry

    lax.fori_loop(0, 16, sort_senders, 0)

    def sort_rows(c, carry):
        y = dot(slots_of(c), mid[c], 0, 0)
        r = pl.ds(pl.multiple_of(c * TOK, TOK), TOK)
        x[r, 0:256] = y[:, 0:256].astype(BF16)
        x[r, 256:384] = jnp.where(first_core, y[:, 256:384], y[:, 384:512]).astype(BF16)
        x[r, 384:512] = jnp.where(first_core, y[:, 384:512], y[:, 256:384]).astype(BF16)
        return carry

    lax.fori_loop(0, CTX, sort_rows, 0)

    dk[...] = jnp.zeros_like(dk)
    dv[...] = jnp.zeros_like(dv)

    def doc_start(position):
        def step(n, carry):
            start, end = carry
            return (jnp.where(end <= position, end, start), end + lengths[n])

        return lax.fori_loop(0, 16, step, (jnp.int32(0), jnp.int32(0)))[0]

    def starts_of(positions):
        def step(n, carry):
            start, end = carry
            return (jnp.where(end <= positions, end, start), end + lengths[n])

        return lax.fori_loop(0, 16, step, (jnp.zeros_like(positions), jnp.int32(0)))[0]

    def tile(i, carry):
        q0 = pl.multiple_of(i * BQ, BQ)
        lo = doc_start(q0) // BK
        width = q0 // BK - lo + 1

        def attend(w):
            k0 = pl.multiple_of(lo * BK, BK)
            span = w * BK
            keys = x[pl.ds(k0, span), 256:384]
            values = x[pl.ds(k0, span), 384:512]
            queries = jnp.concatenate([x[pl.ds(q0, BQ), 0:128], x[pl.ds(q0, BQ), 128:256]], axis=0)
            grads = jnp.concatenate([recvg[i, 0:TOK, 0:128], recvg[i, 0:TOK, 128:256]], axis=0)
            qpos = q0 + iota((BQ, 1), 0)
            qstart = starts_of(qpos)
            qpos = jnp.concatenate([qpos, qpos], axis=0)
            qstart = jnp.concatenate([qstart, qstart], axis=0)
            kpos = k0 + iota((2 * BQ, span), 1)
            s = dot(queries, keys, 1, 1) * scale
            s = jnp.where((kpos >= qstart) & (kpos <= qpos), s, -1e30)
            top = jnp.max(s, axis=1, keepdims=True)
            e = jnp.exp(s - top)
            p = e * (1.0 / jnp.sum(e, axis=1, keepdims=True))
            low = p.astype(BF16)
            out = dot(low, values, 1, 0).astype(BF16)
            att[i, :, 0:128] = out[0:BQ]
            att[i, :, 128:256] = out[BQ:]
            delta = jnp.sum(grads.astype(F32) * out.astype(F32), axis=1, keepdims=True)
            dp = dot(grads, values, 1, 1)
            ds = (p * (dp - delta) * scale).astype(BF16)
            dq = dot(ds, keys, 1, 0).astype(BF16)
            xo[pl.ds(q0, BQ), 0:128] = dq[0:BQ]
            xo[pl.ds(q0, BQ), 128:256] = dq[BQ:]
            dk[pl.ds(k0, span), :] += dot(ds, queries, 0, 0)
            dv[pl.ds(k0, span), :] += dot(low, grads, 0, 0)

        for w in range(1, WMAX + 1):
            pl.when(width == w)(functools.partial(attend, w))
        return carry

    lax.fori_loop(0, SEQ // BQ, tile, 0)
    xo[:, 256:384] = jnp.where(first_core, dk[...], dv[...]).astype(BF16)
    xo[:, 384:512] = jnp.where(first_core, dv[...], dk[...]).astype(BF16)

    def unsort_rows(c, carry):
        mid[c] = dot(
            slots_of(c), xo[pl.ds(pl.multiple_of(c * TOK, TOK), TOK), :], 1, 0
        ).astype(BF16)
        return carry

    lax.fori_loop(0, CTX, unsort_rows, 0)

    def unsort_senders(grp, carry):
        r0 = pl.multiple_of(grp * 16, 16)
        rows = jnp.concatenate([mid[c, pl.ds(r0, 16), :] for c in range(CTX)], axis=0)
        out = dot(ts[grp], rows, 0, 0).astype(BF16)
        back[grp] = out[:, 0:256]
        keep[grp] = out[:, 256:384]
        give[grp] = out[:, 384:512]
        return carry

    lax.fori_loop(0, 16, unsort_senders, 0)


def attention(K, recv, other, recvg):
    vmem = pl.BlockSpec(memory_space=pltpu.VMEM)
    return pl.pallas_call(
        functools.partial(attention_kernel, K),
        in_specs=[vmem] * 3,
        out_specs=[vmem] * 4,
        out_shape=[
            jax.ShapeDtypeStruct((CTX, TOK, 256), BF16),
            jax.ShapeDtypeStruct((16, 8 * K, 256), BF16),
            jax.ShapeDtypeStruct((16, 8 * K, 128), BF16),
            jax.ShapeDtypeStruct((16, 8 * K, 128), BF16),
        ],
        scratch_shapes=[
            pltpu.VMEM((SEQ, 512), BF16),
            pltpu.VMEM((SEQ, 512), BF16),
            pltpu.VMEM((CTX, 256, 512), BF16),
            pltpu.VMEM((16, 256, 8 * K), BF16),
            pltpu.VMEM((SEQ, DH), F32),
            pltpu.VMEM((SEQ, DH), F32),
            pltpu.VMEM((256, 128), F32),
            pltpu.SMEM((16,), jnp.int32),
        ],
        compiler_params=pltpu.CompilerParams(vmem_limit_bytes=VMEM_LIMIT),
        name="attention",
    )(recv, other, recvg)


def unpack_kernel(K, sel, back, backkv, att, attended, gq, gk, gv):
    s = sel[...]
    by_sequence = [(z, e) for z in range(4) for e in range(2)]
    for core, out in ((0, gk), (1, gv)):
        cols = slice(core * 256, (core + 1) * 256)
        attended[:, cols] = att[core, 0]
        rows = [back[z, core, e, 0].astype(F32) for z, e in by_sequence]
        gq[:, cols] = dot(s, jnp.concatenate(rows, axis=0).astype(BF16), 0, 0).astype(BF16)
        rows = [backkv[z, core, e, 0].astype(F32) for z, e in by_sequence]
        out[...] = dot(s, jnp.concatenate(rows, axis=0).astype(BF16), 0, 0).astype(BF16)


def unpack_rows(K, sel, back, backkv, att):
    return pl.pallas_call(
        functools.partial(unpack_kernel, K),
        grid=(KVH,),
        in_specs=[
            pl.BlockSpec((8 * K, TOK), lambda i: (0, 0)),
            pl.BlockSpec((4, 2, 2, 1, K, 256), lambda i: (0, 0, 0, i, 0, 0)),
            pl.BlockSpec((4, 2, 2, 1, K, 128), lambda i: (0, 0, 0, i, 0, 0)),
            pl.BlockSpec((2, 1, TOK, 256), lambda i: (0, i, 0, 0)),
        ],
        out_specs=[
            pl.BlockSpec((TOK, 512), lambda i: (0, i)),
            pl.BlockSpec((TOK, 512), lambda i: (0, i)),
            pl.BlockSpec((TOK, 128), lambda i: (0, i)),
            pl.BlockSpec((TOK, 128), lambda i: (0, i)),
        ],
        out_shape=[
            jax.ShapeDtypeStruct((TOK, H * DH), BF16),
            jax.ShapeDtypeStruct((TOK, H * DH), BF16),
            jax.ShapeDtypeStruct((TOK, KVH * DH), BF16),
            jax.ShapeDtypeStruct((TOK, KVH * DH), BF16),
        ],
        compiler_params=pltpu.CompilerParams(vmem_limit_bytes=VMEM_LIMIT),
        name="messages_to_rows",
    )(sel, back, backkv, att)


def forward(K, q_load, k_load, v_load, grad_out, pack_rows, unpack, doc_lengths):
    flat = pack_rows.reshape(1, 2 * DEV)
    send, sendg, sel = pack(
        K, flat, flat.reshape(2 * DEV, 1), unpack, doc_lengths, q_load, k_load, v_load, grad_out
    )
    return sel, *exchange_in(send.reshape(DEV, K, COLS), sendg.reshape(CTX, GROWS, 256))


def finish(K, sel, recv, other, recvg):
    recv, other = (a.reshape(16, 8 * K, -1) for a in (recv, other))
    att, *parts = attention(K, recv, other, recvg)
    back, keep, give = (a.reshape(DEV, K, -1) for a in parts)
    returned, returnedkv, turned = exchange_out(back, keep, give, att)
    returned, returnedkv = (a.reshape(4, 2, 2, KVH, K, -1) for a in (returned, returnedkv))
    return unpack_rows(K, sel, returned, returnedkv, turned.reshape(2, KVH, TOK, 256))


def local(*operands):
    sel, recv, other, recvg = forward(SHORT, *operands)
    over = jnp.max(recv[:, SHORT - 1, COLS - 1].astype(F32)) > 0.5
    return lax.cond(
        over,
        lambda: finish(FULL, *forward(FULL, *operands)),
        lambda: finish(SHORT, sel, recv, other, recvg),
    )


def solution(mesh):
    rows = P(("dp", "ctx"), None)
    return jax.shard_map(
        local,
        mesh=mesh,
        in_specs=(rows, rows, rows, rows, P(("dp", "ctx"), None, None), rows, P("dp", None)),
        out_specs=(rows, rows, rows, rows),
        check_vma=False,
    )
```

time: 188 us -> 174 us (0.926)
  Pallas kernels: 182 us -> 168 us
    pallas_call x4, Pallas kernels: 174 us -> 161 us  [the longest x1 59.6 us: exchange_in(): pl.pallas_call(exchange_in_kernel, in_specs=[anywhere] * 2, out_specs=[an...]
where the time goes in v3:
time: 174 us
  Pallas kernels  168 us (97%)
  local copies, waits for them, and re-layouts  2.27 us (1%)
  other arithmetic  1.76 us (1%)
    pallas_call x1, Pallas kernels, exchange_in(): pl.pallas_call(exchange_in_kernel, in_specs=[anywhere] * 2, out_specs=[an...  59.6 us
    pallas_call x1, Pallas kernels, exchange_out(): pl.pallas_call(exchange_out_kernel, in_specs=[anywhere, pl.BlockSpec(memo...  51.4 us
    pallas_call x1, Pallas kernels, attention(): pl.pallas_call(functools.partial(attention_kernel, K), in_specs=[vmem] *...  42.7 us
    pallas_call x1, Pallas kernels, pack(): pl.pallas_call(functools.partial(pack_kernel, K), grid=(KVH,), in_specs=[...  7.51 us
    pallas_call x1, Pallas kernels, unpack_rows(): pl.pallas_call(functools.partial(unpack_kernel, K), grid=(KVH,), in_specs...  6.92 us

profile of v3, /device:TPU:1, one launch (start us, length us, event | category | flops | bytes accessed | tf_op | source)
XLA Modules:
  0.0 173.8 jit_solution(14951687847330153297)
XLA Ops:
  0.6 0.8 copy.23
  1.4 0.7 reshape.77.prow
  2.1 0.7 reshape_reshape.4.pcol
  2.9 7.5 %pack_rows_to_messages.3 = (bf16[4,2,2,8,24,384]{5,4,3,2,1,0:T(8,128)(2,1)}, bf16[2,8,144,256]{3,2,1,0:T(8,128)(2,1)}, bf16[192,128]{1,0:T(8,128)(2,1)}) custom-call(s32[1,256]{1,0:T(1,128)} %reshape.77.prow, s32[256,1]{1,0:T(8,128)} %reshape_reshape.4.pcol, s32[1,128]{1,0:T(1,128)} %unp.1, s32[1,16]{1,0:T(1,128)} %lengths.1, bf16[128,4096]{1,0:T(8,128)(2,1)} %q.1, ...), custom_call_target="tpu_custom_call" | custom-call | tf_op jit(solution)/shard_map/pack_rows_to_messages/pallas_call | solution.py:86
  10.4 0.0 copy-start
  10.4 0.0 copy-start.1
  10.4 0.0 copy-start.2
  10.4 0.0 copy-start.4
  10.4 0.0 copy-start.5
  10.4 0.0 copy-start.6
  10.4 59.6 %exchange_in.3 = (bf16[128,24,384]{2,1,0:T(8,128)(2,1)}, bf16[128,24,128]{2,1,0:T(8,128)(2,1)}, bf16[16,144,256]{2,1,0:T(8,128)(2,1)S(1)}) custom-call(bf16[128,24,384]{2,1,0:T(8,128)(2,1)} %bitcast.23, bf16[16,144,256]{2,1,0:T(8,128)(2,1)} %bitcast.28), custom_call_target="tpu_custom_call" | custom-call | tf_op jit(solution)/shard_map/exchange_in/pallas_call | solution.py:213
  70.0 1.8 %slice_reduce_fusion = bf16[]{:T(256)} fusion(bf16[128,24,384]{2,1,0:T(8,128)(2,1)} %get-tuple-element.65), kind=kLoop, calls=%fused_computation | loop fusion | flops 127 | bytes 258 | tf_op jit(solution)/shard_map/reduce_max | solution.py:513
  72.5 0.0 copy-done
  72.5 0.0 copy-done.1
  72.5 0.0 copy-done.2
  72.5 0.0 copy-done.4
  72.5 0.0 copy-done.5
  72.5 0.0 copy-done.6
  72.5 101.1 %conditional.1 = ((bf16[128,4096]{1,0:T(8,128)(2,1)}, bf16[128,4096]{1,0:T(8,128)(2,1)}, bf16[128,1024]{1,0:T(8,128)(2,1)}, bf16[128,1024]{1,0:T(8,128)(2,1)})) conditional(s32[]{:T(128)} %convert_element_type.4, (bf16[128,24,384]{2,1,0:T(8,128)(2,1)}, bf16[128,24,128]{2,1,0:T(8,128)(2,1)}, bf16[16,144,256]{2,1,0:T(8,128)(2,1)S(1)}, ...), branch_computations={%region_1.0_spmd, %region_2.0_spmd} | conditional | bytes 196644 | solution.py:514
  72.5 42.7 %attention.2 = (bf16[16,128,256]{2,1,0:T(8,128)(2,1)}, bf16[16,192,256]{2,1,0:T(8,128)(2,1)}, bf16[16,192,128]{2,1,0:T(8,128)(2,1)}, bf16[16,192,128]{2,1,0:T(8,128)(2,1)}) custom-call(bf16[16,192,384]{2,1,0:T(8,128)(2,1)} %bitcast.22, bf16[16,192,128]{2,1,0:T(8,128)(2,1)} %bitcast.39, bf16[16,144,256]{2,1,0:T(8,128)(2,1)S(1)} %get-tuple-element.25.recvg), custom_call_target="tpu_custom_call" | custom-call | tf_op jit(solution)/shard_map/cond/branch_0_fun/attention/pallas_call | solution.py:430
  115.3 0.0 copy-start.3
  115.3 51.4 %exchange_out.2 = (bf16[128,24,256]{2,1,0:T(8,128)(2,1)}, bf16[128,24,128]{2,1,0:T(8,128)(2,1)}, bf16[16,128,256]{2,1,0:T(8,128)(2,1)}) custom-call(bf16[128,24,256]{2,1,0:T(8,128)(2,1)} %bitcast.27, bf16[128,24,128]{2,1,0:T(8,128)(2,1)} %bitcast.36, bf16[128,24,128]{2,1,0:T(8,128)(2,1)} %bitcast.37, bf16[16,128,256]{2,1,0:T(8,128)(2,1)} %get-tuple-element.29.srcg), custom_call_target="tpu_custom_call" | custom-call | tf_op jit(solution)/shard_map/cond/branch_0_fun/exchange_out/pallas_call | solution.py:281
  166.7 0.0 copy-done.3
  166.7 6.9 %messages_to_rows.2 = (bf16[128,4096]{1,0:T(8,128)(2,1)}, bf16[128,4096]{1,0:T(8,128)(2,1)}, bf16[128,1024]{1,0:T(8,128)(2,1)}, bf16[128,1024]{1,0:T(8,128)(2,1)}) custom-call(bf16[192,128]{1,0:T(8,128)(2,1)S(1)} %copy-done.3, bf16[4,2,2,8,24,256]{5,4,3,2,1,0:T(8,128)(2,1)} %bitcast.26, bf16[4,2,2,8,24,128]{5,4,3,2,1,0:T(8,128)(2,1)} %bitcast.38, ...), custom_call_target="tpu_custom_call" | custom-call | tf_op jit(solution)/shard_map/cond/branch_0_fun/messages_to_rows/pallas_call | solution.py:468
Async XLA Ops:
  10.4 62.1 %copy-start = (bf16[128,4096]{1,0:T(8,128)(2,1)S(1)}, bf16[128,4096]{1,0:T(8,128)(2,1)}, u32[]{:S(2)}) copy-start(bf16[128,4096]{1,0:T(8,128)(2,1)} %q.1) | copy-start | bytes 3145732
  10.4 62.1 %copy-start.1 = (bf16[128,4096]{1,0:T(8,128)(2,1)S(1)}, bf16[128,4096]{1,0:T(8,128)(2,1)}, u32[]{:S(2)}) copy-start(bf16[128,4096]{1,0:T(8,128)(2,1)} %g.1) | copy-start | bytes 3145732
  10.4 62.1 %copy-start.2 = (bf16[128,1024]{1,0:T(8,128)(2,1)S(1)}, bf16[128,1024]{1,0:T(8,128)(2,1)}, u32[]{:S(2)}) copy-start(bf16[128,1024]{1,0:T(8,128)(2,1)} %k.1) | copy-start | bytes 786436
  10.4 62.1 %copy-start.4 = (s32[1,128,2]{1,2,0:T(2,128)S(1)}, s32[1,128,2]{1,2,0:T(2,128)}, u32[]{:S(2)}) copy-start(s32[1,128,2]{1,2,0:T(2,128)} %param.13) | copy-start | bytes 3076
  10.4 62.1 %copy-start.5 = (s32[1,128]{1,0:T(1,128)S(1)}, s32[1,128]{1,0:T(1,128)}, u32[]{:S(2)}) copy-start(s32[1,128]{1,0:T(1,128)} %unp.1) | copy-start | bytes 1540
  10.4 62.1 %copy-start.6 = (s32[1,16]{1,0:T(1,128)S(1)}, s32[1,16]{1,0:T(1,128)}, u32[]{:S(2)}) copy-start(s32[1,16]{1,0:T(1,128)} %lengths.1) | copy-start | bytes 196
  115.3 51.4 %copy-start.3 = (bf16[192,128]{1,0:T(8,128)(2,1)S(1)}, bf16[192,128]{1,0:T(8,128)(2,1)}, u32[]{:S(2)}) copy-start(bf16[192,128]{1,0:T(8,128)(2,1)} %get-tuple-element.22.sel) | copy-start | bytes 147460 | tf_op jit(solution)/shard_map/cond

commit v4 on v3

--- a/solution.py
+++ b/solution.py
@@ -21,7 +21,7 @@
 FULL = 32
 SHORT = 24
 GROWS = 144
-BQ = 128
+BQ = 256
 BK = 256
 WMAX = MOST // BK + 1
 VMEM_LIMIT = 56 * 2**20
@@ -294,7 +294,7 @@
 
 
 def attention_kernel(
-    K, recv, other, recvg, att, back, keep, give, x, xo, mid, ts, dk, dv, col, lengths
+    K, recv, other, recvg, att, back, keep, give, x, keyt, valuet, xo, mid, dk, dv, col, lengths
 ):
     scale = 1.0 / math.sqrt(DH)
     first_core = lax.rem(lax.axis_index("dp"), 2) == 0
@@ -317,15 +317,16 @@
     u = iota((256, 128), 0)
     col[...] = base + (u % 2 + (u // 2) % 8 * K).astype(F32)
 
-    lanes = iota((16, 8 * K), 1).astype(F32)
+    own_c = iota((256, 128), 0) // 16 == iota((256, 128), 1)
+
+    def compact_slot(grp):
+        tab = col[pl.ds(pl.multiple_of(grp * 16, 16), 16), :]
+        return jnp.where(own_c, jnp.concatenate([tab] * CTX, axis=0), 0.0).astype(BF16)
 
     def sort_senders(grp, carry):
         r0 = pl.multiple_of(grp * 16, 16)
-        tab = col[pl.ds(r0, 16), :]
-        t = jnp.concatenate(
-            [(lanes == tab[:, c : c + 1]).astype(F32) for c in range(CTX)], axis=0
-        ).astype(BF16)
-        ts[grp] = t
+        slot = dot(compact_slot(grp), jnp.ones((128, 8 * K), BF16), 1, 0)
+        t = (slot == iota((256, 8 * K), 1).astype(F32)).astype(BF16)
         rows = dot(t, recv[grp], 1, 0).astype(BF16)
         rows2 = dot(t, other[grp], 1, 0).astype(BF16)
         for c in range(CTX):
@@ -333,69 +334,103 @@
             mid[c, pl.ds(r0, 16), 384:512] = rows2[c * 16 : (c + 1) * 16]
         return carry
 
-    lax.fori_loop(0, 16, sort_senders, 0)
+    lax.fori_loop(0, 16, sort_senders, 0, unroll=4)
 
     def sort_rows(c, carry):
         y = dot(slots_of(c), mid[c], 0, 0)
         r = pl.ds(pl.multiple_of(c * TOK, TOK), TOK)
+        keys = jnp.where(first_core, y[:, 256:384], y[:, 384:512])
+        values = jnp.where(first_core, y[:, 384:512], y[:, 256:384])
         x[r, 0:256] = y[:, 0:256].astype(BF16)
-        x[r, 256:384] = jnp.where(first_core, y[:, 256:384], y[:, 384:512]).astype(BF16)
-        x[r, 384:512] = jnp.where(first_core, y[:, 384:512], y[:, 256:384]).astype(BF16)
+        x[r, 256:384] = keys.astype(BF16)
+        x[r, 384:512] = values.astype(BF16)
+        keyt[:, r] = keys.T.astype(BF16)
+        valuet[:, r] = values.T.astype(BF16)
         return carry
 
-    lax.fori_loop(0, CTX, sort_rows, 0)
+    lax.fori_loop(0, CTX, sort_rows, 0, unroll=4)
 
     dk[...] = jnp.zeros_like(dk)
     dv[...] = jnp.zeros_like(dv)
 
     def doc_start(position):
-        def step(n, carry):
-            start, end = carry
-            return (jnp.where(end <= position, end, start), end + lengths[n])
-
-        return lax.fori_loop(0, 16, step, (jnp.int32(0), jnp.int32(0)))[0]
-
-    def starts_of(positions):
-        def step(n, carry):
-            start, end = carry
-            return (jnp.where(end <= positions, end, start), end + lengths[n])
-
-        return lax.fori_loop(0, 16, step, (jnp.zeros_like(positions), jnp.int32(0)))[0]
+        start, end = jnp.zeros_like(position), jnp.int32(0)
+        for n in range(16):
+            start = jnp.where(end <= position, end, start)
+            end = end + lengths[n]
+        return start
 
     def tile(i, carry):
         q0 = pl.multiple_of(i * BQ, BQ)
         lo = doc_start(q0) // BK
-        width = q0 // BK - lo + 1
+        width = i - lo + 1
 
         def attend(w):
             k0 = pl.multiple_of(lo * BK, BK)
-            span = w * BK
-            keys = x[pl.ds(k0, span), 256:384]
-            values = x[pl.ds(k0, span), 384:512]
-            queries = jnp.concatenate([x[pl.ds(q0, BQ), 0:128], x[pl.ds(q0, BQ), 128:256]], axis=0)
-            grads = jnp.concatenate([recvg[i, 0:TOK, 0:128], recvg[i, 0:TOK, 128:256]], axis=0)
-            qpos = q0 + iota((BQ, 1), 0)
-            qstart = starts_of(qpos)
-            qpos = jnp.concatenate([qpos, qpos], axis=0)
-            qstart = jnp.concatenate([qstart, qstart], axis=0)
-            kpos = k0 + iota((2 * BQ, span), 1)
-            s = dot(queries, keys, 1, 1) * scale
-            s = jnp.where((kpos >= qstart) & (kpos <= qpos), s, -1e30)
-            top = jnp.max(s, axis=1, keepdims=True)
-            e = jnp.exp(s - top)
-            p = e * (1.0 / jnp.sum(e, axis=1, keepdims=True))
-            low = p.astype(BF16)
-            out = dot(low, values, 1, 0).astype(BF16)
-            att[i, :, 0:128] = out[0:BQ]
-            att[i, :, 128:256] = out[BQ:]
-            delta = jnp.sum(grads.astype(F32) * out.astype(F32), axis=1, keepdims=True)
-            dp = dot(grads, values, 1, 1)
-            ds = (p * (dp - delta) * scale).astype(BF16)
-            dq = dot(ds, keys, 1, 0).astype(BF16)
-            xo[pl.ds(q0, BQ), 0:128] = dq[0:BQ]
-            xo[pl.ds(q0, BQ), 128:256] = dq[BQ:]
-            dk[pl.ds(k0, span), :] += dot(ds, queries, 0, 0)
-            dv[pl.ds(k0, span), :] += dot(low, grads, 0, 0)
+            span = pl.ds(k0, w * BK)
+            here = pl.ds(q0, BQ)
+            chunks = [pl.ds(pl.multiple_of(k0 + t * BK, BK), BK) for t in range(w)]
+            qpos = q0 + iota((1, BQ), 1)
+            qstart = doc_start(qpos)
+
+            def scores(h):
+                queries = x[here, h * 128 : (h + 1) * 128]
+                out = []
+                for t in range(w):
+                    kpos = k0 + t * BK + iota((BK, BQ), 0)
+                    seen = kpos >= qstart
+                    if t == w - 1:
+                        seen = seen & (kpos <= qpos)
+                    out.append(jnp.where(seen, dot(x[chunks[t], 256:384], queries, 1, 1), -1e30))
+                return out
+
+            def grads_of(h):
+                return jnp.concatenate(
+                    [recvg[2 * i + n, 0:TOK, h * 128 : (h + 1) * 128] for n in range(2)], axis=0
+                )
+
+            def probs(s):
+                top = functools.reduce(jnp.maximum, [jnp.max(a, axis=0, keepdims=True) for a in s])
+                e = [jnp.exp2((a - top) * (scale * math.log2(math.e))) for a in s]
+                total = functools.reduce(jnp.add, [jnp.sum(a, axis=0, keepdims=True) for a in e])
+                inverse = 1.0 / total
+                return [a * inverse for a in e]
+
+            def attend_values(h, p, grads):
+                low = jnp.concatenate([a.astype(BF16) for a in p], axis=0)
+                outt = dot(valuet[:, span], low, 1, 0).astype(BF16)
+                out = outt.astype(F32).T.astype(BF16)
+                for n in range(2):
+                    att[2 * i + n, :, h * 128 : (h + 1) * 128] = out[n * TOK : (n + 1) * TOK]
+                delta = jnp.sum(grads.astype(F32).T * outt.astype(F32), axis=0, keepdims=True)
+                return low, delta
+
+            def dprobs(grads):
+                return [dot(x[r, 384:512], grads, 1, 1) for r in chunks]
+
+            def dscores(p, dp, delta):
+                return jnp.concatenate(
+                    [(a * (b - delta) * scale).astype(BF16) for a, b in zip(p, dp)], axis=0
+                )
+
+            def query_grads(h, ds):
+                xo[here, h * 128 : (h + 1) * 128] = dot(keyt[:, span], ds, 1, 0).T.astype(BF16)
+
+            ga, gb = grads_of(0), grads_of(1)
+            sa = scores(0)
+            sb = scores(1)
+            pa = probs(sa)
+            dpa = dprobs(ga)
+            pb = probs(sb)
+            lowa, deltaa = attend_values(0, pa, ga)
+            dpb = dprobs(gb)
+            dsa = dscores(pa, dpa, deltaa)
+            lowb, deltab = attend_values(1, pb, gb)
+            query_grads(0, dsa)
+            dsb = dscores(pb, dpb, deltab)
+            query_grads(1, dsb)
+            dv[span, :] += dot(lowa, ga, 1, 0) + dot(lowb, gb, 1, 0)
+            dk[span, :] += dot(dsa, x[here, 0:128], 1, 0) + dot(dsb, x[here, 128:256], 1, 0)
 
         for w in range(1, WMAX + 1):
             pl.when(width == w)(functools.partial(attend, w))
@@ -411,18 +446,20 @@
         ).astype(BF16)
         return carry
 
-    lax.fori_loop(0, CTX, unsort_rows, 0)
+    lax.fori_loop(0, CTX, unsort_rows, 0, unroll=4)
 
     def unsort_senders(grp, carry):
         r0 = pl.multiple_of(grp * 16, 16)
         rows = jnp.concatenate([mid[c, pl.ds(r0, 16), :] for c in range(CTX)], axis=0)
-        out = dot(ts[grp], rows, 0, 0).astype(BF16)
+        slot = dot(jnp.ones((8 * K, 128), BF16), compact_slot(grp), 1, 1)
+        t = (slot == iota((8 * K, 256), 0).astype(F32)).astype(BF16)
+        out = dot(t, rows, 1, 0).astype(BF16)
         back[grp] = out[:, 0:256]
         keep[grp] = out[:, 256:384]
         give[grp] = out[:, 384:512]
         return carry
 
-    lax.fori_loop(0, 16, unsort_senders, 0)
+    lax.fori_loop(0, 16, unsort_senders, 0, unroll=4)
 
 
 def attention(K, recv, other, recvg):
@@ -439,9 +476,10 @@
         ],
         scratch_shapes=[
             pltpu.VMEM((SEQ, 512), BF16),
+            pltpu.VMEM((DH, SEQ), BF16),
+            pltpu.VMEM((DH, SEQ), BF16),
             pltpu.VMEM((SEQ, 512), BF16),
             pltpu.VMEM((CTX, 256, 512), BF16),
-            pltpu.VMEM((16, 256, 8 * K), BF16),
             pltpu.VMEM((SEQ, DH), F32),
             pltpu.VMEM((SEQ, DH), F32),
             pltpu.VMEM((256, 128), F32),

time: 174 us -> 161 us (0.925)
  Pallas kernels: 168 us -> 155 us
    pallas_call x1, Pallas kernels: 42.7 us -> 28.3 us  [attention(): pl.pallas_call(functools.partial(attention_kernel, K), in_specs=[vmem] *...]
where the time goes in v4:
time: 161 us; the launch traced here: 160 us
  Pallas kernels  155 us (96%)
  local copies, waits for them, and re-layouts  2.27 us (1%)
  other arithmetic  1.76 us (1%)
    pallas_call x1, Pallas kernels, exchange_in(): pl.pallas_call(exchange_in_kernel, in_specs=[anywhere] * 2, out_specs=[an...  59.6 us
    pallas_call x1, Pallas kernels, exchange_out(): pl.pallas_call(exchange_out_kernel, in_specs=[anywhere, pl.BlockSpec(memo...  52.4 us
    pallas_call x1, Pallas kernels, attention(): pl.pallas_call(functools.partial(attention_kernel, K), in_specs=[vmem] *...  28.3 us
    pallas_call x1, Pallas kernels, pack(): pl.pallas_call(functools.partial(pack_kernel, K), grid=(KVH,), in_specs=[...  7.51 us
    pallas_call x1, Pallas kernels, unpack_rows(): pl.pallas_call(functools.partial(unpack_kernel, K), grid=(KVH,), in_specs...  6.91 us

profile of v4, /device:TPU:1, one launch (start us, length us, event | category | flops | bytes accessed | tf_op | source)
XLA Modules:
  0.0 160.3 jit_solution(7100134566489637037)
XLA Ops:
  0.6 0.8 copy.23
  1.4 0.7 reshape.77.prow
  2.1 0.7 reshape_reshape.4.pcol
  2.9 7.5 %pack_rows_to_messages.3 = (bf16[4,2,2,8,24,384]{5,4,3,2,1,0:T(8,128)(2,1)}, bf16[2,8,144,256]{3,2,1,0:T(8,128)(2,1)}, bf16[192,128]{1,0:T(8,128)(2,1)}) custom-call(s32[1,256]{1,0:T(1,128)} %reshape.77.prow, s32[256,1]{1,0:T(8,128)} %reshape_reshape.4.pcol, s32[1,128]{1,0:T(1,128)} %unp.1, s32[1,16]{1,0:T(1,128)} %lengths.1, bf16[128,4096]{1,0:T(8,128)(2,1)} %q.1, ...), custom_call_target="tpu_custom_call" | custom-call | tf_op jit(solution)/shard_map/pack_rows_to_messages/pallas_call | solution.py:86
  10.4 0.0 copy-start
  10.4 0.0 copy-start.1
  10.4 0.0 copy-start.2
  10.4 0.0 copy-start.4
  10.4 0.0 copy-start.5
  10.4 0.0 copy-start.6
  10.4 59.6 %exchange_in.3 = (bf16[128,24,384]{2,1,0:T(8,128)(2,1)}, bf16[128,24,128]{2,1,0:T(8,128)(2,1)}, bf16[16,144,256]{2,1,0:T(8,128)(2,1)S(1)}) custom-call(bf16[128,24,384]{2,1,0:T(8,128)(2,1)} %bitcast.23, bf16[16,144,256]{2,1,0:T(8,128)(2,1)} %bitcast.28), custom_call_target="tpu_custom_call" | custom-call | tf_op jit(solution)/shard_map/exchange_in/pallas_call | solution.py:213
  70.0 1.8 %slice_reduce_fusion = bf16[]{:T(256)} fusion(bf16[128,24,384]{2,1,0:T(8,128)(2,1)} %get-tuple-element.65), kind=kLoop, calls=%fused_computation | loop fusion | flops 127 | bytes 258 | tf_op jit(solution)/shard_map/reduce_max | solution.py:551
  72.5 0.0 copy-done
  72.5 0.0 copy-done.1
  72.5 0.0 copy-done.2
  72.5 0.0 copy-done.4
  72.5 0.0 copy-done.5
  72.5 0.0 copy-done.6
  72.5 87.7 %conditional.1 = ((bf16[128,4096]{1,0:T(8,128)(2,1)}, bf16[128,4096]{1,0:T(8,128)(2,1)}, bf16[128,1024]{1,0:T(8,128)(2,1)}, bf16[128,1024]{1,0:T(8,128)(2,1)})) conditional(s32[]{:T(128)} %convert_element_type.4, (bf16[128,24,384]{2,1,0:T(8,128)(2,1)}, bf16[128,24,128]{2,1,0:T(8,128)(2,1)}, bf16[16,144,256]{2,1,0:T(8,128)(2,1)S(1)}, ...), branch_computations={%region_1.0_spmd, %region_2.0_spmd} | conditional | bytes 196644 | solution.py:552
  72.5 28.3 %attention.2 = (bf16[16,128,256]{2,1,0:T(8,128)(2,1)}, bf16[16,192,256]{2,1,0:T(8,128)(2,1)}, bf16[16,192,128]{2,1,0:T(8,128)(2,1)}, bf16[16,192,128]{2,1,0:T(8,128)(2,1)}) custom-call(bf16[16,192,384]{2,1,0:T(8,128)(2,1)} %bitcast.22, bf16[16,192,128]{2,1,0:T(8,128)(2,1)} %bitcast.39, bf16[16,144,256]{2,1,0:T(8,128)(2,1)S(1)} %get-tuple-element.25.recvg), custom_call_target="tpu_custom_call" | custom-call | tf_op jit(solution)/shard_map/cond/branch_0_fun/attention/pallas_call | solution.py:467
  100.8 0.0 copy-start.3
  100.8 52.4 %exchange_out.2 = (bf16[128,24,256]{2,1,0:T(8,128)(2,1)}, bf16[128,24,128]{2,1,0:T(8,128)(2,1)}, bf16[16,128,256]{2,1,0:T(8,128)(2,1)}) custom-call(bf16[128,24,256]{2,1,0:T(8,128)(2,1)} %bitcast.27, bf16[128,24,128]{2,1,0:T(8,128)(2,1)} %bitcast.36, bf16[128,24,128]{2,1,0:T(8,128)(2,1)} %bitcast.37, bf16[16,128,256]{2,1,0:T(8,128)(2,1)} %get-tuple-element.29.srcg), custom_call_target="tpu_custom_call" | custom-call | tf_op jit(solution)/shard_map/cond/branch_0_fun/exchange_out/pallas_call | solution.py:281
  153.3 0.0 copy-done.3
  153.3 6.9 %messages_to_rows.2 = (bf16[128,4096]{1,0:T(8,128)(2,1)}, bf16[128,4096]{1,0:T(8,128)(2,1)}, bf16[128,1024]{1,0:T(8,128)(2,1)}, bf16[128,1024]{1,0:T(8,128)(2,1)}) custom-call(bf16[192,128]{1,0:T(8,128)(2,1)S(1)} %copy-done.3, bf16[4,2,2,8,24,256]{5,4,3,2,1,0:T(8,128)(2,1)} %bitcast.26, bf16[4,2,2,8,24,128]{5,4,3,2,1,0:T(8,128)(2,1)} %bitcast.38, ...), custom_call_target="tpu_custom_call" | custom-call | tf_op jit(solution)/shard_map/cond/branch_0_fun/messages_to_rows/pallas_call | solution.py:506
Async XLA Ops:
  10.4 62.1 %copy-start = (bf16[128,4096]{1,0:T(8,128)(2,1)S(1)}, bf16[128,4096]{1,0:T(8,128)(2,1)}, u32[]{:S(2)}) copy-start(bf16[128,4096]{1,0:T(8,128)(2,1)} %q.1) | copy-start | bytes 3145732
  10.4 62.1 %copy-start.1 = (bf16[128,4096]{1,0:T(8,128)(2,1)S(1)}, bf16[128,4096]{1,0:T(8,128)(2,1)}, u32[]{:S(2)}) copy-start(bf16[128,4096]{1,0:T(8,128)(2,1)} %g.1) | copy-start | bytes 3145732
  10.4 62.1 %copy-start.2 = (bf16[128,1024]{1,0:T(8,128)(2,1)S(1)}, bf16[128,1024]{1,0:T(8,128)(2,1)}, u32[]{:S(2)}) copy-start(bf16[128,1024]{1,0:T(8,128)(2,1)} %k.1) | copy-start | bytes 786436
  10.4 62.1 %copy-start.4 = (s32[1,128,2]{1,2,0:T(2,128)S(1)}, s32[1,128,2]{1,2,0:T(2,128)}, u32[]{:S(2)}) copy-start(s32[1,128,2]{1,2,0:T(2,128)} %param.13) | copy-start | bytes 3076
  10.4 62.1 %copy-start.5 = (s32[1,128]{1,0:T(1,128)S(1)}, s32[1,128]{1,0:T(1,128)}, u32[]{:S(2)}) copy-start(s32[1,128]{1,0:T(1,128)} %unp.1) | copy-start | bytes 1540
  10.4 62.1 %copy-start.6 = (s32[1,16]{1,0:T(1,128)S(1)}, s32[1,16]{1,0:T(1,128)}, u32[]{:S(2)}) copy-start(s32[1,16]{1,0:T(1,128)} %lengths.1) | copy-start | bytes 196
  100.8 52.5 %copy-start.3 = (bf16[192,128]{1,0:T(8,128)(2,1)S(1)}, bf16[192,128]{1,0:T(8,128)(2,1)}, u32[]{:S(2)}) copy-start(bf16[192,128]{1,0:T(8,128)(2,1)} %get-tuple-element.22.sel) | copy-start | bytes 147460 | tf_op jit(solution)/shard_map/cond

commit v5 on v4

--- a/solution.py
+++ b/solution.py
@@ -39,79 +39,6 @@
     return lax.broadcasted_iota(jnp.int32, shape, dim)
 
 
-def pack_kernel(K, prow, pcol, unp, lengths, q, k, v, g, send, sendg, sel, sel_s, over_s):
-    @pl.when(pl.program_id(0) == 0)
-    def _():
-        occupied = (prow[...] >= 0).astype(BF16)
-        a, b = iota((256, 256), 0), iota((256, 256), 1)
-        earlier = ((a < b) & (a // 32 == b // 32)).astype(BF16)
-        rank = dot(jnp.broadcast_to(occupied, (16, 256)), earlier, 1, 0)[0:1]
-        rank = rank.astype(jnp.int32)
-        slot = iota((1, 256), 1) // 32 * K + rank
-        slot = jnp.where((prow[...] >= 0) & ((rank < K - 1) | (K == FULL)), slot, -1)
-        over = jnp.max(jnp.where((prow[...] >= 0) & (rank >= K - 1), 1.0, 0.0), axis=1, keepdims=True)
-        last = (iota((8 * K, TOK), 0) % K == K - 1) & (K < FULL)
-        over_s[...] = jnp.where(last, over, 0.0)
-        place = (iota((8 * K, 256), 0) == slot).astype(BF16)
-        holds = (pcol[...] == iota((256, TOK), 1)).astype(BF16)
-        value = dot(place, holds, 1, 0).astype(BF16)
-        sel_s[...] = value
-        sel[...] = value
-
-    s = sel_s[...]
-    yq = dot(s, q[...], 1, 0)
-    yk = dot(s, k[...], 1, 0)
-    yv = dot(s, v[...], 1, 0)
-    ykv = (yk + over_s[...], yv + over_s[...])
-    for z in range(4):
-        for core in range(2):
-            for e in range(2):
-                rows = slice((2 * z + e) * K, (2 * z + e + 1) * K)
-                send[z, core, e, 0, :, 0:256] = yq[rows, core * 256 : (core + 1) * 256].astype(BF16)
-                send[z, core, e, 0, :, 256:384] = ykv[core][rows].astype(BF16)
-    r = iota((16, TOK), 0)
-    spread = (iota((16, TOK), 0) == iota((16, TOK), 1)).astype(BF16)
-    sizes = jnp.broadcast_to(lengths[...], (16, 16))
-    high = dot((sizes // 8).astype(F32).astype(BF16), spread, 1, 0)
-    low = dot((sizes % 8).astype(F32).astype(BF16), spread, 1, 0)
-    ints = jnp.where(r < 8, unp[...].astype(F32), jnp.where(r < 12, high, low)).astype(BF16)
-    for core in range(2):
-        sendg[core, 0, 0:TOK, :] = g[:, core * 256 : (core + 1) * 256]
-        sendg[core, 0, TOK:GROWS, 0:TOK] = ints
-        sendg[core, 0, TOK:GROWS, TOK:256] = jnp.zeros((16, 128), BF16)
-
-
-def pack(K, prow, pcol, unp, lengths, q, k, v, g):
-    whole = lambda shape: pl.BlockSpec(shape, lambda i: (0,) * len(shape))
-    return pl.pallas_call(
-        functools.partial(pack_kernel, K),
-        grid=(KVH,),
-        in_specs=[
-            whole((1, 256)),
-            whole((256, 1)),
-            whole((1, TOK)),
-            whole((1, 16)),
-            pl.BlockSpec((TOK, 512), lambda i: (0, i)),
-            pl.BlockSpec((TOK, 128), lambda i: (0, i)),
-            pl.BlockSpec((TOK, 128), lambda i: (0, i)),
-            pl.BlockSpec((TOK, 512), lambda i: (0, i)),
-        ],
-        out_specs=[
-            pl.BlockSpec((4, 2, 2, 1, K, COLS), lambda i: (0, 0, 0, i, 0, 0)),
-            pl.BlockSpec((2, 1, GROWS, 256), lambda i: (0, i, 0, 0)),
-            whole((8 * K, TOK)),
-        ],
-        out_shape=[
-            jax.ShapeDtypeStruct((4, 2, 2, KVH, K, COLS), BF16),
-            jax.ShapeDtypeStruct((2, KVH, GROWS, 256), BF16),
-            jax.ShapeDtypeStruct((8 * K, TOK), BF16),
-        ],
-        scratch_shapes=[pltpu.VMEM((8 * K, TOK), BF16), pltpu.VMEM((8 * K, TOK), F32)],
-        compiler_params=pltpu.CompilerParams(vmem_limit_bytes=VMEM_LIMIT),
-        name="pack_rows_to_messages",
-    )(prow, pcol, unp, lengths, q, k, v, g)
-
-
 def remote(src, dst, send_sem, recv_sem, target):
     return pltpu.make_async_remote_copy(
         src_ref=src,
@@ -160,69 +87,151 @@
         one(n)
 
 
+def greet_all():
+    barrier = pltpu.get_barrier_semaphore()
+
+    def greet(n, carry):
+        pl.semaphore_signal(barrier, inc=1, device_id=partner(n), device_id_type=MESH)
+        return carry
+
+    lax.fori_loop(1, DEV, greet, 0)
+    return lambda: pl.semaphore_wait(barrier, DEV - 1)
+
+
 def wait_all(src, dst, send_sem, recv_sem, count):
     d, c, _, _ = place()
     remote(src.at[pl.ds(0, count)], dst.at[pl.ds(0, count)], send_sem, recv_sem, (d, c)).wait()
 
 
 def exchange_in_kernel(
-    src, srcg, dst, other, dstg,
+    K, slots, unp, lengths, q, k, v, g, dst, other, dstg, sel,
+    send, sendg, over_s,
     send_sem, recv_sem, sendg_sem, recvg_sem, sendo_sem, recvo_sem, own_sem, owng_sem,
 ):
     d, c, z, core = place()
     me = d * CTX + c
     mine = core == lax.div(c, 8)
     first = core * 8 + lax.rem(c, 8)
+    all_here = greet_all()
+
+    r = iota((16, TOK), 0)
+    spread = (r == iota((16, TOK), 1)).astype(BF16)
+    sizes = jnp.broadcast_to(lengths[...], (16, 16))
+    high = dot((sizes // 8).astype(F32).astype(BF16), spread, 1, 0)
+    low = dot((sizes % 8).astype(F32).astype(BF16), spread, 1, 0)
+    ints = jnp.where(r < 8, unp[...].astype(F32), jnp.where(r < 12, high, low)).astype(BF16)
+    for h in range(KVH):
+        for p in range(2):
+            sendg[p * 8 + h, 0:TOK, :] = g[:, h * 512 + p * 256 : h * 512 + (p + 1) * 256]
+            sendg[p * 8 + h, TOK:GROWS, 0:TOK] = ints
+            sendg[p * 8 + h, TOK:GROWS, TOK:256] = jnp.zeros((16, 128), BF16)
+
+    all_here()
 
     def grads(j):
         target = (2 * z + lax.div(j, 8), core * 8 + lax.rem(j, 8))
-        remote(srcg.at[j], dstg.at[c], sendg_sem, recvg_sem, target).start()
-
-    own = pltpu.make_async_copy(src.at[me], dst.at[me], own_sem)
+        remote(sendg.at[j], dstg.at[c], sendg_sem, recvg_sem, target).start()
+
+    owng = pltpu.make_async_copy(sendg.at[first], dstg.at[c], owng_sem)
+
+    @pl.when(mine)
+    def _():
+        owng.start()
+
+    @pl.when(jnp.logical_not(mine))
+    def _():
+        grads(first)
+
+    def turn(n, carry):
+        grads(lax.rem(first + lax.rem(n * 5, CTX), CTX))
+        return carry
+
+    lax.fori_loop(1, CTX, turn, 0)
+
+    occupied = slots[...] >= 0
+    count = jnp.where(occupied[0:1], 1.0, 0.0) + jnp.where(occupied[1:2], 1.0, 0.0)
+    a, b = iota((DEV, DEV), 0), iota((DEV, DEV), 1)
+    earlier = ((a < b) & (a // CTX == b // CTX)).astype(BF16)
+    base = dot(jnp.broadcast_to(count, (16, DEV)).astype(BF16), earlier, 1, 0)[0:1].astype(jnp.int32)
+    rows_of = jnp.concatenate([slots[...].astype(F32), jnp.zeros((126, DEV), F32)], axis=0).T
+    value = jnp.zeros((8 * K, TOK), F32)
+    over = jnp.zeros((1, 1), F32)
+    for j in range(2):
+        rank = base + j
+        kept = occupied[j : j + 1]
+        if K < FULL:
+            lost = jnp.where(kept & (rank >= K - 1), 1.0, 0.0)
+            over = jnp.maximum(over, jnp.max(lost, axis=1, keepdims=True))
+            kept = kept & (rank < K - 1)
+        slot = jnp.where(kept, iota((1, DEV), 1) // CTX * K + rank, -1)
+        where = (iota((8 * K, DEV), 0) == slot).astype(BF16)
+        holds = (rows_of[:, j : j + 1] == iota((DEV, TOK), 1).astype(F32)).astype(BF16)
+        value = value + dot(where, holds, 1, 0)
+    s = value.astype(BF16)
+    sel[...] = s
+    last = (iota((8 * K, TOK), 0) % K == K - 1) & (K < FULL)
+    over_s[...] = jnp.where(last, over, 0.0)
+
+    def build(h, carry):
+        wide = pl.ds(pl.multiple_of(h * 512, 512), 512)
+        narrow = pl.ds(pl.multiple_of(h * 128, 128), 128)
+        yq = dot(sel[...], q[:, wide], 1, 0)
+        yk = dot(sel[...], k[:, narrow], 1, 0) + over_s[...]
+        yv = dot(sel[...], v[:, narrow], 1, 0) + over_s[...]
+        for n in range(DP):
+            rows = slice(n * K, (n + 1) * K)
+            for p, ykv in ((0, yk), (1, yv)):
+                t = ((n // 2 * 2 + p) * 2 + n % 2) * 8 + h
+                send[t, :, 0:256] = yq[rows, p * 256 : (p + 1) * 256].astype(BF16)
+                send[t, :, 256:384] = ykv[rows].astype(BF16)
+        return carry
+
+    lax.fori_loop(0, KVH, build, 0)
+
+    own = pltpu.make_async_copy(send.at[me], dst.at[me], own_sem)
     own.start()
-    owng = pltpu.make_async_copy(srcg.at[first], dstg.at[c], owng_sem)
-
-    @pl.when(mine)
-    def _():
-        owng.start()
-
-    @pl.when(jnp.logical_not(mine))
-    def _():
-        grads(first)
-
-    to_all(src, dst, send_sem, recv_sem, lambda n: grads(lax.rem(first + lax.rem(n * 5, CTX), CTX)))
+    to_all(send, dst, send_sem, recv_sem)
     own.wait()
-    wait_all(src, dst, send_sem, recv_sem, DEV - 1)
+    wait_all(send, dst, send_sem, recv_sem, DEV - 1)
     swap = remote(dst.at[:, :, pl.ds(256, 128)], other, sendo_sem, recvo_sem, (2 * z + 1 - core, c))
     swap.start()
 
     @pl.when(mine)
     def _():
         owng.wait()
-        wait_all(srcg, dstg, sendg_sem, recvg_sem, CTX - 1)
+        wait_all(sendg, dstg, sendg_sem, recvg_sem, CTX - 1)
 
     @pl.when(jnp.logical_not(mine))
     def _():
-        wait_all(srcg, dstg, sendg_sem, recvg_sem, CTX)
+        wait_all(sendg, dstg, sendg_sem, recvg_sem, CTX)
 
     swap.wait()
 
 
-def exchange_in(src, srcg):
+def exchange_in(K, slots, unp, lengths, q, k, v, g):
     anywhere = pl.BlockSpec(memory_space=pl.ANY)
+    vmem = pl.BlockSpec(memory_space=pltpu.VMEM)
     return pl.pallas_call(
-        exchange_in_kernel,
-        in_specs=[anywhere] * 2,
-        out_specs=[anywhere] * 3,
+        functools.partial(exchange_in_kernel, K),
+        in_specs=[vmem] * 7,
+        out_specs=[anywhere] * 3 + [vmem],
         out_shape=[
-            jax.ShapeDtypeStruct(src.shape, BF16),
-            jax.ShapeDtypeStruct(src.shape[:2] + (128,), BF16),
-            jax.ShapeDtypeStruct(srcg.shape, BF16),
-        ],
-        scratch_shapes=[pltpu.SemaphoreType.DMA] * 8,
-        compiler_params=pltpu.CompilerParams(has_side_effects=True),
+            jax.ShapeDtypeStruct((DEV, K, COLS), BF16),
+            jax.ShapeDtypeStruct((DEV, K, 128), BF16),
+            jax.ShapeDtypeStruct((CTX, GROWS, 256), BF16),
+            jax.ShapeDtypeStruct((8 * K, TOK), BF16),
+        ],
+        scratch_shapes=[
+            pltpu.VMEM((DEV, K, COLS), BF16),
+            pltpu.VMEM((CTX, GROWS, 256), BF16),
+            pltpu.VMEM((8 * K, TOK), F32),
+        ]
+        + [pltpu.SemaphoreType.DMA] * 8,
+        compiler_params=pltpu.CompilerParams(
+            has_side_effects=True, vmem_limit_bytes=VMEM_LIMIT, collective_id=K
+        ),
         name="exchange_in",
-    )(src, srcg)
+    )(slots, unp, lengths, q, k, v, g)
 
 
 def exchange_out_kernel(
@@ -294,7 +303,7 @@
 
 
 def attention_kernel(
-    K, recv, other, recvg, att, back, keep, give, x, keyt, valuet, xo, mid, dk, dv, col, lengths
+    K, recv, other, recvg, att, back, keep, give, over, x, keyt, valuet, xo, mid, dk, dv, col, lengths
 ):
     scale = 1.0 / math.sqrt(DH)
     first_core = lax.rem(lax.axis_index("dp"), 2) == 0
@@ -316,6 +325,12 @@
     base = dot(count.astype(BF16), before, 1, 0)
     u = iota((256, 128), 0)
     col[...] = base + (u % 2 + (u // 2) % 8 * K).astype(F32)
+
+    most = jnp.zeros((8 * K, DH), F32)
+    for grp in range(16):
+        most = jnp.maximum(most, recv[grp, :, 256:384].astype(F32))
+    flags = (iota((8 * K, DH), 0) % K == K - 1) & (K < FULL)
+    over[0] = jnp.max(jnp.where(flags, most, 0.0))
 
     own_c = iota((256, 128), 0) // 16 == iota((256, 128), 1)
 
@@ -467,12 +482,13 @@
     return pl.pallas_call(
         functools.partial(attention_kernel, K),
         in_specs=[vmem] * 3,
-        out_specs=[vmem] * 4,
+        out_specs=[vmem] * 4 + [pl.BlockSpec(memory_space=pltpu.SMEM)],
         out_shape=[
             jax.ShapeDtypeStruct((CTX, TOK, 256), BF16),
             jax.ShapeDtypeStruct((16, 8 * K, 256), BF16),
             jax.ShapeDtypeStruct((16, 8 * K, 128), BF16),
             jax.ShapeDtypeStruct((16, 8 * K, 128), BF16),
+            jax.ShapeDtypeStruct((1,), F32),
         ],
         scratch_shapes=[
             pltpu.VMEM((SEQ, 512), BF16),
@@ -529,30 +545,28 @@
     )(sel, back, backkv, att)
 
 
-def forward(K, q_load, k_load, v_load, grad_out, pack_rows, unpack, doc_lengths):
-    flat = pack_rows.reshape(1, 2 * DEV)
-    send, sendg, sel = pack(
-        K, flat, flat.reshape(2 * DEV, 1), unpack, doc_lengths, q_load, k_load, v_load, grad_out
+def middle(K, q_load, k_load, v_load, grad_out, pack_rows, unpack, doc_lengths):
+    recv, other, recvg, sel = exchange_in(
+        K, pack_rows[0].T, unpack, doc_lengths, q_load, k_load, v_load, grad_out
     )
-    return sel, *exchange_in(send.reshape(DEV, K, COLS), sendg.reshape(CTX, GROWS, 256))
-
-
-def finish(K, sel, recv, other, recvg):
     recv, other = (a.reshape(16, 8 * K, -1) for a in (recv, other))
-    att, *parts = attention(K, recv, other, recvg)
-    back, keep, give = (a.reshape(DEV, K, -1) for a in parts)
+    *parts, over = attention(K, recv, other, recvg)
+    return over[0] > 0.5, (sel, *parts)
+
+
+def finish(K, sel, att, back, keep, give):
+    back, keep, give = (a.reshape(DEV, K, -1) for a in (back, keep, give))
     returned, returnedkv, turned = exchange_out(back, keep, give, att)
     returned, returnedkv = (a.reshape(4, 2, 2, KVH, K, -1) for a in (returned, returnedkv))
     return unpack_rows(K, sel, returned, returnedkv, turned.reshape(2, KVH, TOK, 256))
 
 
 def local(*operands):
-    sel, recv, other, recvg = forward(SHORT, *operands)
-    over = jnp.max(recv[:, SHORT - 1, COLS - 1].astype(F32)) > 0.5
+    over, parts = middle(SHORT, *operands)
     return lax.cond(
         over,
-        lambda: finish(FULL, *forward(FULL, *operands)),
-        lambda: finish(SHORT, sel, recv, other, recvg),
+        lambda: finish(FULL, *middle(FULL, *operands)[1]),
+        lambda: finish(SHORT, *parts),
     )
 
 

time: 161 us -> 149 us (0.925)
  Pallas kernels: 155 us -> 147 us
  local copies, waits for them, and re-layouts: 2.27 us -> 0.04 us
  other arithmetic: 1.76 us -> 0 us
    pallas_call x2 -> x1, Pallas kernels: 67.1 us -> 60.2 us  [exchange_in(): pl.pallas_call(functools.partial(exchange_in_kernel, K), in_specs=[vmem]...]
    reduce_max x1 -> x0, other arithmetic: 1.76 us -> none  [local(): over = jnp.max(recv[:, SHORT - 1, COLS - 1].astype(F32)) > 0.5]
where the time goes in v5:
time: 149 us
  Pallas kernels  147 us (99%)
    pallas_call x1, Pallas kernels, exchange_in(): pl.pallas_call(functools.partial(exchange_in_kernel, K), in_specs=[vmem]...  60.2 us
    pallas_call x1, Pallas kernels, exchange_out(): pl.pallas_call(exchange_out_kernel, in_specs=[anywhere, pl.BlockSpec(memo...  50.9 us
    pallas_call x1, Pallas kernels, attention(): pl.pallas_call(functools.partial(attention_kernel, K), in_specs=[vmem] *...  29.3 us
    pallas_call x1, Pallas kernels, unpack_rows(): pl.pallas_call(functools.partial(unpack_kernel, K), grid=(KVH,), in_specs...  6.91 us

profile of v5, /device:TPU:1, one launch (start us, length us, event | category | flops | bytes accessed | tf_op | source)
XLA Modules:
  0.0 148.8 jit_solution(7160488240687334024)
XLA Ops:
  0.6 60.2 %exchange_in.3 = (bf16[128,24,384]{2,1,0:T(8,128)(2,1)}, bf16[128,24,128]{2,1,0:T(8,128)(2,1)}, bf16[16,144,256]{2,1,0:T(8,128)(2,1)}, bf16[192,128]{1,0:T(8,128)(2,1)S(1)}) custom-call(s32[2,128]{1,0:T(2,128)} %bitcast.39, s32[1,128]{1,0:T(1,128)} %unp.1, s32[1,16]{1,0:T(1,128)} %lengths.1, bf16[128,4096]{1,0:T(8,128)(2,1)} %q.1, bf16[128,1024]{1,0:T(8,128)(2,1)} %k.1, ...), custom_call_target="tpu_custom_call" | custom-call | tf_op jit(solution)/shard_map/exchange_in/pallas_call | solution.py:214
  60.8 0.0 copy-start
  60.8 0.0 copy-start.1
  60.9 0.0 copy-start.2
  60.9 0.0 copy-start.3
  60.9 0.0 copy-start.4
  60.9 0.0 copy-start.5
  60.9 0.0 copy-start.6
  60.9 29.3 %attention.3 = (bf16[16,128,256]{2,1,0:T(8,128)(2,1)S(1)}, bf16[16,192,256]{2,1,0:T(8,128)(2,1)S(1)}, bf16[16,192,128]{2,1,0:T(8,128)(2,1)S(1)}, bf16[16,192,128]{2,1,0:T(8,128)(2,1)S(1)}, f32[1]{0:T(128)}) custom-call(bf16[16,192,384]{2,1,0:T(8,128)(2,1)} %bitcast.24, bf16[16,192,128]{2,1,0:T(8,128)(2,1)} %bitcast.38, ...), custom_call_target="tpu_custom_call" | custom-call | tf_op jit(solution)/shard_map/attention/pallas_call | solution.py:482
  90.9 0.0 copy-done
  90.9 0.0 copy-done.1
  90.9 0.0 copy-done.2
  90.9 0.0 copy-done.3
  90.9 0.0 copy-done.4
  90.9 0.0 copy-done.5
  90.9 0.0 copy-done.6
  90.9 57.8 %conditional.1 = ((bf16[128,4096]{1,0:T(8,128)(2,1)}, bf16[128,4096]{1,0:T(8,128)(2,1)}, bf16[128,1024]{1,0:T(8,128)(2,1)}, bf16[128,1024]{1,0:T(8,128)(2,1)})) conditional(s32[]{:T(128)} %bitcast.21, (bf16[16,192,256]{2,1,0:T(8,128)(2,1)S(1)}, bf16[16,192,128]{2,1,0:T(8,128)(2,1)S(1)}, bf16[16,192,128]{2,1,0:T(8,128)(2,1)S(1)}, ...), branch_computations={%region_0.0_spmd, %region_1.0_spmd} | conditional | bytes 8 | solution.py:566
  91.0 50.9 %exchange_out.2 = (bf16[128,24,256]{2,1,0:T(8,128)(2,1)}, bf16[128,24,128]{2,1,0:T(8,128)(2,1)}, bf16[16,128,256]{2,1,0:T(8,128)(2,1)}) custom-call(bf16[128,24,256]{2,1,0:T(8,128)(2,1)S(1)} %bitcast.27, bf16[128,24,128]{2,1,0:T(8,128)(2,1)S(1)} %bitcast.35, bf16[128,24,128]{2,1,0:T(8,128)(2,1)S(1)} %bitcast.36, bf16[16,128,256]{2,1,0:T(8,128)(2,1)S(1)} %get-tuple-element.28.srcg), custom_call_target="tpu_custom_call" | custom-call | tf_op jit(solution)/shard_map/cond/branch_0_fun/exchange_out/pallas_call | solution.py:290
  141.8 6.9 %messages_to_rows.2 = (bf16[128,4096]{1,0:T(8,128)(2,1)}, bf16[128,4096]{1,0:T(8,128)(2,1)}, bf16[128,1024]{1,0:T(8,128)(2,1)}, bf16[128,1024]{1,0:T(8,128)(2,1)}) custom-call(bf16[192,128]{1,0:T(8,128)(2,1)S(1)} %get-tuple-element.24.sel, bf16[4,2,2,8,24,256]{5,4,3,2,1,0:T(8,128)(2,1)} %bitcast.28, bf16[4,2,2,8,24,128]{5,4,3,2,1,0:T(8,128)(2,1)} %bitcast.37, ...), custom_call_target="tpu_custom_call" | custom-call | tf_op jit(solution)/shard_map/cond/branch_0_fun/messages_to_rows/pallas_call | solution.py:522
Async XLA Ops:
  60.8 30.0 %copy-start = (bf16[128,4096]{1,0:T(8,128)(2,1)S(1)}, bf16[128,4096]{1,0:T(8,128)(2,1)}, u32[]{:S(2)}) copy-start(bf16[128,4096]{1,0:T(8,128)(2,1)} %q.1) | copy-start | bytes 3145732
  60.8 30.0 %copy-start.1 = (bf16[128,4096]{1,0:T(8,128)(2,1)S(1)}, bf16[128,4096]{1,0:T(8,128)(2,1)}, u32[]{:S(2)}) copy-start(bf16[128,4096]{1,0:T(8,128)(2,1)} %g.1) | copy-start | bytes 3145732
  60.9 30.0 %copy-start.2 = (bf16[128,1024]{1,0:T(8,128)(2,1)S(1)}, bf16[128,1024]{1,0:T(8,128)(2,1)}, u32[]{:S(2)}) copy-start(bf16[128,1024]{1,0:T(8,128)(2,1)} %k.1) | copy-start | bytes 786436
  60.9 30.0 %copy-start.3 = (bf16[128,1024]{1,0:T(8,128)(2,1)S(1)}, bf16[128,1024]{1,0:T(8,128)(2,1)}, u32[]{:S(2)}) copy-start(bf16[128,1024]{1,0:T(8,128)(2,1)} %v.1) | copy-start | bytes 786436
  60.9 30.0 %copy-start.4 = (s32[1,128,2]{1,2,0:T(2,128)S(1)}, s32[1,128,2]{1,2,0:T(2,128)}, u32[]{:S(2)}) copy-start(s32[1,128,2]{1,2,0:T(2,128)} %param.13) | copy-start | bytes 3076
  60.9 30.0 %copy-start.5 = (s32[1,128]{1,0:T(1,128)S(1)}, s32[1,128]{1,0:T(1,128)}, u32[]{:S(2)}) copy-start(s32[1,128]{1,0:T(1,128)} %unp.1) | copy-start | bytes 1540
  60.9 30.0 %copy-start.6 = (s32[1,16]{1,0:T(1,128)S(1)}, s32[1,16]{1,0:T(1,128)}, u32[]{:S(2)}) copy-start(s32[1,16]{1,0:T(1,128)} %lengths.1) | copy-start | bytes 196

commit v6 on v5

--- a/solution.py
+++ b/solution.py
@@ -50,6 +50,16 @@
     )
 
 
+def row_slots(row):
+    return (iota((256, TOK), 0).astype(F32) == row).astype(BF16)
+
+
+def compact_slot(col, grp):
+    tab = col[pl.ds(pl.multiple_of(grp * 16, 16), 16), :]
+    own_c = iota((256, 128), 0) // 16 == iota((256, 128), 1)
+    return jnp.where(own_c, jnp.concatenate([tab] * CTX, axis=0), 0.0).astype(BF16)
+
+
 def place():
     d = lax.axis_index("dp")
     c = lax.axis_index("ctx")
@@ -67,7 +77,7 @@
     return lax.rem(z + dz, 4) * 2 + lax.rem(core + dcore, 2), lax.rem(x + dx, 4) * 4 + lax.rem(y + dy, 4)
 
 
-def to_all(src, dst, send_sem, recv_sem, beside=None):
+def to_all(src, dst, send_sem, recv_sem):
     d, c, _, _ = place()
     me = d * CTX + c
 
@@ -76,8 +86,6 @@
         remote(src.at[td * CTX + tc], dst.at[me], send_sem, recv_sem, (td, tc)).start()
 
     def some(n, carry):
-        if beside is not None:
-            beside(n)
         for i in range(8):
             one(8 * n - 7 + i)
         return carry
@@ -235,8 +243,8 @@
 
 
 def exchange_out_kernel(
-    src, keep, give, srcg, dst, dstkv, dstg,
-    other, total,
+    K, rows_in, col, unp, srcg, dst, dstkv, dstg,
+    mid, src, keep, give, other, total,
     send_sem, recv_sem, sendk_sem, recvk_sem, sendg_sem, recvg_sem, sendo_sem, recvo_sem,
     own_sem, ownk_sem, owng_sem,
 ):
@@ -249,21 +257,46 @@
     def grads(j):
         remote(srcg.at[j], dstg.at[slot], sendg_sem, recvg_sem, (2 * z + e, j)).start()
 
+    owng = pltpu.make_async_copy(srcg.at[c], dstg.at[slot], owng_sem)
+
+    @pl.when(mine)
+    def _():
+        owng.start()
+
+    @pl.when(jnp.logical_not(mine))
+    def _():
+        grads(c)
+
+    def turn(n, carry):
+        grads(lax.rem(c + lax.rem(n * 5, CTX), CTX))
+        return carry
+
+    lax.fori_loop(1, CTX, turn, 0)
+
+    for n in range(CTX):
+        slots = row_slots(unp[n : n + 1, :])
+        mid[n] = dot(slots, rows_in[n * TOK : (n + 1) * TOK, :], 1, 0).astype(BF16)
+
+    def unsort_senders(grp, carry):
+        r0 = pl.multiple_of(grp * 16, 16)
+        rows = jnp.concatenate([mid[n, pl.ds(r0, 16), :] for n in range(CTX)], axis=0)
+        where = dot(jnp.ones((8 * K, 128), BF16), compact_slot(col, grp), 1, 1)
+        t = (where == iota((8 * K, 256), 0).astype(F32)).astype(BF16)
+        out = dot(t, rows, 1, 0)
+        for n in range(8):
+            part = out[n * K : (n + 1) * K]
+            src[grp * 8 + n] = part[:, 0:256].astype(BF16)
+            keep[grp * 8 + n] = part[:, 256:384].astype(BF16)
+            give[grp * 8 + n] = part[:, 384:512].astype(BF16)
+        return carry
+
+    lax.fori_loop(0, 16, unsort_senders, 0, unroll=4)
+
     swap = remote(give, other, sendo_sem, recvo_sem, (2 * z + 1 - core, c))
     swap.start()
     own = pltpu.make_async_copy(src.at[me], dst.at[me], own_sem)
     own.start()
-    owng = pltpu.make_async_copy(srcg.at[c], dstg.at[slot], owng_sem)
-
-    @pl.when(mine)
-    def _():
-        owng.start()
-
-    @pl.when(jnp.logical_not(mine))
-    def _():
-        grads(c)
-
-    to_all(src, dst, send_sem, recv_sem, lambda n: grads(lax.rem(c + lax.rem(n * 5, CTX), CTX)))
+    to_all(src, dst, send_sem, recv_sem)
     swap.wait()
     total[...] = (keep[...].astype(F32) + other[...].astype(F32)).astype(BF16)
     ownk = pltpu.make_async_copy(total.at[me], dstkv.at[me], ownk_sem)
@@ -285,25 +318,29 @@
     wait_all(total, dstkv, sendk_sem, recvk_sem, DEV - 1)
 
 
-def exchange_out(src, keep, give, srcg):
+def exchange_out(K, rows, col, unp, srcg):
     anywhere = pl.BlockSpec(memory_space=pl.ANY)
+    vmem = pl.BlockSpec(memory_space=pltpu.VMEM)
+    wide = pltpu.VMEM((DEV, K, 256), BF16)
+    narrow = pltpu.VMEM((DEV, K, 128), BF16)
     return pl.pallas_call(
-        exchange_out_kernel,
-        in_specs=[anywhere, pl.BlockSpec(memory_space=pltpu.VMEM), anywhere, anywhere],
+        functools.partial(exchange_out_kernel, K),
+        in_specs=[vmem, vmem, vmem, anywhere],
         out_specs=[anywhere] * 3,
         out_shape=[
-            jax.ShapeDtypeStruct(src.shape, BF16),
-            jax.ShapeDtypeStruct(keep.shape, BF16),
+            jax.ShapeDtypeStruct((DEV, K, 256), BF16),
+            jax.ShapeDtypeStruct((DEV, K, 128), BF16),
             jax.ShapeDtypeStruct(srcg.shape, BF16),
         ],
-        scratch_shapes=[pltpu.VMEM(keep.shape, BF16)] * 2 + [pltpu.SemaphoreType.DMA] * 11,
+        scratch_shapes=[pltpu.VMEM((CTX, 256, 512), BF16), wide, narrow, narrow, narrow, narrow]
+        + [pltpu.SemaphoreType.DMA] * 11,
         compiler_params=pltpu.CompilerParams(has_side_effects=True, vmem_limit_bytes=VMEM_LIMIT),
         name="exchange_out",
-    )(src, keep, give, srcg)
+    )(rows, col, unp, srcg)
 
 
 def attention_kernel(
-    K, recv, other, recvg, att, back, keep, give, over, x, keyt, valuet, xo, mid, dk, dv, col, lengths
+    K, recv, other, recvg, att, xo, col, unp, over, x, keyt, valuet, mid, dk, dv, lengths
 ):
     scale = 1.0 / math.sqrt(DH)
     first_core = lax.rem(lax.axis_index("dp"), 2) == 0
@@ -313,8 +350,10 @@
         lengths[n] = jnp.sum(jnp.where(iota((1, TOK), 1) == n, sizes, 0))
 
     def slots_of(c):
-        row = recvg[c, TOK : TOK + 8, 0:TOK].astype(F32)[0:1]
-        return (iota((256, TOK), 0).astype(F32) == row).astype(BF16)
+        return row_slots(recvg[c, TOK : TOK + 8, 0:TOK].astype(F32)[0:1])
+
+    for c in range(CTX):
+        unp[c : c + 1, :] = recvg[c, TOK : TOK + 8, 0:TOK].astype(F32)[0:1]
 
     occ = jnp.zeros((256, 128), F32)
     for c in range(CTX):
@@ -332,15 +371,9 @@
     flags = (iota((8 * K, DH), 0) % K == K - 1) & (K < FULL)
     over[0] = jnp.max(jnp.where(flags, most, 0.0))
 
-    own_c = iota((256, 128), 0) // 16 == iota((256, 128), 1)
-
-    def compact_slot(grp):
-        tab = col[pl.ds(pl.multiple_of(grp * 16, 16), 16), :]
-        return jnp.where(own_c, jnp.concatenate([tab] * CTX, axis=0), 0.0).astype(BF16)
-
     def sort_senders(grp, carry):
         r0 = pl.multiple_of(grp * 16, 16)
-        slot = dot(compact_slot(grp), jnp.ones((128, 8 * K), BF16), 1, 0)
+        slot = dot(compact_slot(col, grp), jnp.ones((128, 8 * K), BF16), 1, 0)
         t = (slot == iota((256, 8 * K), 1).astype(F32)).astype(BF16)
         rows = dot(t, recv[grp], 1, 0).astype(BF16)
         rows2 = dot(t, other[grp], 1, 0).astype(BF16)
@@ -349,7 +382,7 @@
             mid[c, pl.ds(r0, 16), 384:512] = rows2[c * 16 : (c + 1) * 16]
         return carry
 
-    lax.fori_loop(0, 16, sort_senders, 0, unroll=4)
+    lax.fori_loop(0, 16, sort_senders, 0, unroll=16)
 
     def sort_rows(c, carry):
         y = dot(slots_of(c), mid[c], 0, 0)
@@ -363,7 +396,7 @@
         valuet[:, r] = values.T.astype(BF16)
         return carry
 
-    lax.fori_loop(0, CTX, sort_rows, 0, unroll=4)
+    lax.fori_loop(0, CTX, sort_rows, 0, unroll=16)
 
     dk[...] = jnp.zeros_like(dk)
     dv[...] = jnp.zeros_like(dv)
@@ -455,27 +488,6 @@
     xo[:, 256:384] = jnp.where(first_core, dk[...], dv[...]).astype(BF16)
     xo[:, 384:512] = jnp.where(first_core, dv[...], dk[...]).astype(BF16)
 
-    def unsort_rows(c, carry):
-        mid[c] = dot(
-            slots_of(c), xo[pl.ds(pl.multiple_of(c * TOK, TOK), TOK), :], 1, 0
-        ).astype(BF16)
-        return carry
-
-    lax.fori_loop(0, CTX, unsort_rows, 0, unroll=4)
-
-    def unsort_senders(grp, carry):
-        r0 = pl.multiple_of(grp * 16, 16)
-        rows = jnp.concatenate([mid[c, pl.ds(r0, 16), :] for c in range(CTX)], axis=0)
-        slot = dot(jnp.ones((8 * K, 128), BF16), compact_slot(grp), 1, 1)
-        t = (slot == iota((8 * K, 256), 0).astype(F32)).astype(BF16)
-        out = dot(t, rows, 1, 0).astype(BF16)
-        back[grp] = out[:, 0:256]
-        keep[grp] = out[:, 256:384]
-        give[grp] = out[:, 384:512]
-        return carry
-
-    lax.fori_loop(0, 16, unsort_senders, 0, unroll=4)
-
 
 def attention(K, recv, other, recvg):
     vmem = pl.BlockSpec(memory_space=pltpu.VMEM)
@@ -485,20 +497,18 @@
         out_specs=[vmem] * 4 + [pl.BlockSpec(memory_space=pltpu.SMEM)],
         out_shape=[
             jax.ShapeDtypeStruct((CTX, TOK, 256), BF16),
-            jax.ShapeDtypeStruct((16, 8 * K, 256), BF16),
-            jax.ShapeDtypeStruct((16, 8 * K, 128), BF16),
-            jax.ShapeDtypeStruct((16, 8 * K, 128), BF16),
+            jax.ShapeDtypeStruct((SEQ, 512), BF16),
+            jax.ShapeDtypeStruct((256, 128), F32),
+            jax.ShapeDtypeStruct((CTX, TOK), F32),
             jax.ShapeDtypeStruct((1,), F32),
         ],
         scratch_shapes=[
             pltpu.VMEM((SEQ, 512), BF16),
             pltpu.VMEM((DH, SEQ), BF16),
             pltpu.VMEM((DH, SEQ), BF16),
-            pltpu.VMEM((SEQ, 512), BF16),
             pltpu.VMEM((CTX, 256, 512), BF16),
             pltpu.VMEM((SEQ, DH), F32),
             pltpu.VMEM((SEQ, DH), F32),
-            pltpu.VMEM((256, 128), F32),
             pltpu.SMEM((16,), jnp.int32),
         ],
         compiler_params=pltpu.CompilerParams(vmem_limit_bytes=VMEM_LIMIT),
@@ -554,9 +564,8 @@
     return over[0] > 0.5, (sel, *parts)
 
 
-def finish(K, sel, att, back, keep, give):
-    back, keep, give = (a.reshape(DEV, K, -1) for a in (back, keep, give))
-    returned, returnedkv, turned = exchange_out(back, keep, give, att)
+def finish(K, sel, att, rows, col, unp):
+    returned, returnedkv, turned = exchange_out(K, rows, col, unp, att)
     returned, returnedkv = (a.reshape(4, 2, 2, KVH, K, -1) for a in (returned, returnedkv))
     return unpack_rows(K, sel, returned, returnedkv, turned.reshape(2, KVH, TOK, 256))
 

time: 149 us -> 143 us (0.960)
  Pallas kernels: 147 us -> 141 us
    pallas_call x1, Pallas kernels: 29.3 us -> 23.2 us  [attention(): pl.pallas_call(functools.partial(attention_kernel, K), in_specs=[vmem] *...]
where the time goes in v6:
time: 143 us
  Pallas kernels  141 us (99%)
  between operations  1.63 us (1%)
    pallas_call x1, Pallas kernels, exchange_in(): pl.pallas_call(functools.partial(exchange_in_kernel, K), in_specs=[vmem]...  60.2 us
    pallas_call x1, Pallas kernels, exchange_out(): pl.pallas_call(functools.partial(exchange_out_kernel, K), in_specs=[vmem,...  50.8 us
    pallas_call x1, Pallas kernels, attention(): pl.pallas_call(functools.partial(attention_kernel, K), in_specs=[vmem] *...  23.2 us
    pallas_call x1, Pallas kernels, unpack_rows(): pl.pallas_call(functools.partial(unpack_kernel, K), grid=(KVH,), in_specs...  6.91 us

profile of v6, /device:TPU:1, one launch (start us, length us, event | category | flops | bytes accessed | tf_op | source)
XLA Modules:
  0.0 143.2 jit_solution(15180123807898792375)
XLA Ops:
  0.6 60.2 %exchange_in.3 = (bf16[128,24,384]{2,1,0:T(8,128)(2,1)}, bf16[128,24,128]{2,1,0:T(8,128)(2,1)}, bf16[16,144,256]{2,1,0:T(8,128)(2,1)}, bf16[192,128]{1,0:T(8,128)(2,1)S(1)}) custom-call(s32[2,128]{1,0:T(2,128)} %bitcast.27, s32[1,128]{1,0:T(1,128)} %unp.1, s32[1,16]{1,0:T(1,128)} %lengths.1, bf16[128,4096]{1,0:T(8,128)(2,1)} %q.1, bf16[128,1024]{1,0:T(8,128)(2,1)} %k.1, ...), custom_call_target="tpu_custom_call" | custom-call | tf_op jit(solution)/shard_map/exchange_in/pallas_call | solution.py:222
  60.8 0.0 copy-start
  60.9 0.0 copy-start.1
  60.9 0.0 copy-start.2
  60.9 0.0 copy-start.3
  60.9 0.0 copy-start.4
  60.9 0.0 copy-start.5
  60.9 0.0 copy-start.6
  60.9 23.2 %attention.3 = (bf16[16,128,256]{2,1,0:T(8,128)(2,1)S(1)}, bf16[2048,512]{1,0:T(8,128)(2,1)S(1)}, f32[256,128]{1,0:T(8,128)S(1)}, f32[16,128]{1,0:T(8,128)S(1)}, f32[1]{0:T(128)}) custom-call(bf16[16,192,384]{2,1,0:T(8,128)(2,1)} %bitcast.18, bf16[16,192,128]{2,1,0:T(8,128)(2,1)} %bitcast.26, bf16[16,144,256]{2,1,0:T(8,128)(2,1)} %get-tuple-element.65.recvg), custom_call_target="tpu_custom_call" | custom-call | tf_op jit(solution)/shard_map/attention/pallas_call | solution.py:494
  84.8 0.0 copy-done
  84.8 0.0 copy-done.1
  84.8 0.0 copy-done.2
  84.9 0.0 copy-done.3
  84.9 0.0 copy-done.4
  84.9 0.0 copy-done.5
  84.9 0.0 copy-done.6
  84.9 58.0 %conditional.1 = ((bf16[128,4096]{1,0:T(8,128)(2,1)}, bf16[128,4096]{1,0:T(8,128)(2,1)}, bf16[128,1024]{1,0:T(8,128)(2,1)}, bf16[128,1024]{1,0:T(8,128)(2,1)})) conditional(s32[]{:T(128)} %bitcast.15, (bf16[2048,512]{1,0:T(8,128)(2,1)S(1)}, f32[256,128]{1,0:T(8,128)S(1)}, f32[16,128]{1,0:T(8,128)S(1)}, bf16[16,128,256]{2,1,0:T(8,128)(2,1)S(1)}, ...), branch_computations={%region_0.0_spmd, %region_1.0_spmd} | conditional | bytes 8 | solution.py:575
  84.9 50.8 %exchange_out.2 = (bf16[128,24,256]{2,1,0:T(8,128)(2,1)}, bf16[128,24,128]{2,1,0:T(8,128)(2,1)}, bf16[16,128,256]{2,1,0:T(8,128)(2,1)}) custom-call(bf16[2048,512]{1,0:T(8,128)(2,1)S(1)} %get-tuple-element.25.rows_in, f32[256,128]{1,0:T(8,128)S(1)} %get-tuple-element.26.col, f32[16,128]{1,0:T(8,128)S(1)} %get-tuple-element.27.unp, ...), custom_call_target="tpu_custom_call" | custom-call | tf_op jit(solution)/shard_map/cond/branch_0_fun/exchange_out/pallas_call | solution.py:326
  135.7 6.9 %messages_to_rows.2 = (bf16[128,4096]{1,0:T(8,128)(2,1)}, bf16[128,4096]{1,0:T(8,128)(2,1)}, bf16[128,1024]{1,0:T(8,128)(2,1)}, bf16[128,1024]{1,0:T(8,128)(2,1)}) custom-call(bf16[192,128]{1,0:T(8,128)(2,1)S(1)} %get-tuple-element.24.sel, bf16[4,2,2,8,24,256]{5,4,3,2,1,0:T(8,128)(2,1)} %bitcast.20, bf16[4,2,2,8,24,128]{5,4,3,2,1,0:T(8,128)(2,1)} %bitcast.25, ...), custom_call_target="tpu_custom_call" | custom-call | tf_op jit(solution)/shard_map/cond/branch_0_fun/messages_to_rows/pallas_call | solution.py:532
Async XLA Ops:
  60.8 24.0 %copy-start = (bf16[128,4096]{1,0:T(8,128)(2,1)S(1)}, bf16[128,4096]{1,0:T(8,128)(2,1)}, u32[]{:S(2)}) copy-start(bf16[128,4096]{1,0:T(8,128)(2,1)} %q.1) | copy-start | bytes 3145732
  60.9 24.0 %copy-start.1 = (bf16[128,4096]{1,0:T(8,128)(2,1)S(1)}, bf16[128,4096]{1,0:T(8,128)(2,1)}, u32[]{:S(2)}) copy-start(bf16[128,4096]{1,0:T(8,128)(2,1)} %g.1) | copy-start | bytes 3145732
  60.9 24.0 %copy-start.2 = (bf16[128,1024]{1,0:T(8,128)(2,1)S(1)}, bf16[128,1024]{1,0:T(8,128)(2,1)}, u32[]{:S(2)}) copy-start(bf16[128,1024]{1,0:T(8,128)(2,1)} %k.1) | copy-start | bytes 786436
  60.9 24.0 %copy-start.3 = (bf16[128,1024]{1,0:T(8,128)(2,1)S(1)}, bf16[128,1024]{1,0:T(8,128)(2,1)}, u32[]{:S(2)}) copy-start(bf16[128,1024]{1,0:T(8,128)(2,1)} %v.1) | copy-start | bytes 786436
  60.9 24.0 %copy-start.4 = (s32[1,128,2]{1,2,0:T(2,128)S(1)}, s32[1,128,2]{1,2,0:T(2,128)}, u32[]{:S(2)}) copy-start(s32[1,128,2]{1,2,0:T(2,128)} %param.13) | copy-start | bytes 3076
  60.9 24.0 %copy-start.5 = (s32[1,128]{1,0:T(1,128)S(1)}, s32[1,128]{1,0:T(1,128)}, u32[]{:S(2)}) copy-start(s32[1,128]{1,0:T(1,128)} %unp.1) | copy-start | bytes 1540
  60.9 24.0 %copy-start.6 = (s32[1,16]{1,0:T(1,128)S(1)}, s32[1,16]{1,0:T(1,128)}, u32[]{:S(2)}) copy-start(s32[1,16]{1,0:T(1,128)} %lengths.1) | copy-start | bytes 196

commit v7 on v6

--- a/solution.py
+++ b/solution.py
@@ -516,33 +516,39 @@
     )(recv, other, recvg)
 
 
-def unpack_kernel(K, sel, back, backkv, att, attended, gq, gk, gv):
+STEP = 4
+
+
+def unpack_kernel(sel, back, backkv, att, attended, gq, gk, gv):
     s = sel[...]
     by_sequence = [(z, e) for z in range(4) for e in range(2)]
-    for core, out in ((0, gk), (1, gv)):
-        cols = slice(core * 256, (core + 1) * 256)
-        attended[:, cols] = att[core, 0]
-        rows = [back[z, core, e, 0].astype(F32) for z, e in by_sequence]
-        gq[:, cols] = dot(s, jnp.concatenate(rows, axis=0).astype(BF16), 0, 0).astype(BF16)
-        rows = [backkv[z, core, e, 0].astype(F32) for z, e in by_sequence]
-        out[...] = dot(s, jnp.concatenate(rows, axis=0).astype(BF16), 0, 0).astype(BF16)
+    for h in range(STEP):
+        for core, out in ((0, gk), (1, gv)):
+            cols = slice(h * 512 + core * 256, h * 512 + (core + 1) * 256)
+            attended[:, cols] = att[core, h]
+            rows = [back[z, core, e, h].astype(F32) for z, e in by_sequence]
+            gq[:, cols] = dot(s, jnp.concatenate(rows, axis=0).astype(BF16), 0, 0).astype(BF16)
+            rows = [backkv[z, core, e, h].astype(F32) for z, e in by_sequence]
+            out[:, h * 128 : (h + 1) * 128] = dot(
+                s, jnp.concatenate(rows, axis=0).astype(BF16), 0, 0
+            ).astype(BF16)
 
 
 def unpack_rows(K, sel, back, backkv, att):
     return pl.pallas_call(
-        functools.partial(unpack_kernel, K),
-        grid=(KVH,),
+        unpack_kernel,
+        grid=(KVH // STEP,),
         in_specs=[
             pl.BlockSpec((8 * K, TOK), lambda i: (0, 0)),
-            pl.BlockSpec((4, 2, 2, 1, K, 256), lambda i: (0, 0, 0, i, 0, 0)),
-            pl.BlockSpec((4, 2, 2, 1, K, 128), lambda i: (0, 0, 0, i, 0, 0)),
-            pl.BlockSpec((2, 1, TOK, 256), lambda i: (0, i, 0, 0)),
+            pl.BlockSpec((4, 2, 2, STEP, K, 256), lambda i: (0, 0, 0, i, 0, 0)),
+            pl.BlockSpec((4, 2, 2, STEP, K, 128), lambda i: (0, 0, 0, i, 0, 0)),
+            pl.BlockSpec((2, STEP, TOK, 256), lambda i: (0, i, 0, 0)),
         ],
         out_specs=[
-            pl.BlockSpec((TOK, 512), lambda i: (0, i)),
-            pl.BlockSpec((TOK, 512), lambda i: (0, i)),
-            pl.BlockSpec((TOK, 128), lambda i: (0, i)),
-            pl.BlockSpec((TOK, 128), lambda i: (0, i)),
+            pl.BlockSpec((TOK, STEP * 512), lambda i: (0, i)),
+            pl.BlockSpec((TOK, STEP * 512), lambda i: (0, i)),
+            pl.BlockSpec((TOK, STEP * 128), lambda i: (0, i)),
+            pl.BlockSpec((TOK, STEP * 128), lambda i: (0, i)),
         ],
         out_shape=[
             jax.ShapeDtypeStruct((TOK, H * DH), BF16),

time: 143 us -> 140 us (0.979)
  Pallas kernels: 141 us -> 138 us
    pallas_call x1, Pallas kernels: 6.91 us -> 3.44 us  [unpack_rows(): pl.pallas_call(unpack_kernel, grid=(KVH // STEP,), in_specs=[pl.BlockSpec...]
where the time goes in v7:
time: 140 us
  Pallas kernels  138 us (99%)
  between operations  1.63 us (1%)
    pallas_call x1, Pallas kernels, exchange_in(): pl.pallas_call(functools.partial(exchange_in_kernel, K), in_specs=[vmem]...  60.2 us
    pallas_call x1, Pallas kernels, exchange_out(): pl.pallas_call(functools.partial(exchange_out_kernel, K), in_specs=[vmem,...  51 us
    pallas_call x1, Pallas kernels, attention(): pl.pallas_call(functools.partial(attention_kernel, K), in_specs=[vmem] *...  23.1 us
    pallas_call x1, Pallas kernels, unpack_rows(): pl.pallas_call(unpack_kernel, grid=(KVH // STEP,), in_specs=[pl.BlockSpec...  3.44 us

profile of v7, /device:TPU:1, one launch (start us, length us, event | category | flops | bytes accessed | tf_op | source)
XLA Modules:
  0.0 139.7 jit_solution(1548812356487897124)
XLA Ops:
  0.6 60.2 %exchange_in.3 = (bf16[128,24,384]{2,1,0:T(8,128)(2,1)}, bf16[128,24,128]{2,1,0:T(8,128)(2,1)}, bf16[16,144,256]{2,1,0:T(8,128)(2,1)}, bf16[192,128]{1,0:T(8,128)(2,1)S(1)}) custom-call(s32[2,128]{1,0:T(2,128)} %bitcast.27, s32[1,128]{1,0:T(1,128)} %unp.1, s32[1,16]{1,0:T(1,128)} %lengths.1, bf16[128,4096]{1,0:T(8,128)(2,1)} %q.1, bf16[128,1024]{1,0:T(8,128)(2,1)} %k.1, ...), custom_call_target="tpu_custom_call" | custom-call | tf_op jit(solution)/shard_map/exchange_in/pallas_call | solution.py:222
  60.8 0.0 copy-start
  60.9 0.0 copy-start.1
  60.9 0.0 copy-start.2
  60.9 0.0 copy-start.3
  60.9 0.0 copy-start.4
  60.9 0.0 copy-start.5
  60.9 0.0 copy-start.6
  60.9 23.1 %attention.3 = (bf16[16,128,256]{2,1,0:T(8,128)(2,1)S(1)}, bf16[2048,512]{1,0:T(8,128)(2,1)S(1)}, f32[256,128]{1,0:T(8,128)S(1)}, f32[16,128]{1,0:T(8,128)S(1)}, f32[1]{0:T(128)}) custom-call(bf16[16,192,384]{2,1,0:T(8,128)(2,1)} %bitcast.18, bf16[16,192,128]{2,1,0:T(8,128)(2,1)} %bitcast.26, bf16[16,144,256]{2,1,0:T(8,128)(2,1)} %get-tuple-element.65.recvg), custom_call_target="tpu_custom_call" | custom-call | tf_op jit(solution)/shard_map/attention/pallas_call | solution.py:494
  84.7 0.0 copy-done
  84.7 0.0 copy-done.1
  84.7 0.0 copy-done.2
  84.7 0.0 copy-done.3
  84.7 0.0 copy-done.4
  84.7 0.0 copy-done.5
  84.8 0.0 copy-done.6
  84.8 54.7 %conditional.1 = ((bf16[128,4096]{1,0:T(8,128)(2,1)}, bf16[128,4096]{1,0:T(8,128)(2,1)}, bf16[128,1024]{1,0:T(8,128)(2,1)}, bf16[128,1024]{1,0:T(8,128)(2,1)})) conditional(s32[]{:T(128)} %bitcast.15, (bf16[2048,512]{1,0:T(8,128)(2,1)S(1)}, f32[256,128]{1,0:T(8,128)S(1)}, f32[16,128]{1,0:T(8,128)S(1)}, bf16[16,128,256]{2,1,0:T(8,128)(2,1)S(1)}, ...), branch_computations={%region_0.0_spmd, %region_1.0_spmd} | conditional | bytes 8 | solution.py:581
  84.8 51.0 %exchange_out.2 = (bf16[128,24,256]{2,1,0:T(8,128)(2,1)}, bf16[128,24,128]{2,1,0:T(8,128)(2,1)}, bf16[16,128,256]{2,1,0:T(8,128)(2,1)}) custom-call(bf16[2048,512]{1,0:T(8,128)(2,1)S(1)} %get-tuple-element.25.rows_in, f32[256,128]{1,0:T(8,128)S(1)} %get-tuple-element.26.col, f32[16,128]{1,0:T(8,128)S(1)} %get-tuple-element.27.unp, ...), custom_call_target="tpu_custom_call" | custom-call | tf_op jit(solution)/shard_map/cond/branch_0_fun/exchange_out/pallas_call | solution.py:326
  135.7 3.4 %messages_to_rows.2 = (bf16[128,4096]{1,0:T(8,128)(2,1)}, bf16[128,4096]{1,0:T(8,128)(2,1)}, bf16[128,1024]{1,0:T(8,128)(2,1)}, bf16[128,1024]{1,0:T(8,128)(2,1)}) custom-call(bf16[192,128]{1,0:T(8,128)(2,1)S(1)} %get-tuple-element.24.sel, bf16[4,2,2,8,24,256]{5,4,3,2,1,0:T(8,128)(2,1)} %bitcast.20, bf16[4,2,2,8,24,128]{5,4,3,2,1,0:T(8,128)(2,1)} %bitcast.25, ...), custom_call_target="tpu_custom_call" | custom-call | tf_op jit(solution)/shard_map/cond/branch_0_fun/messages_to_rows/pallas_call | solution.py:538
Async XLA Ops:
  60.8 23.9 %copy-start = (bf16[128,4096]{1,0:T(8,128)(2,1)S(1)}, bf16[128,4096]{1,0:T(8,128)(2,1)}, u32[]{:S(2)}) copy-start(bf16[128,4096]{1,0:T(8,128)(2,1)} %q.1) | copy-start | bytes 3145732
  60.9 23.9 %copy-start.1 = (bf16[128,4096]{1,0:T(8,128)(2,1)S(1)}, bf16[128,4096]{1,0:T(8,128)(2,1)}, u32[]{:S(2)}) copy-start(bf16[128,4096]{1,0:T(8,128)(2,1)} %g.1) | copy-start | bytes 3145732
  60.9 23.9 %copy-start.2 = (bf16[128,1024]{1,0:T(8,128)(2,1)S(1)}, bf16[128,1024]{1,0:T(8,128)(2,1)}, u32[]{:S(2)}) copy-start(bf16[128,1024]{1,0:T(8,128)(2,1)} %k.1) | copy-start | bytes 786436
  60.9 23.9 %copy-start.3 = (bf16[128,1024]{1,0:T(8,128)(2,1)S(1)}, bf16[128,1024]{1,0:T(8,128)(2,1)}, u32[]{:S(2)}) copy-start(bf16[128,1024]{1,0:T(8,128)(2,1)} %v.1) | copy-start | bytes 786436
  60.9 23.9 %copy-start.4 = (s32[1,128,2]{1,2,0:T(2,128)S(1)}, s32[1,128,2]{1,2,0:T(2,128)}, u32[]{:S(2)}) copy-start(s32[1,128,2]{1,2,0:T(2,128)} %param.13) | copy-start | bytes 3076
  60.9 23.9 %copy-start.5 = (s32[1,128]{1,0:T(1,128)S(1)}, s32[1,128]{1,0:T(1,128)}, u32[]{:S(2)}) copy-start(s32[1,128]{1,0:T(1,128)} %unp.1) | copy-start | bytes 1540
  60.9 23.9 %copy-start.6 = (s32[1,16]{1,0:T(1,128)S(1)}, s32[1,16]{1,0:T(1,128)}, u32[]{:S(2)}) copy-start(s32[1,16]{1,0:T(1,128)} %lengths.1) | copy-start | bytes 196

commit v8 on v7

--- a/solution.py
+++ b/solution.py
@@ -112,15 +112,22 @@
 
 
 def exchange_in_kernel(
-    K, slots, unp, lengths, q, k, v, g, dst, other, dstg, sel,
-    send, sendg, over_s,
+    K, slots, unp, lengths, q_in, k_in, v_in, g, dst, other, dstg, sel,
+    send, sendg, over_s, q, k, v,
     send_sem, recv_sem, sendg_sem, recvg_sem, sendo_sem, recvo_sem, own_sem, owng_sem,
+    q_sem, k_sem, v_sem,
 ):
     d, c, z, core = place()
     me = d * CTX + c
     mine = core == lax.div(c, 8)
     first = core * 8 + lax.rem(c, 8)
     all_here = greet_all()
+    loads = [
+        pltpu.make_async_copy(a, b, sem)
+        for a, b, sem in ((q_in, q, q_sem), (k_in, k, k_sem), (v_in, v, v_sem))
+    ]
+    for load in loads:
+        load.start()
 
     r = iota((16, TOK), 0)
     spread = (r == iota((16, TOK), 1)).astype(BF16)
@@ -180,6 +187,9 @@
     last = (iota((8 * K, TOK), 0) % K == K - 1) & (K < FULL)
     over_s[...] = jnp.where(last, over, 0.0)
 
+    for load in loads:
+        load.wait()
+
     def build(h, carry):
         wide = pl.ds(pl.multiple_of(h * 512, 512), 512)
         narrow = pl.ds(pl.multiple_of(h * 128, 128), 128)
@@ -221,7 +231,7 @@
     vmem = pl.BlockSpec(memory_space=pltpu.VMEM)
     return pl.pallas_call(
         functools.partial(exchange_in_kernel, K),
-        in_specs=[vmem] * 7,
+        in_specs=[vmem] * 3 + [anywhere] * 3 + [vmem],
         out_specs=[anywhere] * 3 + [vmem],
         out_shape=[
             jax.ShapeDtypeStruct((DEV, K, COLS), BF16),
@@ -233,8 +243,11 @@
             pltpu.VMEM((DEV, K, COLS), BF16),
             pltpu.VMEM((CTX, GROWS, 256), BF16),
             pltpu.VMEM((8 * K, TOK), F32),
+            pltpu.VMEM((TOK, H * DH), BF16),
+            pltpu.VMEM((TOK, KVH * DH), BF16),
+            pltpu.VMEM((TOK, KVH * DH), BF16),
         ]
-        + [pltpu.SemaphoreType.DMA] * 8,
+        + [pltpu.SemaphoreType.DMA] * 11,
         compiler_params=pltpu.CompilerParams(
             has_side_effects=True, vmem_limit_bytes=VMEM_LIMIT, collective_id=K
         ),
@@ -243,10 +256,10 @@
 
 
 def exchange_out_kernel(
-    K, rows_in, col, unp, srcg, dst, dstkv, dstg,
-    mid, src, keep, give, other, total,
+    K, rows_hbm, col, unp, srcg, dst, dstkv, dstg,
+    rows_in, mid, src, keep, give, other, total,
     send_sem, recv_sem, sendk_sem, recvk_sem, sendg_sem, recvg_sem, sendo_sem, recvo_sem,
-    own_sem, ownk_sem, owng_sem,
+    own_sem, ownk_sem, owng_sem, rows_sem,
 ):
     d, c, z, core = place()
     me = d * CTX + c
@@ -257,6 +270,8 @@
     def grads(j):
         remote(srcg.at[j], dstg.at[slot], sendg_sem, recvg_sem, (2 * z + e, j)).start()
 
+    load = pltpu.make_async_copy(rows_hbm, rows_in, rows_sem)
+    load.start()
     owng = pltpu.make_async_copy(srcg.at[c], dstg.at[slot], owng_sem)
 
     @pl.when(mine)
@@ -273,6 +288,7 @@
 
     lax.fori_loop(1, CTX, turn, 0)
 
+    load.wait()
     for n in range(CTX):
         slots = row_slots(unp[n : n + 1, :])
         mid[n] = dot(slots, rows_in[n * TOK : (n + 1) * TOK, :], 1, 0).astype(BF16)
@@ -325,15 +341,16 @@
     narrow = pltpu.VMEM((DEV, K, 128), BF16)
     return pl.pallas_call(
         functools.partial(exchange_out_kernel, K),
-        in_specs=[vmem, vmem, vmem, anywhere],
+        in_specs=[anywhere, vmem, vmem, anywhere],
         out_specs=[anywhere] * 3,
         out_shape=[
             jax.ShapeDtypeStruct((DEV, K, 256), BF16),
             jax.ShapeDtypeStruct((DEV, K, 128), BF16),
             jax.ShapeDtypeStruct(srcg.shape, BF16),
         ],
-        scratch_shapes=[pltpu.VMEM((CTX, 256, 512), BF16), wide, narrow, narrow, narrow, narrow]
-        + [pltpu.SemaphoreType.DMA] * 11,
+        scratch_shapes=[pltpu.VMEM((SEQ, 512), BF16), pltpu.VMEM((CTX, 256, 512), BF16)]
+        + [wide, narrow, narrow, narrow, narrow]
+        + [pltpu.SemaphoreType.DMA] * 12,
         compiler_params=pltpu.CompilerParams(has_side_effects=True, vmem_limit_bytes=VMEM_LIMIT),
         name="exchange_out",
     )(rows, col, unp, srcg)

time: 140 us -> 140 us (level)
  no operation moved by 1% of the time
where the time goes in v8:
time: 140 us; the launch traced here: 139 us
  Pallas kernels  137 us (98%)
  between operations  1.63 us (1%)
    pallas_call x1, Pallas kernels, exchange_in(): pl.pallas_call(functools.partial(exchange_in_kernel, K), in_specs=[vmem]...  59.8 us
    pallas_call x1, Pallas kernels, exchange_out(): pl.pallas_call(functools.partial(exchange_out_kernel, K), in_specs=[anywh...  51 us
    pallas_call x1, Pallas kernels, attention(): pl.pallas_call(functools.partial(attention_kernel, K), in_specs=[vmem] *...  23.3 us
    pallas_call x1, Pallas kernels, unpack_rows(): pl.pallas_call(unpack_kernel, grid=(KVH // STEP,), in_specs=[pl.BlockSpec...  3.43 us

profile of v8, /device:TPU:1, one launch (start us, length us, event | category | flops | bytes accessed | tf_op | source)
XLA Modules:
  0.0 139.4 jit_solution(15807521562445510517)
XLA Ops:
  0.6 59.8 %exchange_in.3 = (bf16[128,24,384]{2,1,0:T(8,128)(2,1)}, bf16[128,24,128]{2,1,0:T(8,128)(2,1)}, bf16[16,144,256]{2,1,0:T(8,128)(2,1)}, bf16[192,128]{1,0:T(8,128)(2,1)S(1)}) custom-call(s32[2,128]{1,0:T(2,128)} %bitcast.27, s32[1,128]{1,0:T(1,128)} %unp.1, s32[1,16]{1,0:T(1,128)} %lengths.1, bf16[128,4096]{1,0:T(8,128)(2,1)} %q_in.1, ...), custom_call_target="tpu_custom_call" | custom-call | tf_op jit(solution)/shard_map/exchange_in/pallas_call | solution.py:232
  60.4 0.0 copy-start
  60.5 0.0 copy-start.1
  60.5 0.0 copy-start.2
  60.5 0.0 copy-start.3
  60.5 0.0 copy-start.4
  60.5 0.0 copy-start.5
  60.5 0.0 copy-start.6
  60.5 23.3 %attention.3 = (bf16[16,128,256]{2,1,0:T(8,128)(2,1)S(1)}, bf16[2048,512]{1,0:T(8,128)(2,1)S(1)}, f32[256,128]{1,0:T(8,128)S(1)}, f32[16,128]{1,0:T(8,128)S(1)}, f32[1]{0:T(128)}) custom-call(bf16[16,192,384]{2,1,0:T(8,128)(2,1)} %bitcast.18, bf16[16,192,128]{2,1,0:T(8,128)(2,1)} %bitcast.26, bf16[16,144,256]{2,1,0:T(8,128)(2,1)} %get-tuple-element.65.recvg), custom_call_target="tpu_custom_call" | custom-call | tf_op jit(solution)/shard_map/attention/pallas_call | solution.py:511
  84.4 0.0 copy-done
  84.5 0.0 copy-done.1
  84.5 0.0 copy-done.2
  84.5 0.0 copy-done.3
  84.5 0.0 copy-done.4
  84.5 0.0 copy-done.5
  84.5 0.0 copy-done.6
  84.5 54.7 %conditional.1 = ((bf16[128,4096]{1,0:T(8,128)(2,1)}, bf16[128,4096]{1,0:T(8,128)(2,1)}, bf16[128,1024]{1,0:T(8,128)(2,1)}, bf16[128,1024]{1,0:T(8,128)(2,1)})) conditional(s32[]{:T(128)} %bitcast.15, (bf16[2048,512]{1,0:T(8,128)(2,1)S(1)}, f32[256,128]{1,0:T(8,128)S(1)}, f32[16,128]{1,0:T(8,128)S(1)}, bf16[16,128,256]{2,1,0:T(8,128)(2,1)S(1)}, ...), branch_computations={%region_0.0_spmd, %region_1.0_spmd} | conditional | bytes 8 | solution.py:598
  84.5 51.0 %exchange_out.2 = (bf16[128,24,256]{2,1,0:T(8,128)(2,1)}, bf16[128,24,128]{2,1,0:T(8,128)(2,1)}, bf16[16,128,256]{2,1,0:T(8,128)(2,1)}) custom-call(bf16[2048,512]{1,0:T(8,128)(2,1)S(1)} %get-tuple-element.25.rows_hbm, f32[256,128]{1,0:T(8,128)S(1)} %get-tuple-element.26.col, f32[16,128]{1,0:T(8,128)S(1)} %get-tuple-element.27.unp, ...), custom_call_target="tpu_custom_call" | custom-call | tf_op jit(solution)/shard_map/cond/branch_0_fun/exchange_out/pallas_call | solution.py:342
  135.5 3.4 %messages_to_rows.2 = (bf16[128,4096]{1,0:T(8,128)(2,1)}, bf16[128,4096]{1,0:T(8,128)(2,1)}, bf16[128,1024]{1,0:T(8,128)(2,1)}, bf16[128,1024]{1,0:T(8,128)(2,1)}) custom-call(bf16[192,128]{1,0:T(8,128)(2,1)S(1)} %get-tuple-element.24.sel, bf16[4,2,2,8,24,256]{5,4,3,2,1,0:T(8,128)(2,1)} %bitcast.20, bf16[4,2,2,8,24,128]{5,4,3,2,1,0:T(8,128)(2,1)} %bitcast.25, ...), custom_call_target="tpu_custom_call" | custom-call | tf_op jit(solution)/shard_map/cond/branch_0_fun/messages_to_rows/pallas_call | solution.py:555
Async XLA Ops:
  60.4 24.0 %copy-start = (bf16[128,4096]{1,0:T(8,128)(2,1)S(1)}, bf16[128,4096]{1,0:T(8,128)(2,1)}, u32[]{:S(2)}) copy-start(bf16[128,4096]{1,0:T(8,128)(2,1)} %q_in.1) | copy-start | bytes 3145732
  60.5 24.0 %copy-start.1 = (bf16[128,4096]{1,0:T(8,128)(2,1)S(1)}, bf16[128,4096]{1,0:T(8,128)(2,1)}, u32[]{:S(2)}) copy-start(bf16[128,4096]{1,0:T(8,128)(2,1)} %g.1) | copy-start | bytes 3145732
  60.5 24.0 %copy-start.2 = (bf16[128,1024]{1,0:T(8,128)(2,1)S(1)}, bf16[128,1024]{1,0:T(8,128)(2,1)}, u32[]{:S(2)}) copy-start(bf16[128,1024]{1,0:T(8,128)(2,1)} %k_in.1) | copy-start | bytes 786436
  60.5 24.0 %copy-start.3 = (bf16[128,1024]{1,0:T(8,128)(2,1)S(1)}, bf16[128,1024]{1,0:T(8,128)(2,1)}, u32[]{:S(2)}) copy-start(bf16[128,1024]{1,0:T(8,128)(2,1)} %v_in.1) | copy-start | bytes 786436
  60.5 24.0 %copy-start.4 = (s32[1,128,2]{1,2,0:T(2,128)S(1)}, s32[1,128,2]{1,2,0:T(2,128)}, u32[]{:S(2)}) copy-start(s32[1,128,2]{1,2,0:T(2,128)} %param.13) | copy-start | bytes 3076
  60.5 24.0 %copy-start.5 = (s32[1,128]{1,0:T(1,128)S(1)}, s32[1,128]{1,0:T(1,128)}, u32[]{:S(2)}) copy-start(s32[1,128]{1,0:T(1,128)} %unp.1) | copy-start | bytes 1540
  60.5 24.0 %copy-start.6 = (s32[1,16]{1,0:T(1,128)S(1)}, s32[1,16]{1,0:T(1,128)}, u32[]{:S(2)}) copy-start(s32[1,16]{1,0:T(1,128)} %lengths.1) | copy-start | bytes 196

commit v9 on v8

--- a/solution.py
+++ b/solution.py
@@ -69,7 +69,7 @@
 def partner(n):
     d, c, z, core = place()
     x, y = lax.div(c, 4), lax.rem(c, 4)
-    j = lax.rem(n * 37, DEV)
+    j = lax.rem(n * 5, DEV)
     dy = lax.rem(j, 2) + 2 * lax.rem(lax.div(j, 16), 2)
     dx = lax.rem(lax.div(j, 2), 2) + 2 * lax.rem(lax.div(j, 32), 2)
     dz = lax.rem(lax.div(j, 4), 2) + 2 * lax.div(j, 64)

time: 140 us -> 138 us (0.986)
  Pallas kernels: 137 us -> 135 us
    pallas_call x1, Pallas kernels: 51 us -> 48.4 us  [exchange_out(): pl.pallas_call(functools.partial(exchange_out_kernel, K), in_specs=[anywh...]
where the time goes in v9:
time: 138 us; the launch traced here: 137 us
  Pallas kernels  135 us (98%)
  between operations  1.63 us (1%)
    pallas_call x1, Pallas kernels, exchange_in(): pl.pallas_call(functools.partial(exchange_in_kernel, K), in_specs=[vmem]...  60.3 us
    pallas_call x1, Pallas kernels, exchange_out(): pl.pallas_call(functools.partial(exchange_out_kernel, K), in_specs=[anywh...  48.4 us
    pallas_call x1, Pallas kernels, attention(): pl.pallas_call(functools.partial(attention_kernel, K), in_specs=[vmem] *...  23.3 us
    pallas_call x1, Pallas kernels, unpack_rows(): pl.pallas_call(unpack_kernel, grid=(KVH // STEP,), in_specs=[pl.BlockSpec...  3.46 us

profile of v9, /device:TPU:1, one launch (start us, length us, event | category | flops | bytes accessed | tf_op | source)
XLA Modules:
  0.0 137.4 jit_solution(15000240307569178872)
XLA Ops:
  0.6 60.3 %exchange_in.3 = (bf16[128,24,384]{2,1,0:T(8,128)(2,1)}, bf16[128,24,128]{2,1,0:T(8,128)(2,1)}, bf16[16,144,256]{2,1,0:T(8,128)(2,1)}, bf16[192,128]{1,0:T(8,128)(2,1)S(1)}) custom-call(s32[2,128]{1,0:T(2,128)} %bitcast.27, s32[1,128]{1,0:T(1,128)} %unp.1, s32[1,16]{1,0:T(1,128)} %lengths.1, bf16[128,4096]{1,0:T(8,128)(2,1)} %q_in.1, ...), custom_call_target="tpu_custom_call" | custom-call | tf_op jit(solution)/shard_map/exchange_in/pallas_call | solution.py:232
  60.9 0.0 copy-start
  61.0 0.0 copy-start.1
  61.0 0.0 copy-start.2
  61.0 0.0 copy-start.3
  61.0 0.0 copy-start.4
  61.0 0.0 copy-start.5
  61.0 0.0 copy-start.6
  61.0 23.3 %attention.3 = (bf16[16,128,256]{2,1,0:T(8,128)(2,1)S(1)}, bf16[2048,512]{1,0:T(8,128)(2,1)S(1)}, f32[256,128]{1,0:T(8,128)S(1)}, f32[16,128]{1,0:T(8,128)S(1)}, f32[1]{0:T(128)}) custom-call(bf16[16,192,384]{2,1,0:T(8,128)(2,1)} %bitcast.18, bf16[16,192,128]{2,1,0:T(8,128)(2,1)} %bitcast.26, bf16[16,144,256]{2,1,0:T(8,128)(2,1)} %get-tuple-element.65.recvg), custom_call_target="tpu_custom_call" | custom-call | tf_op jit(solution)/shard_map/attention/pallas_call | solution.py:511
  85.0 0.0 copy-done
  85.0 0.0 copy-done.1
  85.0 0.0 copy-done.2
  85.0 0.0 copy-done.3
  85.0 0.0 copy-done.4
  85.0 0.0 copy-done.5
  85.0 0.0 copy-done.6
  85.0 52.2 %conditional.1 = ((bf16[128,4096]{1,0:T(8,128)(2,1)}, bf16[128,4096]{1,0:T(8,128)(2,1)}, bf16[128,1024]{1,0:T(8,128)(2,1)}, bf16[128,1024]{1,0:T(8,128)(2,1)})) conditional(s32[]{:T(128)} %bitcast.15, (bf16[2048,512]{1,0:T(8,128)(2,1)S(1)}, f32[256,128]{1,0:T(8,128)S(1)}, f32[16,128]{1,0:T(8,128)S(1)}, bf16[16,128,256]{2,1,0:T(8,128)(2,1)S(1)}, ...), branch_computations={%region_0.0_spmd, %region_1.0_spmd} | conditional | bytes 8 | solution.py:598
  85.0 48.4 %exchange_out.2 = (bf16[128,24,256]{2,1,0:T(8,128)(2,1)}, bf16[128,24,128]{2,1,0:T(8,128)(2,1)}, bf16[16,128,256]{2,1,0:T(8,128)(2,1)}) custom-call(bf16[2048,512]{1,0:T(8,128)(2,1)S(1)} %get-tuple-element.25.rows_hbm, f32[256,128]{1,0:T(8,128)S(1)} %get-tuple-element.26.col, f32[16,128]{1,0:T(8,128)S(1)} %get-tuple-element.27.unp, ...), custom_call_target="tpu_custom_call" | custom-call | tf_op jit(solution)/shard_map/cond/branch_0_fun/exchange_out/pallas_call | solution.py:342
  133.5 3.5 %messages_to_rows.2 = (bf16[128,4096]{1,0:T(8,128)(2,1)}, bf16[128,4096]{1,0:T(8,128)(2,1)}, bf16[128,1024]{1,0:T(8,128)(2,1)}, bf16[128,1024]{1,0:T(8,128)(2,1)}) custom-call(bf16[192,128]{1,0:T(8,128)(2,1)S(1)} %get-tuple-element.24.sel, bf16[4,2,2,8,24,256]{5,4,3,2,1,0:T(8,128)(2,1)} %bitcast.20, bf16[4,2,2,8,24,128]{5,4,3,2,1,0:T(8,128)(2,1)} %bitcast.25, ...), custom_call_target="tpu_custom_call" | custom-call | tf_op jit(solution)/shard_map/cond/branch_0_fun/messages_to_rows/pallas_call | solution.py:555
Async XLA Ops:
  60.9 24.0 %copy-start = (bf16[128,4096]{1,0:T(8,128)(2,1)S(1)}, bf16[128,4096]{1,0:T(8,128)(2,1)}, u32[]{:S(2)}) copy-start(bf16[128,4096]{1,0:T(8,128)(2,1)} %q_in.1) | copy-start | bytes 3145732
  61.0 24.0 %copy-start.1 = (bf16[128,4096]{1,0:T(8,128)(2,1)S(1)}, bf16[128,4096]{1,0:T(8,128)(2,1)}, u32[]{:S(2)}) copy-start(bf16[128,4096]{1,0:T(8,128)(2,1)} %g.1) | copy-start | bytes 3145732
  61.0 24.0 %copy-start.2 = (bf16[128,1024]{1,0:T(8,128)(2,1)S(1)}, bf16[128,1024]{1,0:T(8,128)(2,1)}, u32[]{:S(2)}) copy-start(bf16[128,1024]{1,0:T(8,128)(2,1)} %k_in.1) | copy-start | bytes 786436
  61.0 24.0 %copy-start.3 = (bf16[128,1024]{1,0:T(8,128)(2,1)S(1)}, bf16[128,1024]{1,0:T(8,128)(2,1)}, u32[]{:S(2)}) copy-start(bf16[128,1024]{1,0:T(8,128)(2,1)} %v_in.1) | copy-start | bytes 786436
  61.0 24.0 %copy-start.4 = (s32[1,128,2]{1,2,0:T(2,128)S(1)}, s32[1,128,2]{1,2,0:T(2,128)}, u32[]{:S(2)}) copy-start(s32[1,128,2]{1,2,0:T(2,128)} %param.13) | copy-start | bytes 3076
  61.0 24.0 %copy-start.5 = (s32[1,128]{1,0:T(1,128)S(1)}, s32[1,128]{1,0:T(1,128)}, u32[]{:S(2)}) copy-start(s32[1,128]{1,0:T(1,128)} %unp.1) | copy-start | bytes 1540
  61.0 24.0 %copy-start.6 = (s32[1,16]{1,0:T(1,128)S(1)}, s32[1,16]{1,0:T(1,128)}, u32[]{:S(2)}) copy-start(s32[1,16]{1,0:T(1,128)} %lengths.1) | copy-start | bytes 196

commit v10 on v9

--- a/solution.py
+++ b/solution.py
@@ -69,7 +69,7 @@
 def partner(n):
     d, c, z, core = place()
     x, y = lax.div(c, 4), lax.rem(c, 4)
-    j = lax.rem(n * 5, DEV)
+    j = lax.rem(n * 45, DEV)
     dy = lax.rem(j, 2) + 2 * lax.rem(lax.div(j, 16), 2)
     dx = lax.rem(lax.div(j, 2), 2) + 2 * lax.rem(lax.div(j, 32), 2)
     dz = lax.rem(lax.div(j, 4), 2) + 2 * lax.div(j, 64)

time: 138 us -> 139 us (level)
  Pallas kernels: 135 us -> 137 us
    pallas_call x1, Pallas kernels: 48.4 us -> 50.5 us  [exchange_out(): pl.pallas_call(functools.partial(exchange_out_kernel, K), in_specs=[anywh...]
where the time goes in v10:
time: 139 us
  Pallas kernels  137 us (99%)
  between operations  1.63 us (1%)
    pallas_call x1, Pallas kernels, exchange_in(): pl.pallas_call(functools.partial(exchange_in_kernel, K), in_specs=[vmem]...  59.6 us
    pallas_call x1, Pallas kernels, exchange_out(): pl.pallas_call(functools.partial(exchange_out_kernel, K), in_specs=[anywh...  50.5 us
    pallas_call x1, Pallas kernels, attention(): pl.pallas_call(functools.partial(attention_kernel, K), in_specs=[vmem] *...  23.1 us
    pallas_call x1, Pallas kernels, unpack_rows(): pl.pallas_call(unpack_kernel, grid=(KVH // STEP,), in_specs=[pl.BlockSpec...  3.44 us

profile of v10, /device:TPU:1, one launch (start us, length us, event | category | flops | bytes accessed | tf_op | source)
XLA Modules:
  0.0 138.6 jit_solution(17815422688680221243)
XLA Ops:
  0.6 59.6 %exchange_in.3 = (bf16[128,24,384]{2,1,0:T(8,128)(2,1)}, bf16[128,24,128]{2,1,0:T(8,128)(2,1)}, bf16[16,144,256]{2,1,0:T(8,128)(2,1)}, bf16[192,128]{1,0:T(8,128)(2,1)S(1)}) custom-call(s32[2,128]{1,0:T(2,128)} %bitcast.27, s32[1,128]{1,0:T(1,128)} %unp.1, s32[1,16]{1,0:T(1,128)} %lengths.1, bf16[128,4096]{1,0:T(8,128)(2,1)} %q_in.1, ...), custom_call_target="tpu_custom_call" | custom-call | tf_op jit(solution)/shard_map/exchange_in/pallas_call | solution.py:232
  60.2 0.0 copy-start
  60.3 0.0 copy-start.1
  60.3 0.0 copy-start.2
  60.3 0.0 copy-start.3
  60.3 0.0 copy-start.4
  60.3 0.0 copy-start.5
  60.3 0.0 copy-start.6
  60.3 23.1 %attention.3 = (bf16[16,128,256]{2,1,0:T(8,128)(2,1)S(1)}, bf16[2048,512]{1,0:T(8,128)(2,1)S(1)}, f32[256,128]{1,0:T(8,128)S(1)}, f32[16,128]{1,0:T(8,128)S(1)}, f32[1]{0:T(128)}) custom-call(bf16[16,192,384]{2,1,0:T(8,128)(2,1)} %bitcast.18, bf16[16,192,128]{2,1,0:T(8,128)(2,1)} %bitcast.26, bf16[16,144,256]{2,1,0:T(8,128)(2,1)} %get-tuple-element.65.recvg), custom_call_target="tpu_custom_call" | custom-call | tf_op jit(solution)/shard_map/attention/pallas_call | solution.py:511
  84.1 0.0 copy-done
  84.1 0.0 copy-done.1
  84.1 0.0 copy-done.2
  84.1 0.0 copy-done.3
  84.2 0.0 copy-done.4
  84.2 0.0 copy-done.5
  84.2 0.0 copy-done.6
  84.2 54.2 %conditional.1 = ((bf16[128,4096]{1,0:T(8,128)(2,1)}, bf16[128,4096]{1,0:T(8,128)(2,1)}, bf16[128,1024]{1,0:T(8,128)(2,1)}, bf16[128,1024]{1,0:T(8,128)(2,1)})) conditional(s32[]{:T(128)} %bitcast.15, (bf16[2048,512]{1,0:T(8,128)(2,1)S(1)}, f32[256,128]{1,0:T(8,128)S(1)}, f32[16,128]{1,0:T(8,128)S(1)}, bf16[16,128,256]{2,1,0:T(8,128)(2,1)S(1)}, ...), branch_computations={%region_0.0_spmd, %region_1.0_spmd} | conditional | bytes 8 | solution.py:598
  84.2 50.5 %exchange_out.2 = (bf16[128,24,256]{2,1,0:T(8,128)(2,1)}, bf16[128,24,128]{2,1,0:T(8,128)(2,1)}, bf16[16,128,256]{2,1,0:T(8,128)(2,1)}) custom-call(bf16[2048,512]{1,0:T(8,128)(2,1)S(1)} %get-tuple-element.25.rows_hbm, f32[256,128]{1,0:T(8,128)S(1)} %get-tuple-element.26.col, f32[16,128]{1,0:T(8,128)S(1)} %get-tuple-element.27.unp, ...), custom_call_target="tpu_custom_call" | custom-call | tf_op jit(solution)/shard_map/cond/branch_0_fun/exchange_out/pallas_call | solution.py:342
  134.7 3.4 %messages_to_rows.2 = (bf16[128,4096]{1,0:T(8,128)(2,1)}, bf16[128,4096]{1,0:T(8,128)(2,1)}, bf16[128,1024]{1,0:T(8,128)(2,1)}, bf16[128,1024]{1,0:T(8,128)(2,1)}) custom-call(bf16[192,128]{1,0:T(8,128)(2,1)S(1)} %get-tuple-element.24.sel, bf16[4,2,2,8,24,256]{5,4,3,2,1,0:T(8,128)(2,1)} %bitcast.20, bf16[4,2,2,8,24,128]{5,4,3,2,1,0:T(8,128)(2,1)} %bitcast.25, ...), custom_call_target="tpu_custom_call" | custom-call | tf_op jit(solution)/shard_map/cond/branch_0_fun/messages_to_rows/pallas_call | solution.py:555
Async XLA Ops:
  60.2 23.9 %copy-start = (bf16[128,4096]{1,0:T(8,128)(2,1)S(1)}, bf16[128,4096]{1,0:T(8,128)(2,1)}, u32[]{:S(2)}) copy-start(bf16[128,4096]{1,0:T(8,128)(2,1)} %q_in.1) | copy-start | bytes 3145732
  60.3 23.9 %copy-start.1 = (bf16[128,4096]{1,0:T(8,128)(2,1)S(1)}, bf16[128,4096]{1,0:T(8,128)(2,1)}, u32[]{:S(2)}) copy-start(bf16[128,4096]{1,0:T(8,128)(2,1)} %g.1) | copy-start | bytes 3145732
  60.3 23.9 %copy-start.2 = (bf16[128,1024]{1,0:T(8,128)(2,1)S(1)}, bf16[128,1024]{1,0:T(8,128)(2,1)}, u32[]{:S(2)}) copy-start(bf16[128,1024]{1,0:T(8,128)(2,1)} %k_in.1) | copy-start | bytes 786436
  60.3 23.9 %copy-start.3 = (bf16[128,1024]{1,0:T(8,128)(2,1)S(1)}, bf16[128,1024]{1,0:T(8,128)(2,1)}, u32[]{:S(2)}) copy-start(bf16[128,1024]{1,0:T(8,128)(2,1)} %v_in.1) | copy-start | bytes 786436
  60.3 23.9 %copy-start.4 = (s32[1,128,2]{1,2,0:T(2,128)S(1)}, s32[1,128,2]{1,2,0:T(2,128)}, u32[]{:S(2)}) copy-start(s32[1,128,2]{1,2,0:T(2,128)} %param.13) | copy-start | bytes 3076
  60.3 23.9 %copy-start.5 = (s32[1,128]{1,0:T(1,128)S(1)}, s32[1,128]{1,0:T(1,128)}, u32[]{:S(2)}) copy-start(s32[1,128]{1,0:T(1,128)} %unp.1) | copy-start | bytes 1540
  60.3 23.9 %copy-start.6 = (s32[1,16]{1,0:T(1,128)S(1)}, s32[1,16]{1,0:T(1,128)}, u32[]{:S(2)}) copy-start(s32[1,16]{1,0:T(1,128)} %lengths.1) | copy-start | bytes 196
